TPU v7x, 256 devices: a whole 4x4x8 slice. The times are simulated.
256 devices in a mesh: tm: 32 (over z, y), dp: 8 (over x, core).
Axes of the slice: x: 4, y: 4, z: 8, core: 2. Of those that a mesh axis runs over, the one named last changes fastest.
Arguments:
- inputs: bfloat16 [8, 32768, 1024], P('dp', 'tm'), may hold values from -6 to 6
- weights: bfloat16 [1024, 1536], replicated, may hold values from -0.1875 to 0.1875
- out_grad: bfloat16 [8, 32768, 512], P('dp', 'tm'), may hold values from -6 to 6
Outputs:
- input_grad: bfloat16 [8, 32768, 1024], P('dp', 'tm')
- weight_grad: float32 [1024, 1536], P('tm')
All inputs are finite; a program needn't handle non-finite values.
Results may differ from a plain program's by a relative error of at most 0.0075.
Values sent between devices are 32-bit elements; how exact they have to be, the bound alone decides.
No kernel may reach another device: no remote copies, remote signals or barrier semaphores. Data moves between devices by JAX's collectives and lax.ppermute only.
A program may use at most 128 MiB of HBM per device.

v0:
```python
import jax
import jax.numpy as jnp
from jax import lax
from jax.sharding import PartitionSpec as P

H = 4
HD = 128
CH = 256


def carried_in(value, axis, join, neutral, backward):
    count, mine = (lax.axis_size(axis), lax.axis_index(axis))
    pieces = lax.all_gather(value, axis)
    if backward:
        pieces = pieces[::-1]
        mine = count - 1 - mine
    so_far = jnp.full_like(value, 0) + jnp.asarray(neutral, value.dtype)

    def lap(position, so_far):
        longer = join(so_far, pieces[position])
        return jnp.where(position < mine, longer, so_far)

    return lax.fori_loop(0, count - 1, lap, so_far)


def combine(earlier, later):
    return jax.tree.map(jnp.add, earlier, later)


def shards(inputs, weights, out_grad):
    f32 = jnp.float32
    bf16 = jnp.bfloat16
    tok_count = inputs.shape[1]
    width = weights.shape[1] // 3
    block_count = tok_count // CH
    record = inputs[0]
    qkv = jnp.dot(record, weights, preferred_element_type=f32).astype(bf16)
    shape4 = (block_count, CH, H, HD)
    queries = qkv[:, :width].reshape(shape4)
    key_rows = qkv[:, width : 2 * width].reshape(shape4)
    values = qkv[:, 2 * width :].reshape(shape4)
    offset = lax.axis_index("tm") * tok_count
    position = (offset + jnp.arange(tok_count, dtype=jnp.int32)).astype(f32)
    factor = 1.0 / jnp.sqrt(jnp.float32(HD) * (position + 1.0))
    scaled_grad = (out_grad[0].astype(f32) * factor[:, None]).astype(bf16).reshape(shape4)
    tri = (
        lax.broadcasted_iota(jnp.int32, (CH, CH), 0) >= lax.broadcasted_iota(jnp.int32, (CH, CH), 1)
    ).astype(f32)
    kv_group = jnp.einsum("nshd,nshe->nhde", key_rows, values, preferred_element_type=f32)
    qg_group = jnp.einsum("nthd,nthe->nhde", queries, scaled_grad, preferred_element_type=f32)
    kv_device = jnp.sum(kv_group, 0)
    qg_device = jnp.sum(qg_group, 0)
    zeros = jnp.zeros((H, HD, HD), f32)
    state_start = carried_in(kv_device, "tm", combine, zeros, False)
    grad_end = carried_in(qg_device, "tm", combine, zeros, True)
    mix_vg = (
        jnp.einsum("nthe,nshe->nhts", scaled_grad, values, preferred_element_type=f32) * tri
    ).astype(bf16)
    mix_qk = (
        jnp.einsum("nthd,nshd->nhts", queries, key_rows, preferred_element_type=f32) * tri
    ).astype(bf16)
    state_before = (state_start[None] + jnp.cumsum(kv_group, 0) - kv_group).astype(bf16)
    grad_after = (
        grad_end[None] + jnp.flip(jnp.cumsum(jnp.flip(qg_group, 0), 0), 0) - qg_group
    ).astype(bf16)
    grad_q = jnp.einsum(
        "nhts,nshd->nthd", mix_vg, key_rows, preferred_element_type=f32
    ) + jnp.einsum("nthe,nhde->nthd", scaled_grad, state_before, preferred_element_type=f32)
    grad_k = jnp.einsum(
        "nhts,nthd->nshd", mix_vg, queries, preferred_element_type=f32
    ) + jnp.einsum("nshe,nhde->nshd", values, grad_after, preferred_element_type=f32)
    grad_v = jnp.einsum(
        "nhts,nthe->nshe", mix_qk, scaled_grad, preferred_element_type=f32
    ) + jnp.einsum("nshd,nhde->nshe", key_rows, grad_after, preferred_element_type=f32)
    dqkv = jnp.concatenate(
        [
            grad_q.reshape(tok_count, width),
            grad_k.reshape(tok_count, width),
            grad_v.reshape(tok_count, width),
        ],
        axis=1,
    ).astype(bf16)
    record_grad = lax.dot_general(
        dqkv, weights, (((1,), (1,)), ((), ())), preferred_element_type=f32
    ).astype(bf16)
    partial_rows = lax.psum_scatter(
        lax.dot_general(record, dqkv, (((0,), (0,)), ((), ())), preferred_element_type=f32),
        "tm",
        scatter_dimension=0,
        tiled=True,
    )
    proj_grad = lax.psum(partial_rows, "dp")
    return (record_grad[None], proj_grad)


def solution(mesh):
    placed = (P("dp", "tm", None), P(), P("dp", "tm", None))
    return jax.shard_map(
        shards,
        mesh=mesh,
        in_specs=placed,
        out_specs=(P("dp", "tm", None), P("tm", None)),
        check_vma=False,
    )
```

profile of v0, /device:TPU:1, one launch (start us, length us, event | category | flops | bytes accessed | tf_op | source)
XLA Modules:
  0.0 590.9 jit_solution(9342990960004668326)
XLA Ops:
  7.2 2.8 reshape.58
  10.1 2.9 copy.36
  13.0 5.2 convolution_convert_fusion
  20.0 2.2 reshape.55
  22.1 1.9 multiply_convert_fusion.2
  25.1 2.2 fusion.27
  27.4 2.2 reshape.53
  29.5 2.1 reshape.52
  31.7 3.8 fusion.26
  35.7 2.3 rev.11
  38.0 2.5 fusion.28
  40.5 2.3 multiply_convert_fusion.1
  42.8 1.9 fusion.10
  44.7 2.2 fusion.19
  46.9 4.3 fusion.2
  51.1 78.3 %all-gather.7.cloned.1.call-done = f32[128,128,128]{2,1,0:T(8,128)} async-done(((f32[4,128,128]{2,1,0:T(8,128)}), f32[128,128,128]{2,1,0:T(8,128)}) %all-gather.7.cloned.1.call-update) | async-done | bytes 8388624 | tf_op jit(solution)/shard_map/all_gather | solution.py:13
  129.4 7.7 %rev.10 = f32[32,4,128,128]{3,2,1,0:T(8,128)} reverse(f32[32,4,128,128]{3,2,1,0:T(8,128)} %bitcast.53), dimensions={0} | reverse | bytes 16777216 | tf_op jit(solution)/shard_map/rev | solution.py:15
  137.1 54.8 %while.29 = (s32[]{:T(128)}, f32[4,128,128]{2,1,0:T(8,128)}, s32[]{:T(128)}, f32[32,4,128,128]{3,2,1,0:T(8,128)}, s32[]{:T(128)}, /*index=5*/s32[]{:T(128)}) while((s32[]{:T(128)}, f32[4,128,128]{2,1,0:T(8,128)}, s32[]{:T(128)}, f32[32,4,128,128]{3,2,1,0:T(8,128)}, s32[]{:T(128)}, /*index=5*/s32[]{:T(128)}) %tuple.73), condition=%wide.region_6.7_spmd.clone, body=%wide.region_5.6_spmd.clone.sunk | while | flops 196612 | bytes 786525 | solution.py:23
  138.8 1.8 add_select_fusion.5
  140.6 1.8 add_select_fusion.5
  142.4 1.8 add_select_fusion.5
  144.2 1.8 add_select_fusion.5
  145.9 1.8 add_select_fusion.5
  147.7 1.8 add_select_fusion.5
  149.5 1.8 add_select_fusion.5
  151.2 1.8 add_select_fusion.5
  153.0 1.8 add_select_fusion.5
  154.8 1.8 add_select_fusion.5
  156.6 1.8 add_select_fusion.5
  158.3 1.8 add_select_fusion.5
  160.1 1.8 add_select_fusion.5
  161.9 1.8 add_select_fusion.5
  163.7 1.8 add_select_fusion.5
  165.4 1.8 add_select_fusion.5
  167.2 1.8 add_select_fusion.5
  169.0 1.8 add_select_fusion.5
  174.3 1.8 add_select_fusion.5
  176.0 1.8 add_select_fusion.5
  177.8 1.8 add_select_fusion.5
  179.6 1.8 add_select_fusion.5
  181.3 1.8 add_select_fusion.5
  183.1 1.8 add_select_fusion.5
  186.6 1.8 add_select_fusion.5
  190.2 1.8 add_select_fusion.5
  192.0 1.9 subtract_convert_fusion
  194.6 3.1 fusion.5
  197.8 2.4 copy.48
  200.1 27.5 %all-gather.5.cloned.1.call-done = f32[128,128,128]{2,1,0:T(8,128)} async-done(((f32[4,128,128]{2,1,0:T(8,128)}), f32[128,128,128]{2,1,0:T(8,128)}) %all-gather.5.cloned.1.call-update) | async-done | bytes 8388624 | tf_op jit(solution)/shard_map/all_gather | solution.py:13
  227.7 33.0 %while.28 = (s32[]{:T(128)}, f32[4,128,128]{2,1,0:T(8,128)S(1)}, s32[]{:T(128)}, f32[32,4,128,128]{3,2,1,0:T(8,128)}, s32[]{:T(128)}, /*index=5*/s32[]{:T(128)}) while((s32[]{:T(128)}, f32[4,128,128]{2,1,0:T(8,128)S(1)}, s32[]{:T(128)}, f32[32,4,128,128]{3,2,1,0:T(8,128)}, s32[]{:T(128)}, /*index=5*/s32[]{:T(128)}) %tuple.84), condition=%wide.region_2.3_spmd.clone, body=%wide.region_1.0_spmd.clone.sunk | while | flops 196612 | bytes 786525 | solution.py:23
  260.7 1.8 fusion.7
  262.5 3.0 fusion.4
  265.5 2.3 copy.43
  267.9 2.5 bitcast_dynamic-update-slice_fusion.2
  270.4 2.9 fusion.6
  273.3 2.4 copy.53
  275.6 2.6 bitcast_dynamic-update-slice_fusion.1
  278.2 2.4 bitcast_dynamic-update-slice_fusion
  280.6 7.3 %convolution_bitcast_fusion = f32[1024,1536]{0,1:T(8,128)} fusion(bf16[1024,1536]{1,0:T(8,128)(2,1)} %bitcast_dynamic-update-slice_fusion, bf16[1,1024,1024]{2,1,0:T(8,128)(2,1)S(1)} %copy-done.10), kind=kOutput, calls=%fused_computation.2 | convolution fusion | flops 3221225472 | bytes 11534336 | tf_op jit(solution)/shard_map/dot_general | solution.py:87
  288.0 6.6 %copy.59 = f32[1024,1536]{1,0:T(8,128)} copy(f32[1024,1536]{0,1:T(8,128)} %convolution_bitcast_fusion) | data formatting | bytes 12582912
  294.6 218.5 %reduce-scatter.4.cloned.1.call-done = f32[32,1536]{1,0:T(8,128)} async-done(((f32[1024,1536]{1,0:T(8,128)}), f32[32,1536]{1,0:T(8,128)}) %reduce-scatter.4.cloned.1.call-update) | async-done | bytes 196624
  513.2 2.1 copy.60
  515.3 6.5 %convert_bitcast_fusion = bf16[1,1024,1024]{2,1,0:T(8,128)(2,1)} fusion(bf16[1024,1536]{1,0:T(8,128)(2,1)} %bitcast_dynamic-update-slice_fusion, bf16[1024,1536]{1,0:T(8,128)(2,1)S(1)} %copy-done), kind=kOutput, calls=%fused_computation.8 | convolution fusion | flops 3222274048 | bytes 8388608 | tf_op jit(solution)/shard_map/dot_general | solution.py:83
  521.8 60.5 %all-reduce.2.cloned.1.call-done = f32[32,1536]{0,1:T(8,128)} async-done(((f32[32,1536]{0,1:T(8,128)}), f32[32,1536]{0,1:T(8,128)}) %all-reduce.2.cloned.1.call-update) | async-done | bytes 196624 | tf_op jit(solution)/shard_map/psum | solution.py:92
  582.3 2.1 copy.54
  (71 shorter events, 45.1 us)
Async XLA Ops:
  7.2 5.9 copy-start
  7.2 122.2 %all-gather.7.cloned.1.call-start = ((), (), s32[]{:S(2)}) async-start(), calls=%async_computation.3 | async-start | bytes 8650752 | tf_op jit(solution)/shard_map/all_gather | solution.py:13
  22.1 3.0 copy-start.5
  24.0 1.1 copy-start.1
  27.3 200.3 %all-gather.5.cloned.1.call-start = ((), (), s32[]{:S(2)}) async-start(), calls=%async_computation.2 | async-start | bytes 8650752 | tf_op jit(solution)/shard_map/all_gather | solution.py:13
  35.5 477.7 %reduce-scatter.4.cloned.1.call-start = ((), (), s32[]{:S(2)}) async-start(), calls=%async_computation.4 | async-start | bytes 6488064
  38.0 4.8 copy-start.9
  38.0 4.8 copy-start.6
  42.8 1.9 copy-start.3
  191.9 2.7 copy-start.4
  193.8 0.8 copy-start.8
  260.6 1.9 copy-start.2
  267.9 2.5 copy-start.7
  275.6 5.0 copy-start.10
  294.6 287.7 %all-reduce.2.cloned.1.call-start = ((), (), s32[]{:S(2)}) async-start(), calls=%async_computation.1 | async-start | bytes 1572864 | tf_op jit(solution)/shard_map/psum | solution.py:92
Sparse Core Ops, SparseCore 0:
  27.4 101.9 all-gather.6
  132.0 95.6 all-gather.4
  294.7 218.4 reduce-scatter.3
  515.5 66.7 all-reduce.1
where the time goes:
time: 594 us; the launch traced here: 591 us
  waiting for transfers between devices  385 us (65%)
  other arithmetic  95.1 us (16%)
  local copies, waits for them, and re-layouts  51.2 us (9%)
  matrix products  44.7 us (8%)
  between operations  13.9 us (2%)
    unnamed x5, waiting for transfers between devices  219 us
    all_gather x2, waiting for transfers between devices, carried_in(): pieces = lax.all_gather(value, axis)  106 us
    select_n x62, other arithmetic, lap(): return jnp.where(position < mine, longer, so_far)  87 us
    psum x1, waiting for transfers between devices, shards(): proj_grad = lax.psum(partial_rows, 'dp')  60.5 us
    unnamed x27, local copies, waits for them, and re-layouts  17.8 us
  transfers between devices with their start and end apart: 4, of which 4 were waited for; matrix products, arithmetic and copies ran while one was open for 17% of the time, Pallas kernels for 0%

commit v1 on v0

v1 whole, which is shorter than its diff:
```python
import functools

import jax
import jax.numpy as jnp
from jax import lax
from jax.experimental import pallas as pl
from jax.experimental.pallas import tpu as pltpu
from jax.sharding import Mesh, PartitionSpec as P

H = 4
HD = 128
CH = 256
NB = 4
D = H * HD
DM = 1024
TOK = NB * CH
F32 = jnp.float32
BF16 = jnp.bfloat16

NN = (((1,), (0,)), ((), ()))
NT = (((1,), (1,)), ((), ()))
TN = (((0,), (0,)), ((), ()))


def dot(a, b, dims):
    return lax.dot_general(a, b, dims, preferred_element_type=F32)


def params():
    return pltpu.CompilerParams(vmem_limit_bytes=56 * 1024 * 1024)


def head(part, h):
    return pl.ds(part * D + h * HD, HD)


def project_body(pos_ref, x_ref, w_ref, g_ref, qkv_ref, sg_ref, xt_ref, kv_ref, qg_ref, total_ref):
    n = pl.program_id(0)
    qkv_ref[...] = dot(x_ref[...], w_ref[...], NN).astype(BF16)
    pos = (pos_ref[0] + n * CH + lax.broadcasted_iota(jnp.int32, (CH, 1), 0)).astype(F32)
    factor = 1.0 / jnp.sqrt(jnp.float32(HD) * (pos + 1.0))
    sg_ref[...] = (g_ref[...].astype(F32) * factor).astype(BF16)
    xt_ref[...] = x_ref[...].T

    @pl.when(n == 0)
    def _():
        total_ref[...] = jnp.zeros_like(total_ref)

    for h in range(H):
        kv = dot(qkv_ref[:, head(1, h)], qkv_ref[:, head(2, h)], TN)
        qg = dot(qkv_ref[:, head(0, h)], sg_ref[:, pl.ds(h * HD, HD)], TN)
        kv_ref[0, h] = kv
        qg_ref[0, h] = qg
        total_ref[0, h] += kv
        total_ref[1, h] += qg


def project(offset, x, w, g):
    block = lambda cols: pl.BlockSpec((CH, cols), lambda n, s: (n, 0))
    sums = pl.BlockSpec((1, H, HD, HD), lambda n, s: (n, 0, 0, 0))
    return pl.pallas_call(
        project_body,
        grid_spec=pltpu.PrefetchScalarGridSpec(
            num_scalar_prefetch=1,
            grid=(NB,),
            in_specs=[block(DM), pl.BlockSpec((DM, 3 * D), lambda n, s: (0, 0)), block(D)],
            out_specs=[
                block(3 * D),
                block(D),
                pl.BlockSpec((DM, CH), lambda n, s: (0, n)),
                sums,
                sums,
                pl.BlockSpec((2, H, HD, HD), lambda n, s: (0, 0, 0, 0)),
            ],
        ),
        out_shape=[
            jax.ShapeDtypeStruct((TOK, 3 * D), BF16),
            jax.ShapeDtypeStruct((TOK, D), BF16),
            jax.ShapeDtypeStruct((DM, TOK), BF16),
            jax.ShapeDtypeStruct((NB, H, HD, HD), F32),
            jax.ShapeDtypeStruct((NB, H, HD, HD), F32),
            jax.ShapeDtypeStruct((2, H, HD, HD), F32),
        ],
        compiler_params=params(),
        name="project",
    )(offset, x, w, g)


def scan_body(count, back_ref, v_ref, o_ref):
    def step(t, so_far):
        i = jnp.where(back_ref[0] == 1, count - 1 - t, t)
        o_ref[i] = so_far
        return so_far + v_ref[i]

    lax.fori_loop(0, count, step, jnp.zeros(v_ref.shape[1:], F32))


def scan_states(back, v):
    return pl.pallas_call(
        functools.partial(scan_body, v.shape[0]),
        in_specs=[pl.BlockSpec(memory_space=pltpu.SMEM), pl.BlockSpec(memory_space=pltpu.VMEM)],
        out_specs=pl.BlockSpec(memory_space=pltpu.VMEM),
        out_shape=jax.ShapeDtypeStruct(v.shape, F32),
        compiler_params=params(),
        name="scan_states",
    )(back, v)


def grads_body(qkv_ref, sg_ref, kv_ref, qg_ref, s_ref, o_ref):
    n = pl.program_id(0)
    keep = lax.broadcasted_iota(jnp.int32, (CH, CH), 0) >= lax.broadcasted_iota(jnp.int32, (CH, CH), 1)
    for h in range(H):
        q, k, v = (qkv_ref[:, head(p, h)] for p in range(3))
        g = sg_ref[:, pl.ds(h * HD, HD)]
        before = s_ref[0, h]
        after = s_ref[1, h]
        for m in range(NB):
            before = before + jnp.where(m < n, kv_ref[m, h], 0.0)
            after = after + jnp.where(m > n, qg_ref[m, h], 0.0)
        before = before.astype(BF16)
        after = after.astype(BF16)
        mvg = jnp.where(keep, dot(g, v, NT), 0.0).astype(BF16)
        mqk = jnp.where(keep, dot(q, k, NT), 0.0).astype(BF16)
        dq = dot(mvg, k, NN) + dot(g, before, NT)
        dk = dot(mvg, q, TN) + dot(v, after, NT)
        dv = dot(mqk, g, TN) + dot(k, after, NN)
        for p, d in enumerate((dq, dk, dv)):
            o_ref[:, head(p, h)] = d.astype(BF16)


def grads(qkv, sg, kv, qg, states):
    block = lambda cols: pl.BlockSpec((CH, cols), lambda n: (n, 0))
    sums = pl.BlockSpec((NB, H, HD, HD), lambda n: (0, 0, 0, 0))
    return pl.pallas_call(
        grads_body,
        grid=(NB,),
        in_specs=[block(3 * D), block(D), sums, sums, pl.BlockSpec((2, H, HD, HD), lambda n: (0, 0, 0, 0))],
        out_specs=block(3 * D),
        out_shape=jax.ShapeDtypeStruct((TOK, 3 * D), BF16),
        compiler_params=params(),
        name="grads",
    )(qkv, sg, kv, qg, states)


def give_body(at_ref, xt_ref, d_ref, o_ref):
    o_ref[...] = dot(xt_ref[...], d_ref[...], NN)


def give_half(at, xt, dqkv):
    return pl.pallas_call(
        give_body,
        grid_spec=pltpu.PrefetchScalarGridSpec(
            num_scalar_prefetch=1,
            grid=(3,),
            in_specs=[
                pl.BlockSpec((DM, TOK), lambda j, s: (0, 0)),
                pl.BlockSpec((TOK, 256), lambda j, s: (0, 2 * j + 1 - s[0])),
            ],
            out_specs=pl.BlockSpec((DM, 256), lambda j, s: (0, j)),
        ),
        out_shape=jax.ShapeDtypeStruct((DM, 768), F32),
        compiler_params=params(),
        name="give_half",
    )(at, xt, dqkv)


def pick(at_ref, axis):
    mine, far, first, second = (at_ref[1 + 4 * axis + i] for i in range(4))
    return (mine, second), (first, far)


def keep_body(at_ref, xt_ref, d_ref, r_ref, kx_ref, sx_ref, ky_ref, sy_ref, s_ref):
    s_ref[...] = (dot(xt_ref[...], d_ref[...], NN) + r_ref[...]).reshape(8, 4, 4, 8, 256)
    kept, sent = pick(at_ref, 0)
    for i in range(2):
        kx_ref[:, :, i] = s_ref[:, :, kept[i], :, 0:128]
        sx_ref[:, :, i] = s_ref[:, :, sent[i], :, 0:128]
    kept, sent = pick(at_ref, 1)
    for i in range(2):
        ky_ref[:, i] = s_ref[:, kept[i], :, :, 128:256]
        sy_ref[:, i] = s_ref[:, sent[i], :, :, 128:256]


def keep_half(at, xt, dqkv, arrived):
    bx = pl.BlockSpec((8, 4, 2, 8, 128), lambda j, s: (0, 0, 0, 0, j))
    by = pl.BlockSpec((8, 2, 4, 8, 128), lambda j, s: (0, 0, 0, 0, j))
    return pl.pallas_call(
        keep_body,
        grid_spec=pltpu.PrefetchScalarGridSpec(
            num_scalar_prefetch=1,
            grid=(3,),
            in_specs=[
                pl.BlockSpec((DM, TOK), lambda j, s: (0, 0)),
                pl.BlockSpec((TOK, 256), lambda j, s: (0, 2 * j + s[0])),
                pl.BlockSpec((DM, 256), lambda j, s: (0, j)),
            ],
            out_specs=[bx, bx, by, by],
            scratch_shapes=[pltpu.VMEM((8, 4, 4, 8, 256), F32)],
        ),
        out_shape=[jax.ShapeDtypeStruct((8, 4, 2, 8, 384), F32)] * 2
        + [jax.ShapeDtypeStruct((8, 2, 4, 8, 384), F32)] * 2,
        compiler_params=params(),
        name="keep_half",
    )(at, xt, dqkv, arrived)


def whole_call(body, name, shapes, *args, scratch=()):
    vmem = pl.BlockSpec(memory_space=pltpu.VMEM)
    smem = pl.BlockSpec(memory_space=pltpu.SMEM)
    return pl.pallas_call(
        body,
        in_specs=[smem if a.dtype == jnp.int32 else vmem for a in args],
        out_specs=[vmem] * len(shapes),
        out_shape=[jax.ShapeDtypeStruct(s, F32) for s in shapes],
        scratch_shapes=list(scratch),
        compiler_params=params(),
        name=name,
    )(*args)


def add1_body(kx, rx, ky, ry, kx2, sx2, ky2, sy2):
    kx2[...] = kx[:, :, 0] + rx[:, :, 0]
    sx2[...] = kx[:, :, 1] + rx[:, :, 1]
    ky2[...] = ky[:, 0] + ry[:, 0]
    sy2[...] = ky[:, 1] + ry[:, 1]


def add2_body(at, kx, rx, ky, ry, kp, sp, kq, sq):
    for axis, k, r, ko, so in ((1, kx, rx, kp, sp), (0, ky, ry, kq, sq)):
        kept, sent = pick(at, axis)
        for i in range(2):
            ko[:, i] = k[:, kept[i]] + r[:, kept[i]]
            so[:, i] = k[:, sent[i]] + r[:, sent[i]]


def add3_body(kp, rp, kq, rq, kp2, sp2, kq2, sq2):
    for k, r, ko, so in ((kp, rp, kp2, sp2), (kq, rq, kq2, sq2)):
        ko[...] = k[:, 0] + r[:, 0]
        so[...] = k[:, 1] + r[:, 1]


def add4_body(kp, rp, kq, rq, o):
    o[:, :, 0:384] = kp[...] + rp[...]
    o[:, :, 384:768] = kq[...] + rq[...]


def sum_body(v, o):
    total = v[0]
    for i in range(1, v.shape[0]):
        total = total + v[i]
    o[...] = total


def rows_body(at, a0, a1, a2, a3, o):
    x = at[1]
    for d, a in enumerate((a0, a1, a2, a3)):
        o[(x + 4 - d) % 4] = a[...]


def columns_body(at, mine, other, o):
    c = at[0]

    def put(core, a):
        for j in range(3):
            for half in range(2):
                value = a[:, half * 384 + j * 128 : half * 384 + (j + 1) * 128]
                o[:, j * 512 + core * 256 + half * 128 : j * 512 + core * 256 + (half + 1) * 128] = value

    @pl.when(c == 0)
    def _():
        put(0, mine[...])
        put(1, other[...])

    @pl.when(c == 1)
    def _():
        put(1, mine[...])
        put(0, other[...])


def exchange(value, axis, step):
    pairs = []
    for i in range(4):
        for c in range(2):
            j = i ^ ((1, 3), (3, 1))[c][step]
            pairs.append((2 * i + c, 2 * j + c))
    return lax.ppermute(value, (axis, "core"), pairs)


def shards(inputs, weights, out_grad):
    x = inputs[0]
    z_at, y_at, x_at, core = (lax.axis_index(a) for a in ("z", "y", "x", "core"))
    tm_at = z_at * 4 + y_at
    first = jnp.where(core == 0, 1, 3)
    second = 4 - first
    at = jnp.stack(
        [core]
        + [v for i in (x_at, y_at) for v in (i, i ^ first ^ second, i ^ first, i ^ second)]
    ).astype(jnp.int32)
    offset = (tm_at * TOK).astype(jnp.int32)[None]
    back = (tm_at >= 16).astype(jnp.int32)[None]

    qkv, sg, xt, kv, qg, total = project(offset, x, weights, out_grad[0])
    slices = lax.all_to_all(total.reshape(32, 32, HD), ("z", "y"), 0, 0, tiled=True)
    states = lax.all_to_all(scan_states(back, slices), ("z", "y"), 0, 0, tiled=True)
    dqkv = grads(qkv, sg, kv, qg, states.reshape(2, H, HD, HD))

    given = give_half(at, xt, dqkv)
    arrived = lax.ppermute(given, "core", [(0, 1), (1, 0)])
    record_grad = dot(dqkv, weights, NT).astype(BF16)
    arrived, record_grad = lax.optimization_barrier((arrived, record_grad))
    kx, sx, ky, sy = keep_half(at, xt, dqkv, arrived)
    rx = exchange(sx, "x", 0)
    ry = exchange(sy, "y", 0)
    kx, sx, ky, sy = whole_call(add1_body, "add1", [(8, 4, 8, 384)] * 4, kx, rx, ky, ry)
    rx = exchange(sx, "x", 1)
    ry = exchange(sy, "y", 1)
    kp, sp, kq, sq = whole_call(add2_body, "add2", [(8, 2, 8, 384)] * 4, at, kx, rx, ky, ry)
    rp = exchange(sp, "y", 0)
    rq = exchange(sq, "x", 0)
    kp, sp, kq, sq = whole_call(add3_body, "add3", [(8, 8, 384)] * 4, kp, rp, kq, rq)
    rp = exchange(sp, "y", 1)
    rq = exchange(sq, "x", 1)
    (part,) = whole_call(add4_body, "add4", [(8, 8, 768)], kp, rp, kq, rq)
    part = lax.all_to_all(part, "z", 0, 0, tiled=True)
    (mine,) = whole_call(sum_body, "sum_z", [(8, 768)], part)
    around = [mine] + [
        lax.ppermute(mine, "x", [(i, (i + d) % 4) for i in range(4)]) for d in range(1, 4)
    ]
    (rows,) = whole_call(rows_body, "rows", [(4, 8, 768)], at, *around)
    rows = rows.reshape(32, 768)
    other = lax.ppermute(rows, "core", [(0, 1), (1, 0)])
    (proj_grad,) = whole_call(columns_body, "columns", [(32, 3 * D)], at, rows, other)
    return record_grad[None], proj_grad


def solution(mesh):
    fine = Mesh(mesh.devices.reshape(8, 4, 4, 2), ("z", "y", "x", "core"))
    tm, dp = ("z", "y"), ("x", "core")
    placed = (P(dp, tm, None), P(), P(dp, tm, None))
    return jax.shard_map(
        shards,
        mesh=fine,
        in_specs=placed,
        out_specs=(P(dp, tm, None), P(tm, None)),
        check_vma=False,
    )
```

time: 594 us -> 174 us (0.29)
  waiting for transfers between devices: 385 us -> 61.4 us
  other arithmetic: 95.1 us -> 0 us
  Pallas kernels: 0 us -> 48.1 us
  local copies, waits for them, and re-layouts: 51.2 us -> 7.26 us
  matrix products: 44.7 us -> 4.62 us
  starting transfers between devices: 0.34 us -> 38.8 us
  between operations: 13.9 us -> 0.73 us
  blocking collectives: 0 us -> 12.6 us
    unnamed x5 -> x0, waiting for transfers between devices: 219 us -> none
    all_gather x2 -> x0, waiting for transfers between devices: 106 us -> none  [carried_in(): pieces = lax.all_gather(value, axis)]
    select_n x62 -> x0, other arithmetic: 87 us -> none  [lap(): return jnp.where(position < mine, longer, so_far)]
    psum x1 -> x0, waiting for transfers between devices: 60.5 us -> none  [shards(): proj_grad = lax.psum(partial_rows, 'dp')]
    pallas_call x0 -> x12, Pallas kernels: none -> 48.1 us  [the longest x7 13.7 us: whole_call(): pl.pallas_call(body, in_specs=[smem if a.dtype == jnp.int32 else vmem for...]
    dot_general x12 -> x1, matrix products: 44.7 us -> 4.62 us  [dot(): return lax.dot_general(a, b, dims, preferred_element_type=F32)]
    ppermute x0 -> x13, waiting for transfers between devices: none -> 30.8 us  [the longest x8 26.2 us: exchange(): return lax.ppermute(value, (axis, 'core'), pairs)]
    all_to_all x0 -> x2, waiting for transfers between devices: none -> 30.6 us  [the longest x1 16.3 us: shards(): lax.all_to_all(total.reshape(32, 32, HD), ('z', 'y'), 0, 0, tiled=True)]
  transfers between devices with their start and end apart: 4 -> 15, of which waited for: 4 -> 12; matrix products, arithmetic and copies ran while one was open for 17% -> 3% of each run, Pallas kernels for 0% -> 0%
where the time goes in v1:
time: 174 us
  waiting for transfers between devices  61.4 us (35%)
  Pallas kernels  48.1 us (28%)
  starting transfers between devices  38.8 us (22%)
  blocking collectives  12.6 us (7%)
  local copies, waits for them, and re-layouts  7.26 us (4%)
  matrix products  4.62 us (3%)
    ppermute x8, waiting for transfers between devices, exchange(): return lax.ppermute(value, (axis, 'core'), pairs)  26.2 us
    all_to_all x1, waiting for transfers between devices, shards(): lax.all_to_all(total.reshape(32, 32, HD), ('z', 'y'), 0, 0, tiled=True)  16.3 us
    all_to_all x1, waiting for transfers between devices, shards(): lax.all_to_all(scan_states(back, slices), ('z', 'y'), 0, 0, tiled=True)  14.4 us
    pallas_call x7, Pallas kernels, whole_call(): pl.pallas_call(body, in_specs=[smem if a.dtype == jnp.int32 else vmem for...  13.7 us
    all_to_all x1, blocking collectives, shards(): part = lax.all_to_all(part, 'z', 0, 0, tiled=True)  12.6 us
    all_to_all x1, starting transfers between devices, shards(): lax.all_to_all(total.reshape(32, 32, HD), ('z', 'y'), 0, 0, tiled=True)  12 us
    pallas_call x1, Pallas kernels, project(): pl.pallas_call(project_body, grid_spec=pltpu.PrefetchScalarGridSpec(num_s...  9.45 us
    pallas_call x1, Pallas kernels, grads(): pl.pallas_call(grads_body, grid=(NB,), in_specs=[block(3 * D), block(D),...  8.77 us
  transfers between devices with their start and end apart: 15, of which 12 were waited for; matrix products, arithmetic and copies ran while one was open for 3% of the time, Pallas kernels for 0%

profile of v1, /device:TPU:1, one launch (start us, length us, event | category | flops | bytes accessed | tf_op | source)
XLA Modules:
  0.0 173.5 jit_solution(7089242059688955798)
XLA Ops:
  0.6 9.5 %project.1 = (bf16[1024,1536]{1,0:T(8,128)(2,1)}, bf16[1024,512]{1,0:T(8,128)(2,1)}, bf16[1024,1024]{1,0:T(8,128)(2,1)}, f32[4,4,128,128]{3,2,1,0:T(8,128)}, f32...) custom-call(s32[1]{0:T(128)} %bitcast.9.pos_ref, bf16[1024,1024]{1,0:T(8,128)(2,1)} %bitcast.19, ...), custom_call_target="tpu_custom_call" | custom-call | tf_op jit(solution)/shard_map/project/pallas_call | solution.py:61
  10.1 12.0 %all-to-all-start = ((f32[32,32,128]{2,1,0:T(8,128)}), f32[32,32,128]{2,1,0:T(8,128)S(1)}, u32[]{:S(2)}, u32[]{:S(2)}) async-start(f32[32,32,128]{2,1,0:T(8,128)} %bitcast.22), calls=%async_computation | async-start | bytes 1048576 | tf_op jit(solution)/shard_map/all_to_all | solution.py:303
  22.2 16.3 %all-to-all-done.v_ref = f32[32,32,128]{2,1,0:T(8,128)S(1)} async-done(((f32[32,32,128]{2,1,0:T(8,128)}), f32[32,32,128]{2,1,0:T(8,128)S(1)}, u32[]{:S(2)}, u32[]{:S(2)}) %all-to-all-start) | async-done | bytes 524320 | tf_op jit(solution)/shard_map/all_to_all | solution.py:303
  38.4 0.0 copy-start.3
  38.4 0.8 copy-done.3
  39.2 2.1 %scan_states.1 = f32[32,32,128]{2,1,0:T(8,128)} custom-call(s32[1]{0:T(128)} %bitcast.12.back_ref, f32[32,32,128]{2,1,0:T(8,128)} %copy-done.3), custom_call_target="tpu_custom_call" | custom-call | tf_op jit(solution)/shard_map/scan_states/pallas_call | solution.py:99
  41.3 5.2 %all-to-all-start.1 = ((f32[32,32,128]{2,1,0:T(8,128)}), f32[32,32,128]{2,1,0:T(8,128)S(1)}, u32[]{:S(2)}, u32[]{:S(2)}) async-start(f32[32,32,128]{2,1,0:T(8,128)} %scan_states.1), calls=%async_computation.1 | async-start | bytes 1048576 | tf_op jit(solution)/shard_map/all_to_all | solution.py:304
  46.6 0.7 stack.39.at_ref.at
  47.3 14.4 %all-to-all-done.1 = f32[32,32,128]{2,1,0:T(8,128)S(1)} async-done(((f32[32,32,128]{2,1,0:T(8,128)}), f32[32,32,128]{2,1,0:T(8,128)S(1)}, u32[]{:S(2)}, u32[]{:S(2)}) %all-to-all-start.1) | async-done | bytes 524320 | tf_op jit(solution)/shard_map/all_to_all | solution.py:304
  61.6 0.0 copy-start.2
  61.6 0.8 copy-done.2
  62.4 8.8 %grads.1.d_ref = bf16[1024,1536]{1,0:T(8,128)(2,1)} custom-call(bf16[1024,1536]{1,0:T(8,128)(2,1)} %get-tuple-element.27.qkv_ref, bf16[1024,512]{1,0:T(8,128)(2,1)} %get-tuple-element.28.sg_ref, f32[4,4,128,128]{3,2,1,0:T(8,128)} %get-tuple-element.29.kv_ref, f32[4,4,128,128]{3,2,1,0:T(8,128)} %get-tuple-element.30.qg_ref, f32[2,4,128,128]{3,2,1,0:T(8,128)} %bitcast.20), custom_call_target="tpu_custom_call" | custom-call | tf_op jit(solution)/shard_map/grads/pallas_call | solution.py:134
  71.2 0.0 copy-start
  71.2 6.9 %give_half.1 = f32[1024,768]{1,0:T(8,128)} custom-call(s32[9]{0:T(128)} %stack.39.at_ref.at, bf16[1024,1024]{1,0:T(8,128)(2,1)} %get-tuple-element.26.xt_ref, bf16[1024,1536]{1,0:T(8,128)(2,1)} %grads.1.d_ref), custom_call_target="tpu_custom_call" | custom-call | tf_op jit(solution)/shard_map/give_half/pallas_call | solution.py:150
  78.1 3.8 %collective-permute-start = (f32[1024,768]{1,0:T(8,128)}, f32[1024,768]{1,0:T(8,128)}, u32[]{:S(2)}, u32[]{:S(2)}) collective-permute-start(f32[1024,768]{1,0:T(8,128)} %give_half.1), channel_id=1, source_target_pairs={{0,1},{1,0},{2,3},{3,2},{4,5},{5,4},{6,7},{7,6},{8,9},{9,8},{10,11... | collective-permute-start | bytes 9437192 | tf_op jit(solution)/shard_map/ppermute | solution.py:308
  81.8 0.0 copy-done
  81.9 0.0 copy-done.1
  81.9 4.6 %convolution_convert_fusion = bf16[1024,1024]{1,0:T(8,128)(2,1)} fusion(bf16[1024,1536]{1,0:T(8,128)(2,1)S(1)} %copy-done, bf16[1024,1536]{1,0:T(8,128)(2,1)S(1)} %copy-done.1), kind=kOutput, calls=%fused_computation | convolution fusion | flops 3222274048 | bytes 8388608 | tf_op jit(solution)/shard_map/dot_general | solution.py:26
  86.5 1.0 collective-permute-done.r_ref
  87.5 7.2 %keep_half.1 = (f32[8,4,2,8,384]{4,3,2,1,0:T(8,128)}, f32[8,4,2,8,384]{4,3,2,1,0:T(8,128)}, f32[8,2,4,8,384]{4,3,2,1,0:T(8,128)}, f32[8,2,4,8,384]{4,3,2,1,0:T(8,128)}) custom-call(s32[9]{0:T(128)} %stack.39.at_ref.at, bf16[1024,1024]{1,0:T(8,128)(2,1)} %get-tuple-element.26.xt_ref, bf16[1024,1536]{1,0:T(8,128)(2,1)} %grads.1.d_ref, ...), custom_call_target="tpu_custom_call" | custom-call | tf_op jit(solution)/shard_map/keep_half/pallas_call | solution.py:187
  94.7 2.5 %collective-permute-start.1 = (f32[8,4,2,8,384]{4,3,2,1,0:T(8,128)}, f32[8,4,2,8,384]{4,3,2,1,0:T(8,128)S(1)}, u32[]{:S(2)}, u32[]{:S(2)}) collective-permute-start(f32[8,4,2,8,384]{4,3,2,1,0:T(8,128)} %get-tuple-element.35), channel_id=1, source_target_pairs={{0,2},{1,7},{2,0},{3,5},{4,6},{5,3},{6,4},{7,1},{8,10},{9,15},{10,... | collective-permute-start | bytes 2359304 | tf_op jit(solution)/shard_map/ppermute | solution.py:286
  97.2 1.7 collective-permute-start.2
  98.8 8.1 %collective-permute-done.1.rx = f32[8,4,2,8,384]{4,3,2,1,0:T(8,128)S(1)} collective-permute-done((f32[8,4,2,8,384]{4,3,2,1,0:T(8,128)}, f32[8,4,2,8,384]{4,3,2,1,0:T(8,128)S(1)}, u32[]{:S(2)}, u32[]{:S(2)}) %collective-permute-start.1) | collective-permute-done | bytes 786464 | tf_op jit(solution)/shard_map/ppermute | solution.py:286
  106.9 2.5 %collective-permute-done.2.ry = f32[8,2,4,8,384]{4,3,2,1,0:T(8,128)S(1)} collective-permute-done((f32[8,2,4,8,384]{4,3,2,1,0:T(8,128)}, f32[8,2,4,8,384]{4,3,2,1,0:T(8,128)S(1)}, u32[]{:S(2)}, u32[]{:S(2)}) %collective-permute-start.2) | collective-permute-done | bytes 786464 | tf_op jit(solution)/shard_map/ppermute | solution.py:286
  109.4 0.0 copy-done.4
  109.4 0.9 copy-done.5
  110.3 3.0 %add1.1 = (f32[8,4,8,384]{3,2,1,0:T(8,128)}, f32[8,4,8,384]{3,2,1,0:T(8,128)}, f32[8,4,8,384]{3,2,1,0:T(8,128)}, f32[8,4,8,384]{3,2,1,0:T(8,128)}) custom-call(f32[8,4,2,8,384]{4,3,2,1,0:T(8,128)} %get-tuple-element.34.kx, f32[8,4,2,8,384]{4,3,2,1,0:T(8,128)} %copy-done.4, f32[8,2,4,8,384]{4,3,2,1,0:T(8,128)} %get-tuple-element.36.ky, ...), custom_call_target="tpu_custom_call" | custom-call | tf_op jit(solution)/shard_map/add1/pallas_call | solution.py:210
  113.4 0.0 collective-permute-start.3
  113.4 0.0 collective-permute-start.4
  113.4 7.1 %collective-permute-done.3.rx = f32[8,4,8,384]{3,2,1,0:T(8,128)S(1)} collective-permute-done((f32[8,4,8,384]{3,2,1,0:T(8,128)}, f32[8,4,8,384]{3,2,1,0:T(8,128)S(1)}, u32[]{:S(2)}, u32[]{:S(2)}) %collective-permute-start.3) | collective-permute-done | bytes 393248 | tf_op jit(solution)/shard_map/ppermute | solution.py:286
  120.5 0.0 collective-permute-done.4.ry
  120.5 0.7 copy-done.6
  121.3 0.1 copy-done.7
  121.4 2.3 %add2.1 = (f32[8,2,8,384]{3,2,1,0:T(8,128)}, f32[8,2,8,384]{3,2,1,0:T(8,128)}, f32[8,2,8,384]{3,2,1,0:T(8,128)}, f32[8,2,8,384]{3,2,1,0:T(8,128)}) custom-call(s32[9]{0:T(128)} %stack.39.at_ref.at, f32[8,4,8,384]{3,2,1,0:T(8,128)} %get-tuple-element.38.kx, f32[8,4,8,384]{3,2,1,0:T(8,128)} %copy-done.6, f32[8,4,8,384]{3,2,1,0:T(8,128)} %get-tuple-element.40.ky, ...), custom_call_target="tpu_custom_call" | custom-call | tf_op jit(solution)/shard_map/add2/pallas_call | solution.py:210
  123.7 1.7 collective-permute-start.5
  125.4 0.7 collective-permute-start.6
  126.1 3.6 %collective-permute-done.5.rp = f32[8,2,8,384]{3,2,1,0:T(8,128)S(1)} collective-permute-done((f32[8,2,8,384]{3,2,1,0:T(8,128)}, f32[8,2,8,384]{3,2,1,0:T(8,128)S(1)}, u32[]{:S(2)}, u32[]{:S(2)}) %collective-permute-start.5) | collective-permute-done | bytes 196640 | tf_op jit(solution)/shard_map/ppermute | solution.py:286
  129.6 1.7 collective-permute-done.6.rq
  131.3 0.0 copy-done.8
  131.3 0.7 copy-done.9
  132.0 2.0 %add3.1 = (f32[8,8,384]{2,1,0:T(8,128)}, f32[8,8,384]{2,1,0:T(8,128)}, f32[8,8,384]{2,1,0:T(8,128)}, f32[8,8,384]{2,1,0:T(8,128)}) custom-call(f32[8,2,8,384]{3,2,1,0:T(8,128)} %get-tuple-element.42.kp, f32[8,2,8,384]{3,2,1,0:T(8,128)} %copy-done.8, f32[8,2,8,384]{3,2,1,0:T(8,128)} %get-tuple-element.44.kq, f32[8,2,8,384]{3,2,1,0:T(8,128)} %copy-done.9), custom_call_target="tpu_custom_call" | custom-call | tf_op jit(solution)/shard_map/add3/pallas_call | solution.py:210
  134.0 0.0 collective-permute-start.7
  134.0 0.4 collective-permute-start.8
  134.4 3.3 %collective-permute-done.7.rp = f32[8,8,384]{2,1,0:T(8,128)S(1)} collective-permute-done((f32[8,8,384]{2,1,0:T(8,128)}, f32[8,8,384]{2,1,0:T(8,128)S(1)}, u32[]{:S(2)}, u32[]{:S(2)}) %collective-permute-start.7) | collective-permute-done | bytes 98336 | tf_op jit(solution)/shard_map/ppermute | solution.py:286
  137.7 0.0 collective-permute-done.8.rq
  137.7 0.6 copy-done.10
  138.3 0.0 copy-done.11
  138.3 1.7 add4.1
  140.1 12.6 %all_to_all.15.v = f32[8,8,768]{2,1,0:T(8,128)} all-to-all(f32[8,8,768]{2,1,0:T(8,128)} %add4.1), channel_id=1, replica_groups=mesh['z'=8,'y'=4,'x'=4,'core'=2] {'z'}, dimensions={0} | all-to-all | bytes 393216 | tf_op jit(solution)/shard_map/all_to_all | solution.py:324
  152.7 1.5 sum_z.1.a0
  154.3 0.4 collective-permute-start.9
  154.7 1.4 collective-permute-start.10
  156.1 1.0 collective-permute-start.11
  157.1 1.7 collective-permute-done.9.a1
  158.8 0.7 collective-permute-done.10.a2
  159.4 0.0 collective-permute-done.11.a3
  159.4 0.0 copy-done.13
  159.5 0.6 copy-done.14
  160.0 0.6 copy-done.15
  160.6 1.5 rows.1
  162.1 8.0 %collective-permute-start.12 = (f32[32,768]{1,0:T(8,128)}, f32[32,768]{1,0:T(8,128)S(1)}, u32[]{:S(2)}, u32[]{:S(2)}) collective-permute-start(f32[32,768]{1,0:T(8,128)} %bitcast.23), channel_id=1, source_target_pairs={{0,1},{1,0},{2,3},{3,2},{4,5},{5,4},{6,7},{7,6},{8,9},{9,8},{10,11... | collective-permute-start | bytes 294920 | tf_op jit(solution)/shard_map/ppermute | solution.py:331
  170.1 1.2 collective-permute-done.12.other
  171.2 0.6 copy-done.12
  171.9 1.6 columns.1
  (13 shorter events, 0.0 us)
Async XLA Ops:
  10.1 28.3 %all-to-all-start = ((f32[32,32,128]{2,1,0:T(8,128)}), f32[32,32,128]{2,1,0:T(8,128)S(1)}, u32[]{:S(2)}, u32[]{:S(2)}) async-start(f32[32,32,128]{2,1,0:T(8,128)} %bitcast.22), calls=%async_computation | async-start | bytes 1048576 | tf_op jit(solution)/shard_map/all_to_all | solution.py:303
  38.4 0.8 copy-start.3
  41.3 20.3 %all-to-all-start.1 = ((f32[32,32,128]{2,1,0:T(8,128)}), f32[32,32,128]{2,1,0:T(8,128)S(1)}, u32[]{:S(2)}, u32[]{:S(2)}) async-start(f32[32,32,128]{2,1,0:T(8,128)} %scan_states.1), calls=%async_computation.1 | async-start | bytes 1048576 | tf_op jit(solution)/shard_map/all_to_all | solution.py:304
  61.6 0.8 copy-start.2
  71.2 10.6 %copy-start = (bf16[1024,1536]{1,0:T(8,128)(2,1)S(1)}, bf16[1024,1536]{1,0:T(8,128)(2,1)}, u32[]{:S(2)}) copy-start(bf16[1024,1536]{1,0:T(8,128)(2,1)} %grads.1.d_ref) | copy-start | bytes 9437188
  71.2 10.6 %copy-start.1 = (bf16[1024,1536]{1,0:T(8,128)(2,1)S(1)}, bf16[1024,1536]{1,0:T(8,128)(2,1)}, u32[]{:S(2)}) copy-start(bf16[1024,1536]{1,0:T(8,128)(2,1)} %w_ref.1) | copy-start | bytes 9437188
  78.1 9.4 %collective-permute-start = (f32[1024,768]{1,0:T(8,128)}, f32[1024,768]{1,0:T(8,128)}, u32[]{:S(2)}, u32[]{:S(2)}) collective-permute-start(f32[1024,768]{1,0:T(8,128)} %give_half.1), channel_id=1, source_target_pairs={{0,1},{1,0},{2,3},{3,2},{4,5},{5,4},{6,7},{7,6},{8,9},{9,8},{10,11... | collective-permute-start | bytes 9437192 | tf_op jit(solution)/shard_map/ppermute | solution.py:308
  94.7 12.3 %collective-permute-start.1 = (f32[8,4,2,8,384]{4,3,2,1,0:T(8,128)}, f32[8,4,2,8,384]{4,3,2,1,0:T(8,128)S(1)}, u32[]{:S(2)}, u32[]{:S(2)}) collective-permute-start(f32[8,4,2,8,384]{4,3,2,1,0:T(8,128)} %get-tuple-element.35), channel_id=1, source_target_pairs={{0,2},{1,7},{2,0},{3,5},{4,6},{5,3},{6,4},{7,1},{8,10},{9,15},{10,... | collective-permute-start | bytes 2359304 | tf_op jit(solution)/shard_map/ppermute | solution.py:286
  97.2 12.3 %collective-permute-start.2 = (f32[8,2,4,8,384]{4,3,2,1,0:T(8,128)}, f32[8,2,4,8,384]{4,3,2,1,0:T(8,128)S(1)}, u32[]{:S(2)}, u32[]{:S(2)}) collective-permute-start(f32[8,2,4,8,384]{4,3,2,1,0:T(8,128)} %get-tuple-element.37), channel_id=1, source_target_pairs={{0,8},{1,25},{8,0},{9,17},{16,24},{17,9},{24,16},{25,1},{2,10},{3,... | collective-permute-start | bytes 2359304 | tf_op jit(solution)/shard_map/ppermute | solution.py:286
  106.9 2.5 %copy-start.4 = (f32[8,4,2,8,384]{4,3,2,1,0:T(8,128)}, f32[8,4,2,8,384]{4,3,2,1,0:T(8,128)S(1)}, u32[]{:S(2)}) copy-start(f32[8,4,2,8,384]{4,3,2,1,0:T(8,128)S(1)} %collective-permute-done.1.rx) | copy-start | bytes 2359300
  109.4 0.9 copy-start.5
  113.4 7.1 %collective-permute-start.3 = (f32[8,4,8,384]{3,2,1,0:T(8,128)}, f32[8,4,8,384]{3,2,1,0:T(8,128)S(1)}, u32[]{:S(2)}, u32[]{:S(2)}) collective-permute-start(f32[8,4,8,384]{3,2,1,0:T(8,128)} %get-tuple-element.39), channel_id=1, source_target_pairs={{0,6},{1,3},{2,4},{3,1},{4,2},{5,7},{6,0},{7,5},{8,14},{9,11},{10,... | collective-permute-start | bytes 1179656 | tf_op jit(solution)/shard_map/ppermute | solution.py:286
  113.4 7.1 %collective-permute-start.4 = (f32[8,4,8,384]{3,2,1,0:T(8,128)}, f32[8,4,8,384]{3,2,1,0:T(8,128)S(1)}, u32[]{:S(2)}, u32[]{:S(2)}) collective-permute-start(f32[8,4,8,384]{3,2,1,0:T(8,128)} %get-tuple-element.41), channel_id=1, source_target_pairs={{0,24},{1,9},{8,16},{9,1},{16,8},{17,25},{24,0},{25,17},{2,26},{3,... | collective-permute-start | bytes 1179656 | tf_op jit(solution)/shard_map/ppermute | solution.py:286
  120.5 0.7 copy-start.6
  120.5 0.9 copy-start.7
  123.7 5.9 %collective-permute-start.5 = (f32[8,2,8,384]{3,2,1,0:T(8,128)}, f32[8,2,8,384]{3,2,1,0:T(8,128)S(1)}, u32[]{:S(2)}, u32[]{:S(2)}) collective-permute-start(f32[8,2,8,384]{3,2,1,0:T(8,128)} %get-tuple-element.43), channel_id=1, source_target_pairs={{0,8},{1,25},{8,0},{9,17},{16,24},{17,9},{24,16},{25,1},{2,10},{3,... | collective-permute-start | bytes 589832 | tf_op jit(solution)/shard_map/ppermute | solution.py:286
  125.4 5.9 %collective-permute-start.6 = (f32[8,2,8,384]{3,2,1,0:T(8,128)}, f32[8,2,8,384]{3,2,1,0:T(8,128)S(1)}, u32[]{:S(2)}, u32[]{:S(2)}) collective-permute-start(f32[8,2,8,384]{3,2,1,0:T(8,128)} %get-tuple-element.45), channel_id=1, source_target_pairs={{0,2},{1,7},{2,0},{3,5},{4,6},{5,3},{6,4},{7,1},{8,10},{9,15},{10,... | collective-permute-start | bytes 589832 | tf_op jit(solution)/shard_map/ppermute | solution.py:286
  129.6 1.7 copy-start.8
  131.3 0.7 copy-start.9
  134.0 3.7 %collective-permute-start.7 = (f32[8,8,384]{2,1,0:T(8,128)}, f32[8,8,384]{2,1,0:T(8,128)S(1)}, u32[]{:S(2)}, u32[]{:S(2)}) collective-permute-start(f32[8,8,384]{2,1,0:T(8,128)} %get-tuple-element.47), channel_id=1, source_target_pairs={{0,24},{1,9},{8,16},{9,1},{16,8},{17,25},{24,0},{25,17},{2,26},{3,... | collective-permute-start | bytes 294920 | tf_op jit(solution)/shard_map/ppermute | solution.py:286
  134.0 3.7 %collective-permute-start.8 = (f32[8,8,384]{2,1,0:T(8,128)}, f32[8,8,384]{2,1,0:T(8,128)S(1)}, u32[]{:S(2)}, u32[]{:S(2)}) collective-permute-start(f32[8,8,384]{2,1,0:T(8,128)} %get-tuple-element.49), channel_id=1, source_target_pairs={{0,6},{1,3},{2,4},{3,1},{4,2},{5,7},{6,0},{7,5},{8,14},{9,11},{10,... | collective-permute-start | bytes 294920 | tf_op jit(solution)/shard_map/ppermute | solution.py:286
  137.7 0.6 copy-start.10
  137.7 0.7 copy-start.11
  154.3 4.5 %collective-permute-start.9 = (f32[8,768]{1,0:T(8,128)}, f32[8,768]{1,0:T(8,128)S(1)}, u32[]{:S(2)}, u32[]{:S(2)}) collective-permute-start(f32[8,768]{1,0:T(8,128)} %sum_z.1.a0), channel_id=1, source_target_pairs={{0,2},{2,4},{4,6},{6,0},{1,3},{3,5},{5,7},{7,1},{8,10},{10,12},{12... | collective-permute-start | bytes 73736 | tf_op jit(solution)/shard_map/ppermute | solution.py:327
  154.7 4.8 %collective-permute-start.10 = (f32[8,768]{1,0:T(8,128)}, f32[8,768]{1,0:T(8,128)S(1)}, u32[]{:S(2)}, u32[]{:S(2)}) collective-permute-start(f32[8,768]{1,0:T(8,128)} %sum_z.1.a0), channel_id=1, source_target_pairs={{0,4},{2,6},{4,0},{6,2},{1,5},{3,7},{5,1},{7,3},{8,12},{10,14},{12... | collective-permute-start | bytes 73736 | tf_op jit(solution)/shard_map/ppermute | solution.py:327
  156.1 3.3 %collective-permute-start.11 = (f32[8,768]{1,0:T(8,128)}, f32[8,768]{1,0:T(8,128)S(1)}, u32[]{:S(2)}, u32[]{:S(2)}) collective-permute-start(f32[8,768]{1,0:T(8,128)} %sum_z.1.a0), channel_id=1, source_target_pairs={{0,6},{2,0},{4,2},{6,4},{1,7},{3,1},{5,3},{7,5},{8,14},{10,8},{12,... | collective-permute-start | bytes 73736 | tf_op jit(solution)/shard_map/ppermute | solution.py:327
  158.8 0.7 copy-start.13
  159.4 0.6 copy-start.14
  160.0 0.6 copy-start.15
  162.1 9.1 %collective-permute-start.12 = (f32[32,768]{1,0:T(8,128)}, f32[32,768]{1,0:T(8,128)S(1)}, u32[]{:S(2)}, u32[]{:S(2)}) collective-permute-start(f32[32,768]{1,0:T(8,128)} %bitcast.23), channel_id=1, source_target_pairs={{0,1},{1,0},{2,3},{3,2},{4,5},{5,4},{6,7},{7,6},{8,9},{9,8},{10,11... | collective-permute-start | bytes 294920 | tf_op jit(solution)/shard_map/ppermute | solution.py:331
  171.2 0.6 copy-start.12

commit v2 on v1

v2 whole, which is shorter than its diff:
```python
import functools

import jax
import jax.numpy as jnp
from jax import lax
from jax.experimental import pallas as pl
from jax.experimental.pallas import tpu as pltpu
from jax.sharding import Mesh, PartitionSpec as P

H = 4
HD = 128
CH = 256
NB = 4
D = H * HD
DM = 1024
TOK = NB * CH
F32 = jnp.float32
BF16 = jnp.bfloat16

NN = (((1,), (0,)), ((), ()))
NT = (((1,), (1,)), ((), ()))
TN = (((0,), (0,)), ((), ()))


def dot(a, b, dims):
    return lax.dot_general(a, b, dims, preferred_element_type=F32)


MIB = 1024 * 1024
SWAP = [(0, 1), (1, 0)]


def params(mib=40):
    return pltpu.CompilerParams(vmem_limit_bytes=mib * MIB)


def cost(flops, moved):
    return pl.CostEstimate(flops=int(flops), bytes_accessed=int(moved), transcendentals=0)


def head(part, h):
    return pl.ds(part * D + h * HD, HD)


def project_body(pos_ref, x_ref, w_ref, g_ref, qkv_ref, sg_ref, kv_ref, qg_ref, total_ref):
    n = pl.program_id(0)
    qkv_ref[...] = dot(x_ref[...], w_ref[...], NN).astype(BF16)
    pos = (pos_ref[0] + n * CH + lax.broadcasted_iota(jnp.int32, (CH, 1), 0)).astype(F32)
    factor = 1.0 / jnp.sqrt(jnp.float32(HD) * (pos + 1.0))
    sg_ref[...] = (g_ref[...].astype(F32) * factor).astype(BF16)

    @pl.when(n == 0)
    def _():
        total_ref[...] = jnp.zeros_like(total_ref)

    for h in range(H):
        kv = dot(qkv_ref[:, head(1, h)], qkv_ref[:, head(2, h)], TN)
        qg = dot(qkv_ref[:, head(0, h)], sg_ref[:, pl.ds(h * HD, HD)], TN)
        kv_ref[0, h] = kv
        qg_ref[0, h] = qg
        total_ref[0, h] += kv
        total_ref[1, h] += qg


def project(offset, x, w, g):
    block = lambda cols: pl.BlockSpec((CH, cols), lambda n, s: (n, 0))
    sums = pl.BlockSpec((1, H, HD, HD), lambda n, s: (n, 0, 0, 0))
    return pl.pallas_call(
        project_body,
        grid_spec=pltpu.PrefetchScalarGridSpec(
            num_scalar_prefetch=1,
            grid=(NB,),
            in_specs=[block(DM), pl.BlockSpec((DM, 3 * D), lambda n, s: (0, 0)), block(D)],
            out_specs=[
                block(3 * D),
                block(D),
                sums,
                sums,
                pl.BlockSpec((2, H, HD, HD), lambda n, s: (0, 0, 0, 0)),
            ],
        ),
        out_shape=[
            jax.ShapeDtypeStruct((TOK, 3 * D), BF16),
            jax.ShapeDtypeStruct((TOK, D), BF16),
            jax.ShapeDtypeStruct((NB, H, HD, HD), F32),
            jax.ShapeDtypeStruct((NB, H, HD, HD), F32),
            jax.ShapeDtypeStruct((2, H, HD, HD), F32),
        ],
        compiler_params=params(),
        name="project",
    )(offset, x, w, g)


def scan_body(count, back_ref, v_ref, *refs):
    o_ref = refs[-1]

    def step(t, so_far):
        i = jnp.where(back_ref[0] == 1, count - 1 - t, t)
        o_ref[i] = so_far
        return so_far + v_ref[i]

    lax.fori_loop(0, count, step, jnp.zeros(v_ref.shape[1:], F32))


def scan_states(back, v, after):
    return pl.pallas_call(
        functools.partial(scan_body, v.shape[0]),
        in_specs=[pl.BlockSpec(memory_space=pltpu.SMEM), pl.BlockSpec(memory_space=pltpu.VMEM)]
        + [pl.BlockSpec(memory_space=pl.ANY)] * len(after),
        out_specs=pl.BlockSpec(memory_space=pltpu.VMEM),
        out_shape=jax.ShapeDtypeStruct(v.shape, F32),
        compiler_params=params(4),
        name="scan_states",
    )(back, v, *after)


def local_body(qkv_ref, sg_ref, kv_ref, qg_ref, o_ref):
    n = pl.program_id(0)
    keep = lax.broadcasted_iota(jnp.int32, (CH, CH), 0) >= lax.broadcasted_iota(jnp.int32, (CH, CH), 1)
    for h in range(H):
        q, k, v = (qkv_ref[:, head(p, h)] for p in range(3))
        g = sg_ref[:, pl.ds(h * HD, HD)]
        before = jnp.zeros((HD, HD), F32)
        after = jnp.zeros((HD, HD), F32)
        for m in range(NB):
            before = before + jnp.where(m < n, kv_ref[m, h], 0.0)
            after = after + jnp.where(m > n, qg_ref[m, h], 0.0)
        before = before.astype(BF16)
        after = after.astype(BF16)
        mvg = jnp.where(keep, dot(g, v, NT), 0.0).astype(BF16)
        mqk = jnp.where(keep, dot(q, k, NT), 0.0).astype(BF16)
        dq = dot(mvg, k, NN) + dot(g, before, NT)
        dk = dot(mvg, q, TN) + dot(v, after, NT)
        dv = dot(mqk, g, TN) + dot(k, after, NN)
        for p, d in enumerate((dq, dk, dv)):
            o_ref[:, head(p, h)] = d.astype(BF16)


def local(qkv, sg, kv, qg):
    block = lambda cols: pl.BlockSpec((CH, cols), lambda n: (n, 0))
    sums = pl.BlockSpec((NB, H, HD, HD), lambda n: (0, 0, 0, 0))
    return pl.pallas_call(
        local_body,
        grid=(NB,),
        in_specs=[block(3 * D), block(D), sums, sums],
        out_specs=block(3 * D),
        out_shape=jax.ShapeDtypeStruct((TOK, 3 * D), BF16),
        compiler_params=params(20),
        cost_estimate=cost(4e9, 20e6),
        name="local",
    )(qkv, sg, kv, qg)


def factors_body(at_ref, x_ref, g_ref, k_ref, v_ref, o_ref):
    for j, ref in enumerate((g_ref, v_ref, k_ref)):
        o_ref[:, j * 256 : (j + 1) * 256] = dot(x_ref[...], ref[...], TN).astype(o_ref.dtype)


def factors(at, x, sg, qkv, mine, kind, name):
    def cols(first):
        return pl.BlockSpec((TOK, 256), lambda i, s: (0, first + (s[0] if mine else 1 - s[0])))

    return pl.pallas_call(
        factors_body,
        grid_spec=pltpu.PrefetchScalarGridSpec(
            num_scalar_prefetch=1,
            grid=(2,),
            in_specs=[pl.BlockSpec((TOK, DM // 2), lambda i, s: (0, i)), cols(0), cols(2), cols(4)],
            out_specs=pl.BlockSpec((DM // 2, 768), lambda i, s: (i, 0)),
        ),
        out_shape=jax.ShapeDtypeStruct((DM, 768), kind),
        compiler_params=params(24),
        cost_estimate=cost(3e9, 12e6),
        name=name,
    )(at, x, sg, qkv, qkv)


def give_body(at_ref, x_ref, q_ref, k_ref, v_ref, o_ref):
    for j, ref in enumerate((q_ref, k_ref, v_ref)):
        o_ref[:, j * 256 : (j + 1) * 256] = dot(x_ref[...], ref[...], TN)


def keep_body(at_ref, x_ref, q_ref, k_ref, v_ref, r_ref, o_ref):
    for j, ref in enumerate((q_ref, k_ref, v_ref)):
        cols = slice(j * 256, (j + 1) * 256)
        o_ref[:, cols] = dot(x_ref[...], ref[...], TN) + r_ref[:, cols]


def local_part(at, x, loc, arrived, name):
    mine = arrived is not None

    def cols(first):
        return pl.BlockSpec((TOK, 256), lambda i, s: (0, first + (s[0] if mine else 1 - s[0])))

    rows = pl.BlockSpec((DM // 2, 768), lambda i, s: (i, 0))
    return pl.pallas_call(
        keep_body if mine else give_body,
        grid_spec=pltpu.PrefetchScalarGridSpec(
            num_scalar_prefetch=1,
            grid=(2,),
            in_specs=[pl.BlockSpec((TOK, DM // 2), lambda i, s: (0, i)), cols(0), cols(2), cols(4)]
            + ([rows] if mine else []),
            out_specs=rows,
        ),
        out_shape=jax.ShapeDtypeStruct((DM, 768), F32),
        compiler_params=params(24),
        cost_estimate=cost(3e9, 12e6),
        name=name,
    )(at, x, loc, loc, loc, *([arrived] if mine else []))


def pick(at_ref, axis):
    mine, far, first, second = (at_ref[1 + 4 * axis + i] for i in range(4))
    return (mine, second), (first, far)


def finish_body(at_ref, w_ref, a_ref, b_ref, sa_ref, sb_ref, kx_ref, sx_ref, ky_ref, sy_ref, s_ref):
    j = pl.program_id(0)
    core = at_ref[0]

    def add(kind, dims):
        for i in range(2):
            cols = slice(i * HD, (i + 1) * HD)
            h = 2 * core + i
            term = dot(a_ref[:, cols], sa_ref[kind, h].astype(BF16), dims)
            term += dot(b_ref[:, cols].astype(BF16), sb_ref[kind, h].astype(BF16), dims)
            s_ref[:, :, :, :, cols] = (w_ref[:, cols] + term).reshape(8, 4, 4, 8, HD)

    @pl.when(j == 0)
    def _():
        add(0, NT)

    @pl.when(j == 1)
    def _():
        add(1, NT)

    @pl.when(j == 2)
    def _():
        add(1, NN)

    kept, sent = pick(at_ref, 0)
    for i in range(2):
        kx_ref[:, :, i] = s_ref[:, :, kept[i], :, 0:128]
        sx_ref[:, :, i] = s_ref[:, :, sent[i], :, 0:128]
    kept, sent = pick(at_ref, 1)
    for i in range(2):
        ky_ref[:, i] = s_ref[:, kept[i], :, :, 128:256]
        sy_ref[:, i] = s_ref[:, sent[i], :, :, 128:256]


def finish(at, w, a, b, sa, sb):
    bx = pl.BlockSpec((8, 4, 2, 8, 128), lambda j, s: (0, 0, 0, 0, j))
    by = pl.BlockSpec((8, 2, 4, 8, 128), lambda j, s: (0, 0, 0, 0, j))
    cols = pl.BlockSpec((DM, 256), lambda j, s: (0, j))
    states = pl.BlockSpec((2, H, HD, HD), lambda j, s: (0, 0, 0, 0))
    return pl.pallas_call(
        finish_body,
        grid_spec=pltpu.PrefetchScalarGridSpec(
            num_scalar_prefetch=1,
            grid=(3,),
            in_specs=[cols, cols, cols, states, states],
            out_specs=[bx, bx, by, by],
            scratch_shapes=[pltpu.VMEM((8, 4, 4, 8, 256), F32)],
        ),
        out_shape=[jax.ShapeDtypeStruct((8, 4, 2, 8, 384), F32)] * 2
        + [jax.ShapeDtypeStruct((8, 2, 4, 8, 384), F32)] * 2,
        compiler_params=params(24),
        cost_estimate=cost(1e9, 12e6),
        name="finish",
    )(at, w, a, b, sa, sb)


def inputs_body(loc_ref, qkv_ref, sg_ref, s_ref, w_ref, o_ref, d_ref):
    for h in range(H):
        before = s_ref[0, h].astype(BF16)
        after = s_ref[1, h].astype(BF16)
        parts = (
            dot(sg_ref[:, pl.ds(h * HD, HD)], before, NT),
            dot(qkv_ref[:, head(2, h)], after, NT),
            dot(qkv_ref[:, head(1, h)], after, NN),
        )
        for p, d in enumerate(parts):
            d_ref[:, head(p, h)] = (loc_ref[:, head(p, h)].astype(F32) + d).astype(BF16)
    o_ref[...] = dot(d_ref[...], w_ref[...], NT).astype(BF16)


def inputs_grad(loc, qkv, sg, states, weights):
    block = lambda cols: pl.BlockSpec((CH, cols), lambda n: (n, 0))
    return pl.pallas_call(
        inputs_body,
        grid=(NB,),
        in_specs=[
            block(3 * D),
            block(3 * D),
            block(D),
            pl.BlockSpec((2, H, HD, HD), lambda n: (0, 0, 0, 0)),
            pl.BlockSpec((DM, 3 * D), lambda n: (0, 0)),
        ],
        out_specs=block(DM),
        out_shape=jax.ShapeDtypeStruct((TOK, DM), BF16),
        scratch_shapes=[pltpu.VMEM((CH, 3 * D), BF16)],
        compiler_params=params(24),
        cost_estimate=cost(5e9, 14e6),
        name="inputs_grad",
    )(loc, qkv, sg, states, weights)


def whole_call(body, name, shapes, *args, scratch=()):
    vmem = pl.BlockSpec(memory_space=pltpu.VMEM)
    smem = pl.BlockSpec(memory_space=pltpu.SMEM)
    return pl.pallas_call(
        body,
        in_specs=[smem if a.dtype == jnp.int32 else vmem for a in args],
        out_specs=[vmem] * len(shapes),
        out_shape=[jax.ShapeDtypeStruct(s, F32) for s in shapes],
        scratch_shapes=list(scratch),
        compiler_params=params(16),
        name=name,
    )(*args)


def add1_body(kx, rx, ky, ry, kx2, sx2, ky2, sy2):
    kx2[...] = kx[:, :, 0] + rx[:, :, 0]
    sx2[...] = kx[:, :, 1] + rx[:, :, 1]
    ky2[...] = ky[:, 0] + ry[:, 0]
    sy2[...] = ky[:, 1] + ry[:, 1]


def add2_body(at, kx, rx, ky, ry, kp, sp, kq, sq):
    for axis, k, r, ko, so in ((1, kx, rx, kp, sp), (0, ky, ry, kq, sq)):
        kept, sent = pick(at, axis)
        for i in range(2):
            ko[:, i] = k[:, kept[i]] + r[:, kept[i]]
            so[:, i] = k[:, sent[i]] + r[:, sent[i]]


def add3_body(kp, rp, kq, rq, kp2, sp2, kq2, sq2):
    for k, r, ko, so in ((kp, rp, kp2, sp2), (kq, rq, kq2, sq2)):
        ko[...] = k[:, 0] + r[:, 0]
        so[...] = k[:, 1] + r[:, 1]


def add4_body(kp, rp, kq, rq, o):
    o[:, :, 0:384] = kp[...] + rp[...]
    o[:, :, 384:768] = kq[...] + rq[...]


def sum_body(v, o):
    total = v[0]
    for i in range(1, v.shape[0]):
        total = total + v[i]
    for i in range(o.shape[0]):
        o[i] = total


def place_body(v, o):
    for i in range(8):
        for p in range(6):
            at = (p % 3) * 512 + (i % 2) * 256 + (p // 3) * 128
            o[i // 2 * 8 : i // 2 * 8 + 8, at : at + 128] = v[i, :, p * 128 : (p + 1) * 128]


def exchange(value, axis, step):
    pairs = []
    for i in range(4):
        for c in range(2):
            j = i ^ ((1, 3), (3, 1))[c][step]
            pairs.append((2 * i + c, 2 * j + c))
    return lax.ppermute(value, (axis, "core"), pairs)


def shards(inputs, weights, out_grad):
    x = inputs[0]
    z_at, y_at, x_at, core = (lax.axis_index(a) for a in ("z", "y", "x", "core"))
    tm_at = z_at * 4 + y_at
    first = jnp.where(core == 0, 1, 3)
    second = 4 - first
    at = jnp.stack(
        [core]
        + [v for i in (x_at, y_at) for v in (i, i ^ first ^ second, i ^ first, i ^ second)]
    ).astype(jnp.int32)
    offset = (tm_at * TOK).astype(jnp.int32)[None]
    back = (tm_at >= 16).astype(jnp.int32)[None]

    qkv, sg, kv, qg, total = project(offset, x, weights, out_grad[0])
    slices = lax.all_to_all(total.reshape(32, 32, HD), ("z", "y"), 0, 0, tiled=True)
    factors_out = factors(at, x, sg, qkv, False, F32, "factors_give")
    loc = local(qkv, sg, kv, qg)
    local_out = local_part(at, x, loc, None, "local_give")
    slices, factors_out, local_out = lax.optimization_barrier((slices, factors_out, local_out))
    factors_in = lax.ppermute(factors_out, "core", SWAP)
    local_in = lax.ppermute(local_out, "core", SWAP)

    scanned = scan_states(back, slices, [])
    states = lax.all_to_all(scanned, ("z", "y"), 0, 0, tiled=True)
    mine = factors(at, x, sg, qkv, True, BF16, "factors_keep")
    both = local_part(at, x, loc, local_in, "local_keep")
    states, mine, both = lax.optimization_barrier((states, mine, both))

    states = states.reshape(2, H, HD, HD)
    states_in = lax.ppermute(states, "core", SWAP)
    kx, sx, ky, sy = finish(at, both, mine, factors_in, states, states_in)
    rx = exchange(sx, "x", 0)
    ry = exchange(sy, "y", 0)
    record_grad = inputs_grad(loc, qkv, sg, states, weights)
    kx, sx, ky, sy = whole_call(add1_body, "add1", [(8, 4, 8, 384)] * 4, kx, rx, ky, ry)
    rx = exchange(sx, "x", 1)
    ry = exchange(sy, "y", 1)
    kp, sp, kq, sq = whole_call(add2_body, "add2", [(8, 2, 8, 384)] * 4, at, kx, rx, ky, ry)
    rp = exchange(sp, "y", 0)
    rq = exchange(sq, "x", 0)
    kp, sp, kq, sq = whole_call(add3_body, "add3", [(8, 8, 384)] * 4, kp, rp, kq, rq)
    rp = exchange(sp, "y", 1)
    rq = exchange(sq, "x", 1)
    (part,) = whole_call(add4_body, "add4", [(8, 8, 768)], kp, rp, kq, rq)
    part = lax.all_to_all(part, "z", 0, 0, tiled=True)
    (mine,) = whole_call(sum_body, "sum_z", [(8, 8, 768)], part)
    rows = lax.all_to_all(mine, ("x", "core"), 0, 0, tiled=True)
    (proj_grad,) = whole_call(place_body, "place", [(32, 3 * D)], rows)
    return record_grad[None], proj_grad


def solution(mesh):
    fine = Mesh(mesh.devices.reshape(8, 4, 4, 2), ("z", "y", "x", "core"))
    tm, dp = ("z", "y"), ("x", "core")
    placed = (P(dp, tm, None), P(), P(dp, tm, None))
    return jax.shard_map(
        shards,
        mesh=fine,
        in_specs=placed,
        out_specs=(P(dp, tm, None), P(tm, None)),
        check_vma=False,
    )
```

time: 174 us -> 157 us (0.902)
  waiting for transfers between devices: 61.4 us -> 28.7 us
  local copies, waits for them, and re-layouts: 7.26 us -> 30.8 us
  Pallas kernels: 48.1 us -> 39.7 us
  starting transfers between devices: 38.8 us -> 43.6 us
  matrix products: 4.62 us -> 0 us
    unnamed x32 -> x58, local copies, waits for them, and re-layouts: 6.57 us -> 30.7 us
    all_to_all x1, waiting for transfers between devices: 16.3 us -> 0.01 us  [shards(): lax.all_to_all(total.reshape(32, 32, HD), ('z', 'y'), 0, 0, tiled=True)]
    all_to_all x1 -> x2, starting transfers between devices: 5.21 us -> 19.4 us  [the longest x1 10.7 us: shards(): rows = lax.all_to_all(mine, ('x', 'core'), 0, 0, tiled=True)]
    all_to_all x1 -> x2, waiting for transfers between devices: 14.4 us -> 1.7 us  [the longest x1 1.7 us: shards(): states = lax.all_to_all(scanned, ('z', 'y'), 0, 0, tiled=True)]
    pallas_call x7 -> x6, Pallas kernels: 13.7 us -> 2.25 us  [whole_call(): pl.pallas_call(body, in_specs=[smem if a.dtype == jnp.int32 else vmem for...]
    ppermute x5 -> x3, starting transfers between devices: 14.6 us -> 4.14 us  [the longest x1 2.29 us: shards(): states_in = lax.ppermute(states, 'core', SWAP)]
    pallas_call x3 -> x7, Pallas kernels: 22.8 us -> 30.3 us  [the longest x2 7.1 us: local_part(): pl.pallas_call(keep_body if mine else give_body, grid_spec=pltpu.Prefetch...]
    dot_general x1 -> x0, matrix products: 4.62 us -> none  [dot(): return lax.dot_general(a, b, dims, preferred_element_type=F32)]
  transfers between devices with their start and end apart: 15 -> 14, of which waited for: 12 -> 10; matrix products, arithmetic and copies ran while one was open for 3% -> 0% of each run, Pallas kernels for 0% -> 17%
where the time goes in v2:
time: 157 us; the launch traced here: 156 us
  starting transfers between devices  43.6 us (28%)
  Pallas kernels  39.7 us (25%)
  local copies, waits for them, and re-layouts  30.8 us (20%)
  waiting for transfers between devices  28.7 us (18%)
  blocking collectives  12.5 us (8%)
    unnamed x58, local copies, waits for them, and re-layouts  30.7 us
    ppermute x8, waiting for transfers between devices, exchange(): return lax.ppermute(value, (axis, 'core'), pairs)  25.2 us
    all_to_all x1, blocking collectives, shards(): part = lax.all_to_all(part, 'z', 0, 0, tiled=True)  12.5 us
    all_to_all x1, starting transfers between devices, shards(): lax.all_to_all(total.reshape(32, 32, HD), ('z', 'y'), 0, 0, tiled=True)  12.2 us
    all_to_all x1, starting transfers between devices, shards(): rows = lax.all_to_all(mine, ('x', 'core'), 0, 0, tiled=True)  10.7 us
    all_to_all x1, starting transfers between devices, shards(): states = lax.all_to_all(scanned, ('z', 'y'), 0, 0, tiled=True)  8.67 us
    ppermute x8, starting transfers between devices, exchange(): return lax.ppermute(value, (axis, 'core'), pairs)  7.9 us
    pallas_call x2, Pallas kernels, local_part(): pl.pallas_call(keep_body if mine else give_body, grid_spec=pltpu.Prefetch...  7.1 us
  transfers between devices with their start and end apart: 14, of which 10 were waited for; matrix products, arithmetic and copies ran while one was open for 0% of the time, Pallas kernels for 17%

profile of v2, /device:TPU:1, one launch (start us, length us, event | category | flops | bytes accessed | tf_op | source)
XLA Modules:
  0.0 156.1 jit_solution(6436142305192506848)
XLA Ops:
  0.6 0.0 copy-start
  0.7 1.6 %copy-done = bf16[1,1024,1024]{2,1,0:T(8,128)(2,1)S(1)} copy-done((bf16[1,1024,1024]{2,1,0:T(8,128)(2,1)S(1)}, bf16[1,1024,1024]{2,1,0:T(8,128)(2,1)}, u32[]{:S(2)}) %copy-start) | copy-done | bytes 2097176
  2.2 1.9 %copy-done.11 = bf16[1024,1536]{1,0:T(8,128)(2,1)S(1)} copy-done((bf16[1024,1536]{1,0:T(8,128)(2,1)S(1)}, bf16[1024,1536]{1,0:T(8,128)(2,1)}, u32[]{:S(2)}) %copy-start.11) | copy-done | bytes 3145752
  4.1 1.2 copy-done.18
  5.4 5.9 %project.1 = (bf16[1024,1536]{1,0:T(8,128)(2,1)S(1)}, bf16[1024,512]{1,0:T(8,128)(2,1)S(1)}, f32[4,4,128,128]{3,2,1,0:T(8,128)S(1)}, f32[4,4,128,128]{3,2,1,0:T(8,128)S(1)}, f32[2,4,128,128]{3,2,1,0:T(8,128)S(1)}) custom-call(s32[1]{0:T(128)} %bitcast.pos_ref, bf16[1024,1024]{1,0:T(8,128)(2,1)S(1)} %bitcast.16, bf16[1024,1536]{1,0:T(8,128)(2,1)S(1)} %copy-done.11, ...), custom_call_target="tpu_custom_call" | custom-call | tf_op jit(solution)/shard_map/project/pallas_call | solution.py:68
  11.2 1.6 %copy-done.6 = bf16[1024,1536]{1,0:T(8,128)(2,1)} copy-done((bf16[1024,1536]{1,0:T(8,128)(2,1)}, bf16[1024,1536]{1,0:T(8,128)(2,1)S(1)}, u32[]{:S(2)}) %copy-start.6) | copy-done | bytes 3145752
  12.9 1.0 copy-done.19
  13.8 0.8 copy-done.24
  14.7 1.0 copy-done.27
  15.7 12.2 %all-to-all-start = ((f32[32,32,128]{2,1,0:T(8,128)}), f32[32,32,128]{2,1,0:T(8,128)}, u32[]{:S(2)}, u32[]{:S(2)}) async-start(f32[32,32,128]{2,1,0:T(8,128)} %bitcast.22), calls=%async_computation | async-start | bytes 1048576 | tf_op jit(solution)/shard_map/all_to_all | solution.py:386
  27.9 0.1 stack.39.at_ref.at
  28.0 1.9 %copy-done.7 = bf16[1024,1536]{1,0:T(8,128)(2,1)S(1)} copy-done((bf16[1024,1536]{1,0:T(8,128)(2,1)S(1)}, bf16[1024,1536]{1,0:T(8,128)(2,1)}, u32[]{:S(2)}) %copy-start.7) | copy-done | bytes 3145752
  29.9 1.2 copy-done.20
  31.1 2.9 %factors_give.1 = f32[1024,768]{1,0:T(8,128)S(1)} custom-call(s32[9]{0:T(128)S(1)} %stack.39.at_ref.at, bf16[1024,1024]{1,0:T(8,128)(2,1)S(1)} %bitcast.17, bf16[1024,512]{1,0:T(8,128)(2,1)S(1)} %copy-done.20, bf16[1024,1536]{1,0:T(8,128)(2,1)S(1)} %copy-done.7, bf16[1024,1536]{1,0:T(8,128)(2,1)S(1)} %copy-done.7), custom_call_target="tpu_custom_call" | custom-call | flops 3000000000 | bytes 12000000 | tf_op jit(solution)/shard_map/factors_give/pallas_call | solution.py:163
  34.1 0.0 copy-start.2
  34.1 5.8 %local.1.q_ref.k_ref.v_ref.loc_ref = bf16[1024,1536]{1,0:T(8,128)(2,1)S(1)} custom-call(bf16[1024,1536]{1,0:T(8,128)(2,1)S(1)} %copy-done.8, bf16[1024,512]{1,0:T(8,128)(2,1)S(1)} %copy-done.21, f32[4,4,128,128]{3,2,1,0:T(8,128)S(1)} %copy-done.26, f32[4,4,128,128]{3,2,1,0:T(8,128)S(1)} %copy-done.28), custom_call_target="tpu_custom_call" | custom-call | flops 4000000000 | bytes 20000000 | tf_op jit(solution)/shard_map/local/pallas_call | solution.py:142
  39.9 2.9 %local_give.1 = f32[1024,768]{1,0:T(8,128)S(1)} custom-call(s32[9]{0:T(128)S(1)} %stack.39.at_ref.at, bf16[1024,1024]{1,0:T(8,128)(2,1)S(1)} %bitcast.18, bf16[1024,1536]{1,0:T(8,128)(2,1)S(1)} %local.1.q_ref.k_ref.v_ref.loc_ref, bf16[1024,1536]{1,0:T(8,128)(2,1)S(1)} %local.1.q_ref.k_ref.v_ref.loc_ref, bf16[1024,1536]{1,0:T(8,128)(2,1)S(1)} %local.1.q_ref.k_ref.v_ref.loc_ref), custom_call_target="tpu_custom_call" | custom-call | flops 3000000000 | bytes 12000000 | tf_op jit(solution)/shard_map/local_give/pallas_call | solution.py:196
  42.9 1.7 %copy-done.14 = f32[1024,768]{1,0:T(8,128)} copy-done((f32[1024,768]{1,0:T(8,128)}, f32[1024,768]{1,0:T(8,128)S(1)}, u32[]{:S(2)}) %copy-start.14) | copy-done | bytes 3145752
  44.6 1.8 %collective-permute-start = (f32[1024,768]{1,0:T(8,128)}, f32[1024,768]{1,0:T(8,128)}, u32[]{:S(2)}, u32[]{:S(2)}) collective-permute-start(f32[1024,768]{1,0:T(8,128)} %copy-done.14), channel_id=1, source_target_pairs={{0,1},{1,0},{2,3},{3,2},{4,5},{5,4},{6,7},{7,6},{8,9},{9,8},{10,11... | collective-permute-start | bytes 9437192 | tf_op jit(solution)/shard_map/ppermute | solution.py:392
  46.5 0.0 collective-permute-start.1
  46.5 1.3 scan_states.1
  47.8 0.8 copy-done.15
  48.6 8.7 %all-to-all-start.1 = ((f32[32,32,128]{2,1,0:T(8,128)}), f32[32,32,128]{2,1,0:T(8,128)}, u32[]{:S(2)}, u32[]{:S(2)}) async-start(f32[32,32,128]{2,1,0:T(8,128)} %copy-done.15), calls=%async_computation.1 | async-start | bytes 1048576 | tf_op jit(solution)/shard_map/all_to_all | solution.py:395
  57.3 0.0 copy-start.3
  57.3 1.6 %copy-done.3 = bf16[1,1024,1024]{2,1,0:T(8,128)(2,1)S(1)} copy-done((bf16[1,1024,1024]{2,1,0:T(8,128)(2,1)S(1)}, bf16[1,1024,1024]{2,1,0:T(8,128)(2,1)}, u32[]{:S(2)}) %copy-start.3) | copy-done | bytes 2097176
  58.9 1.9 %copy-done.9 = bf16[1024,1536]{1,0:T(8,128)(2,1)S(1)} copy-done((bf16[1024,1536]{1,0:T(8,128)(2,1)S(1)}, bf16[1024,1536]{1,0:T(8,128)(2,1)}, u32[]{:S(2)}) %copy-start.9) | copy-done | bytes 3145752
  60.8 1.2 copy-done.22
  62.0 2.9 %factors_keep.1.a_ref = bf16[1024,768]{1,0:T(8,128)(2,1)S(1)} custom-call(s32[9]{0:T(128)S(1)} %stack.39.at_ref.at, bf16[1024,1024]{1,0:T(8,128)(2,1)S(1)} %bitcast.19, bf16[1024,512]{1,0:T(8,128)(2,1)S(1)} %copy-done.22, bf16[1024,1536]{1,0:T(8,128)(2,1)S(1)} %copy-done.9, bf16[1024,1536]{1,0:T(8,128)(2,1)S(1)} %copy-done.9), custom_call_target="tpu_custom_call" | custom-call | flops 3000000000 | bytes 12000000 | tf_op jit(solution)/shard_map/factors_keep/pallas_call | solution.py:163
  64.9 0.0 copy-start.16
  65.0 1.1 copy-done.16
  66.1 4.2 %local_keep.1.w_ref = f32[1024,768]{1,0:T(8,128)S(1)} custom-call(s32[9]{0:T(128)S(1)} %stack.39.at_ref.at, bf16[1024,1024]{1,0:T(8,128)(2,1)S(1)} %bitcast.20, bf16[1024,1536]{1,0:T(8,128)(2,1)S(1)} %local.1.q_ref.k_ref.v_ref.loc_ref, bf16[1024,1536]{1,0:T(8,128)(2,1)S(1)} %local.1.q_ref.k_ref.v_ref.loc_ref, ...), custom_call_target="tpu_custom_call" | custom-call | flops 3000000000 | bytes 12000000 | tf_op jit(solution)/shard_map/local_keep/pallas_call | solution.py:196
  70.3 1.7 %copy-done.4 = f32[1024,768]{1,0:T(8,128)} copy-done((f32[1024,768]{1,0:T(8,128)}, f32[1024,768]{1,0:T(8,128)S(1)}, u32[]{:S(2)}) %copy-start.4) | copy-done | bytes 3145752
  72.0 1.7 %all-to-all-done.1 = f32[32,32,128]{2,1,0:T(8,128)} async-done(((f32[32,32,128]{2,1,0:T(8,128)}), f32[32,32,128]{2,1,0:T(8,128)}, u32[]{:S(2)}, u32[]{:S(2)}) %all-to-all-start.1) | async-done | bytes 524320 | tf_op jit(solution)/shard_map/all_to_all | solution.py:395
  73.7 2.3 %collective-permute-start.2 = (f32[2,4,128,128]{3,2,1,0:T(8,128)}, f32[2,4,128,128]{3,2,1,0:T(8,128)S(1)}, u32[]{:S(2)}, u32[]{:S(2)}) collective-permute-start(f32[2,4,128,128]{3,2,1,0:T(8,128)} %bitcast.14.s_ref.sa_ref), channel_id=1, source_target_pairs={{0,1},{1,0},{2,3},{3,2},{4,5},{5,4},{6,7},{7,6},{8,9},{9,8},{10,11... | collective-permute-start | bytes 1572872 | tf_op jit(solution)/shard_map/ppermute | solution.py:401
  76.0 1.7 %collective-permute-done.2.sb_ref = f32[2,4,128,128]{3,2,1,0:T(8,128)S(1)} collective-permute-done((f32[2,4,128,128]{3,2,1,0:T(8,128)}, f32[2,4,128,128]{3,2,1,0:T(8,128)S(1)}, u32[]{:S(2)}, u32[]{:S(2)}) %collective-permute-start.2) | collective-permute-done | bytes 524320 | tf_op jit(solution)/shard_map/ppermute | solution.py:401
  77.7 1.9 %copy-done.5 = f32[1024,768]{1,0:T(8,128)S(1)} copy-done((f32[1024,768]{1,0:T(8,128)S(1)}, f32[1024,768]{1,0:T(8,128)}, u32[]{:S(2)}) %copy-start.5) | copy-done | bytes 3145752
  79.6 1.4 copy-done.17
  81.0 4.6 %finish.1 = (f32[8,4,2,8,384]{4,3,2,1,0:T(8,128)S(1)}, f32[8,4,2,8,384]{4,3,2,1,0:T(8,128)S(1)}, f32[8,2,4,8,384]{4,3,2,1,0:T(8,128)S(1)}, f32[8,2,4,8,384]{4,3,2,1,0:T(8,128)S(1)}) custom-call(s32[9]{0:T(128)S(1)} %stack.39.at_ref.at, f32[1024,768]{1,0:T(8,128)S(1)} %copy-done.5, bf16[1024,768]{1,0:T(8,128)(2,1)S(1)} %copy-done.17, ...), custom_call_target="tpu_custom_call" | custom-call | flops 1000000000 | bytes 12000000 | tf_op jit(solution)/shard_map/finish/pallas_call | solution.py:256
  85.6 2.7 %collective-permute-start.3 = (f32[8,4,2,8,384]{4,3,2,1,0:T(8,128)S(1)}, f32[8,4,2,8,384]{4,3,2,1,0:T(8,128)S(1)}, u32[]{:S(2)}, u32[]{:S(2)}) collective-permute-start(f32[8,4,2,8,384]{4,3,2,1,0:T(8,128)S(1)} %get-tuple-element.41), channel_id=1, source_target_pairs={{0,2},{1,7},{2,0},{3,5},{4,6},{5,3},{6,4},{7,1},{8,10},{9,15},{10,... | collective-permute-start | bytes 2359304 | tf_op jit(solution)/shard_map/ppermute | solution.py:369
  88.4 1.8 %collective-permute-start.4 = (f32[8,2,4,8,384]{4,3,2,1,0:T(8,128)S(1)}, f32[8,2,4,8,384]{4,3,2,1,0:T(8,128)S(1)}, u32[]{:S(2)}, u32[]{:S(2)}) collective-permute-start(f32[8,2,4,8,384]{4,3,2,1,0:T(8,128)S(1)} %get-tuple-element.43), channel_id=1, source_target_pairs={{0,8},{1,25},{8,0},{9,17},{16,24},{17,9},{24,16},{25,1},{2,10},{3,... | collective-permute-start | bytes 2359304 | tf_op jit(solution)/shard_map/ppermute | solution.py:369
  90.2 7.8 %collective-permute-done.3.rx = f32[8,4,2,8,384]{4,3,2,1,0:T(8,128)S(1)} collective-permute-done((f32[8,4,2,8,384]{4,3,2,1,0:T(8,128)S(1)}, f32[8,4,2,8,384]{4,3,2,1,0:T(8,128)S(1)}, u32[]{:S(2)}, u32[]{:S(2)}) %collective-permute-start.3) | collective-permute-done | bytes 786464 | tf_op jit(solution)/shard_map/ppermute | solution.py:369
  98.0 2.5 %collective-permute-done.4.ry = f32[8,2,4,8,384]{4,3,2,1,0:T(8,128)S(1)} collective-permute-done((f32[8,2,4,8,384]{4,3,2,1,0:T(8,128)S(1)}, f32[8,2,4,8,384]{4,3,2,1,0:T(8,128)S(1)}, u32[]{:S(2)}, u32[]{:S(2)}) %collective-permute-start.4) | collective-permute-done | bytes 786464 | tf_op jit(solution)/shard_map/ppermute | solution.py:369
  100.4 0.2 add1.1
  100.6 0.1 collective-permute-start.5
  100.7 0.1 collective-permute-start.6
  100.8 6.8 %collective-permute-done.5.rx = f32[8,4,8,384]{3,2,1,0:T(8,128)S(1)} collective-permute-done((f32[8,4,8,384]{3,2,1,0:T(8,128)S(1)}, f32[8,4,8,384]{3,2,1,0:T(8,128)S(1)}, u32[]{:S(2)}, u32[]{:S(2)}) %collective-permute-start.5) | collective-permute-done | bytes 393248 | tf_op jit(solution)/shard_map/ppermute | solution.py:369
  107.6 0.1 collective-permute-done.6.ry
  107.7 0.6 add2.1
  108.3 1.9 %collective-permute-start.7 = (f32[8,2,8,384]{3,2,1,0:T(8,128)S(1)}, f32[8,2,8,384]{3,2,1,0:T(8,128)S(1)}, u32[]{:S(2)}, u32[]{:S(2)}) collective-permute-start(f32[8,2,8,384]{3,2,1,0:T(8,128)S(1)} %get-tuple-element.49), channel_id=1, source_target_pairs={{0,8},{1,25},{8,0},{9,17},{16,24},{17,9},{24,16},{25,1},{2,10},{3,... | collective-permute-start | bytes 589832 | tf_op jit(solution)/shard_map/ppermute | solution.py:369
  110.2 0.7 collective-permute-start.8
  110.9 3.3 %collective-permute-done.7.rp = f32[8,2,8,384]{3,2,1,0:T(8,128)S(1)} collective-permute-done((f32[8,2,8,384]{3,2,1,0:T(8,128)S(1)}, f32[8,2,8,384]{3,2,1,0:T(8,128)S(1)}, u32[]{:S(2)}, u32[]{:S(2)}) %collective-permute-start.7) | collective-permute-done | bytes 196640 | tf_op jit(solution)/shard_map/ppermute | solution.py:369
  114.2 1.8 %collective-permute-done.8.rq = f32[8,2,8,384]{3,2,1,0:T(8,128)S(1)} collective-permute-done((f32[8,2,8,384]{3,2,1,0:T(8,128)S(1)}, f32[8,2,8,384]{3,2,1,0:T(8,128)S(1)}, u32[]{:S(2)}, u32[]{:S(2)}) %collective-permute-start.8) | collective-permute-done | bytes 196640 | tf_op jit(solution)/shard_map/ppermute | solution.py:369
  116.0 0.1 collective-permute-start.9
  116.1 0.5 collective-permute-start.10
  116.6 2.9 %collective-permute-done.9.rp = f32[8,8,384]{2,1,0:T(8,128)S(1)} collective-permute-done((f32[8,8,384]{2,1,0:T(8,128)S(1)}, f32[8,8,384]{2,1,0:T(8,128)S(1)}, u32[]{:S(2)}, u32[]{:S(2)}) %collective-permute-start.9) | collective-permute-done | bytes 98336 | tf_op jit(solution)/shard_map/ppermute | solution.py:369
  119.5 0.1 collective-permute-done.10.rq
  119.7 12.5 %all_to_all.20.v = f32[8,8,768]{2,1,0:T(8,128)S(1)} all-to-all(f32[8,8,768]{2,1,0:T(8,128)S(1)} %add4.1), channel_id=1, replica_groups=mesh['z'=8,'y'=4,'x'=4,'core'=2] {'z'}, dimensions={0} | all-to-all | bytes 393216 | tf_op jit(solution)/shard_map/all_to_all | solution.py:416
  132.2 0.7 sum_z.1
  132.9 10.7 %all-to-all-start.3 = ((f32[8,8,768]{2,1,0:T(8,128)}), f32[8,8,768]{2,1,0:T(8,128)S(1)}, u32[]{:S(2)}, u32[]{:S(2)}) async-start(f32[8,8,768]{2,1,0:T(8,128)} %sum_z.1), calls=%async_computation.3 | async-start | bytes 393216 | tf_op jit(solution)/shard_map/all_to_all | solution.py:418
  143.5 1.9 %copy-done.10 = bf16[1024,1536]{1,0:T(8,128)(2,1)S(1)} copy-done((bf16[1024,1536]{1,0:T(8,128)(2,1)S(1)}, bf16[1024,1536]{1,0:T(8,128)(2,1)}, u32[]{:S(2)}) %copy-start.10) | copy-done | bytes 3145752
  145.4 1.9 %copy-done.12 = bf16[1024,1536]{1,0:T(8,128)(2,1)S(1)} copy-done((bf16[1024,1536]{1,0:T(8,128)(2,1)S(1)}, bf16[1024,1536]{1,0:T(8,128)(2,1)}, u32[]{:S(2)}) %copy-start.12) | copy-done | bytes 3145752
  147.3 1.2 copy-done.23
  148.5 6.9 %inputs_grad.1 = bf16[1024,1024]{1,0:T(8,128)(2,1)} custom-call(bf16[1024,1536]{1,0:T(8,128)(2,1)S(1)} %local.1.q_ref.k_ref.v_ref.loc_ref, bf16[1024,1536]{1,0:T(8,128)(2,1)S(1)} %copy-done.10, bf16[1024,512]{1,0:T(8,128)(2,1)S(1)} %copy-done.23, f32[2,4,128,128]{3,2,1,0:T(8,128)} %bitcast.14.s_ref.sa_ref, bf16[1024,1536]{1,0:T(8,128)(2,1)S(1)} %copy-done.12), custom_call_target="tpu_custom_call" | custom-call | flops 5000000000 | bytes 14000000 | tf_op jit(solution)/shard_map/inputs_grad/pallas_call | solution.py:289
  155.4 0.7 place.1
  (39 shorter events, 0.1 us)
Async XLA Ops:
  0.6 1.6 %copy-start = (bf16[1,1024,1024]{2,1,0:T(8,128)(2,1)S(1)}, bf16[1,1024,1024]{2,1,0:T(8,128)(2,1)}, u32[]{:S(2)}) copy-start(bf16[1,1024,1024]{2,1,0:T(8,128)(2,1)} %param.3) | copy-start | bytes 6291460
  2.2 1.9 %copy-start.11 = (bf16[1024,1536]{1,0:T(8,128)(2,1)S(1)}, bf16[1024,1536]{1,0:T(8,128)(2,1)}, u32[]{:S(2)}) copy-start(bf16[1024,1536]{1,0:T(8,128)(2,1)} %w_ref.3) | copy-start | bytes 9437188
  4.1 1.2 copy-start.18
  5.3 22.6 %copy-start.1 = (bf16[1,1024,1024]{2,1,0:T(8,128)(2,1)S(1)}, bf16[1,1024,1024]{2,1,0:T(8,128)(2,1)}, u32[]{:S(2)}) copy-start(bf16[1,1024,1024]{2,1,0:T(8,128)(2,1)} %param.3) | copy-start | bytes 6291460
  11.2 1.6 %copy-start.6 = (bf16[1024,1536]{1,0:T(8,128)(2,1)}, bf16[1024,1536]{1,0:T(8,128)(2,1)S(1)}, u32[]{:S(2)}) copy-start(bf16[1024,1536]{1,0:T(8,128)(2,1)S(1)} %get-tuple-element.29.qkv_ref.k_ref.v_ref) | copy-start | bytes 9437188
  12.9 1.0 copy-start.19
  13.8 0.8 copy-start.24
  14.7 1.0 copy-start.27
  15.7 12.3 %copy-start.25 = (f32[4,4,128,128]{3,2,1,0:T(8,128)}, f32[4,4,128,128]{3,2,1,0:T(8,128)S(1)}, u32[]{:S(2)}) copy-start(f32[4,4,128,128]{3,2,1,0:T(8,128)S(1)} %get-tuple-element.31.kv_ref) | copy-start | bytes 3145732
  15.7 29.0 %all-to-all-start = ((f32[32,32,128]{2,1,0:T(8,128)}), f32[32,32,128]{2,1,0:T(8,128)}, u32[]{:S(2)}, u32[]{:S(2)}) async-start(f32[32,32,128]{2,1,0:T(8,128)} %bitcast.22), calls=%async_computation | async-start | bytes 1048576 | tf_op jit(solution)/shard_map/all_to_all | solution.py:386
  28.0 1.9 %copy-start.7 = (bf16[1024,1536]{1,0:T(8,128)(2,1)S(1)}, bf16[1024,1536]{1,0:T(8,128)(2,1)}, u32[]{:S(2)}) copy-start(bf16[1024,1536]{1,0:T(8,128)(2,1)} %copy-done.6) | copy-start | bytes 9437188
  29.8 1.2 copy-start.20
  31.1 3.0 %copy-start.8 = (bf16[1024,1536]{1,0:T(8,128)(2,1)S(1)}, bf16[1024,1536]{1,0:T(8,128)(2,1)}, u32[]{:S(2)}) copy-start(bf16[1024,1536]{1,0:T(8,128)(2,1)} %copy-done.6) | copy-start | bytes 9437188
  31.1 3.0 %copy-start.21 = (bf16[1024,512]{1,0:T(8,128)(2,1)S(1)}, bf16[1024,512]{1,0:T(8,128)(2,1)}, u32[]{:S(2)}) copy-start(bf16[1024,512]{1,0:T(8,128)(2,1)} %copy-done.19) | copy-start | bytes 3145732
  31.1 3.0 %copy-start.26 = (f32[4,4,128,128]{3,2,1,0:T(8,128)S(1)}, f32[4,4,128,128]{3,2,1,0:T(8,128)}, u32[]{:S(2)}) copy-start(f32[4,4,128,128]{3,2,1,0:T(8,128)} %copy-done.25) | copy-start | bytes 3145732
  31.1 3.0 %copy-start.28 = (f32[4,4,128,128]{3,2,1,0:T(8,128)S(1)}, f32[4,4,128,128]{3,2,1,0:T(8,128)}, u32[]{:S(2)}) copy-start(f32[4,4,128,128]{3,2,1,0:T(8,128)} %copy-done.27) | copy-start | bytes 3145732
  34.0 5.9 %copy-start.13 = (f32[1024,768]{1,0:T(8,128)}, f32[1024,768]{1,0:T(8,128)S(1)}, u32[]{:S(2)}) copy-start(f32[1024,768]{1,0:T(8,128)S(1)} %factors_give.1) | copy-start | bytes 9437188
  34.1 5.8 %copy-start.2 = (bf16[1,1024,1024]{2,1,0:T(8,128)(2,1)S(1)}, bf16[1,1024,1024]{2,1,0:T(8,128)(2,1)}, u32[]{:S(2)}) copy-start(bf16[1,1024,1024]{2,1,0:T(8,128)(2,1)} %param.3) | copy-start | bytes 6291460
  42.9 1.7 %copy-start.14 = (f32[1024,768]{1,0:T(8,128)}, f32[1024,768]{1,0:T(8,128)S(1)}, u32[]{:S(2)}) copy-start(f32[1024,768]{1,0:T(8,128)S(1)} %local_give.1) | copy-start | bytes 9437188
  44.6 21.5 %collective-permute-start = (f32[1024,768]{1,0:T(8,128)}, f32[1024,768]{1,0:T(8,128)}, u32[]{:S(2)}, u32[]{:S(2)}) collective-permute-start(f32[1024,768]{1,0:T(8,128)} %copy-done.14), channel_id=1, source_target_pairs={{0,1},{1,0},{2,3},{3,2},{4,5},{5,4},{6,7},{7,6},{8,9},{9,8},{10,11... | collective-permute-start | bytes 9437192 | tf_op jit(solution)/shard_map/ppermute | solution.py:392
  46.5 29.5 %collective-permute-start.1 = (f32[1024,768]{1,0:T(8,128)}, f32[1024,768]{1,0:T(8,128)}, u32[]{:S(2)}, u32[]{:S(2)}) collective-permute-start(f32[1024,768]{1,0:T(8,128)} %copy-done.13), channel_id=1, source_target_pairs={{0,1},{1,0},{2,3},{3,2},{4,5},{5,4},{6,7},{7,6},{8,9},{9,8},{10,11... | collective-permute-start | bytes 9437192 | tf_op jit(solution)/shard_map/ppermute | solution.py:391
  47.8 0.8 copy-start.15
  48.6 25.1 %all-to-all-start.1 = ((f32[32,32,128]{2,1,0:T(8,128)}), f32[32,32,128]{2,1,0:T(8,128)}, u32[]{:S(2)}, u32[]{:S(2)}) async-start(f32[32,32,128]{2,1,0:T(8,128)} %copy-done.15), calls=%async_computation.1 | async-start | bytes 1048576 | tf_op jit(solution)/shard_map/all_to_all | solution.py:395
  57.3 1.6 %copy-start.3 = (bf16[1,1024,1024]{2,1,0:T(8,128)(2,1)S(1)}, bf16[1,1024,1024]{2,1,0:T(8,128)(2,1)}, u32[]{:S(2)}) copy-start(bf16[1,1024,1024]{2,1,0:T(8,128)(2,1)} %param.3) | copy-start | bytes 6291460
  58.9 1.9 %copy-start.9 = (bf16[1024,1536]{1,0:T(8,128)(2,1)S(1)}, bf16[1024,1536]{1,0:T(8,128)(2,1)}, u32[]{:S(2)}) copy-start(bf16[1024,1536]{1,0:T(8,128)(2,1)} %copy-done.6) | copy-start | bytes 9437188
  60.8 1.2 copy-start.22
  64.9 1.1 copy-start.16
  70.3 1.7 %copy-start.4 = (f32[1024,768]{1,0:T(8,128)}, f32[1024,768]{1,0:T(8,128)S(1)}, u32[]{:S(2)}) copy-start(f32[1024,768]{1,0:T(8,128)S(1)} %local_keep.1.w_ref) | copy-start | bytes 9437188
  73.7 4.0 %collective-permute-start.2 = (f32[2,4,128,128]{3,2,1,0:T(8,128)}, f32[2,4,128,128]{3,2,1,0:T(8,128)S(1)}, u32[]{:S(2)}, u32[]{:S(2)}) collective-permute-start(f32[2,4,128,128]{3,2,1,0:T(8,128)} %bitcast.14.s_ref.sa_ref), channel_id=1, source_target_pairs={{0,1},{1,0},{2,3},{3,2},{4,5},{5,4},{6,7},{7,6},{8,9},{9,8},{10,11... | collective-permute-start | bytes 1572872 | tf_op jit(solution)/shard_map/ppermute | solution.py:401
  77.7 1.9 %copy-start.5 = (f32[1024,768]{1,0:T(8,128)S(1)}, f32[1024,768]{1,0:T(8,128)}, u32[]{:S(2)}) copy-start(f32[1024,768]{1,0:T(8,128)} %copy-done.4) | copy-start | bytes 9437188
  79.6 1.4 copy-start.17
  85.6 12.3 %collective-permute-start.3 = (f32[8,4,2,8,384]{4,3,2,1,0:T(8,128)S(1)}, f32[8,4,2,8,384]{4,3,2,1,0:T(8,128)S(1)}, u32[]{:S(2)}, u32[]{:S(2)}) collective-permute-start(f32[8,4,2,8,384]{4,3,2,1,0:T(8,128)S(1)} %get-tuple-element.41), channel_id=1, source_target_pairs={{0,2},{1,7},{2,0},{3,5},{4,6},{5,3},{6,4},{7,1},{8,10},{9,15},{10,... | collective-permute-start | bytes 2359304 | tf_op jit(solution)/shard_map/ppermute | solution.py:369
  88.4 12.1 %collective-permute-start.4 = (f32[8,2,4,8,384]{4,3,2,1,0:T(8,128)S(1)}, f32[8,2,4,8,384]{4,3,2,1,0:T(8,128)S(1)}, u32[]{:S(2)}, u32[]{:S(2)}) collective-permute-start(f32[8,2,4,8,384]{4,3,2,1,0:T(8,128)S(1)} %get-tuple-element.43), channel_id=1, source_target_pairs={{0,8},{1,25},{8,0},{9,17},{16,24},{17,9},{24,16},{25,1},{2,10},{3,... | collective-permute-start | bytes 2359304 | tf_op jit(solution)/shard_map/ppermute | solution.py:369
  100.6 7.0 %collective-permute-start.5 = (f32[8,4,8,384]{3,2,1,0:T(8,128)S(1)}, f32[8,4,8,384]{3,2,1,0:T(8,128)S(1)}, u32[]{:S(2)}, u32[]{:S(2)}) collective-permute-start(f32[8,4,8,384]{3,2,1,0:T(8,128)S(1)} %get-tuple-element.45), channel_id=1, source_target_pairs={{0,6},{1,3},{2,4},{3,1},{4,2},{5,7},{6,0},{7,5},{8,14},{9,11},{10,... | collective-permute-start | bytes 1179656 | tf_op jit(solution)/shard_map/ppermute | solution.py:369
  100.7 7.0 %collective-permute-start.6 = (f32[8,4,8,384]{3,2,1,0:T(8,128)S(1)}, f32[8,4,8,384]{3,2,1,0:T(8,128)S(1)}, u32[]{:S(2)}, u32[]{:S(2)}) collective-permute-start(f32[8,4,8,384]{3,2,1,0:T(8,128)S(1)} %get-tuple-element.47), channel_id=1, source_target_pairs={{0,24},{1,9},{8,16},{9,1},{16,8},{17,25},{24,0},{25,17},{2,26},{3,... | collective-permute-start | bytes 1179656 | tf_op jit(solution)/shard_map/ppermute | solution.py:369
  108.3 5.8 %collective-permute-start.7 = (f32[8,2,8,384]{3,2,1,0:T(8,128)S(1)}, f32[8,2,8,384]{3,2,1,0:T(8,128)S(1)}, u32[]{:S(2)}, u32[]{:S(2)}) collective-permute-start(f32[8,2,8,384]{3,2,1,0:T(8,128)S(1)} %get-tuple-element.49), channel_id=1, source_target_pairs={{0,8},{1,25},{8,0},{9,17},{16,24},{17,9},{24,16},{25,1},{2,10},{3,... | collective-permute-start | bytes 589832 | tf_op jit(solution)/shard_map/ppermute | solution.py:369
  110.2 5.7 %collective-permute-start.8 = (f32[8,2,8,384]{3,2,1,0:T(8,128)S(1)}, f32[8,2,8,384]{3,2,1,0:T(8,128)S(1)}, u32[]{:S(2)}, u32[]{:S(2)}) collective-permute-start(f32[8,2,8,384]{3,2,1,0:T(8,128)S(1)} %get-tuple-element.51), channel_id=1, source_target_pairs={{0,2},{1,7},{2,0},{3,5},{4,6},{5,3},{6,4},{7,1},{8,10},{9,15},{10,... | collective-permute-start | bytes 589832 | tf_op jit(solution)/shard_map/ppermute | solution.py:369
  116.0 3.6 %collective-permute-start.9 = (f32[8,8,384]{2,1,0:T(8,128)S(1)}, f32[8,8,384]{2,1,0:T(8,128)S(1)}, u32[]{:S(2)}, u32[]{:S(2)}) collective-permute-start(f32[8,8,384]{2,1,0:T(8,128)S(1)} %get-tuple-element.53), channel_id=1, source_target_pairs={{0,24},{1,9},{8,16},{9,1},{16,8},{17,25},{24,0},{25,17},{2,26},{3,... | collective-permute-start | bytes 294920 | tf_op jit(solution)/shard_map/ppermute | solution.py:369
  116.1 3.6 %collective-permute-start.10 = (f32[8,8,384]{2,1,0:T(8,128)S(1)}, f32[8,8,384]{2,1,0:T(8,128)S(1)}, u32[]{:S(2)}, u32[]{:S(2)}) collective-permute-start(f32[8,8,384]{2,1,0:T(8,128)S(1)} %get-tuple-element.55), channel_id=1, source_target_pairs={{0,6},{1,3},{2,4},{3,1},{4,2},{5,7},{6,0},{7,5},{8,14},{9,11},{10,... | collective-permute-start | bytes 294920 | tf_op jit(solution)/shard_map/ppermute | solution.py:369
  132.9 22.6 %all-to-all-start.3 = ((f32[8,8,768]{2,1,0:T(8,128)}), f32[8,8,768]{2,1,0:T(8,128)S(1)}, u32[]{:S(2)}, u32[]{:S(2)}) async-start(f32[8,8,768]{2,1,0:T(8,128)} %sum_z.1), calls=%async_computation.3 | async-start | bytes 393216 | tf_op jit(solution)/shard_map/all_to_all | solution.py:418
  143.5 1.9 %copy-start.10 = (bf16[1024,1536]{1,0:T(8,128)(2,1)S(1)}, bf16[1024,1536]{1,0:T(8,128)(2,1)}, u32[]{:S(2)}) copy-start(bf16[1024,1536]{1,0:T(8,128)(2,1)} %copy-done.6) | copy-start | bytes 9437188
  145.4 1.9 %copy-start.12 = (bf16[1024,1536]{1,0:T(8,128)(2,1)S(1)}, bf16[1024,1536]{1,0:T(8,128)(2,1)}, u32[]{:S(2)}) copy-start(bf16[1024,1536]{1,0:T(8,128)(2,1)} %w_ref.3) | copy-start | bytes 9437188
  147.3 1.2 copy-start.23

commit v3 on v2

--- a/solution.py
+++ b/solution.py
@@ -86,13 +86,12 @@
             jax.ShapeDtypeStruct((NB, H, HD, HD), F32),
             jax.ShapeDtypeStruct((2, H, HD, HD), F32),
         ],
-        compiler_params=params(),
+        compiler_params=params(60),
         name="project",
     )(offset, x, w, g)
 
 
-def scan_body(count, back_ref, v_ref, *refs):
-    o_ref = refs[-1]
+def scan_body(count, back_ref, v_ref, o_ref):
 
     def step(t, so_far):
         i = jnp.where(back_ref[0] == 1, count - 1 - t, t)
@@ -102,16 +101,15 @@
     lax.fori_loop(0, count, step, jnp.zeros(v_ref.shape[1:], F32))
 
 
-def scan_states(back, v, after):
+def scan_states(back, v):
     return pl.pallas_call(
         functools.partial(scan_body, v.shape[0]),
-        in_specs=[pl.BlockSpec(memory_space=pltpu.SMEM), pl.BlockSpec(memory_space=pltpu.VMEM)]
-        + [pl.BlockSpec(memory_space=pl.ANY)] * len(after),
+        in_specs=[pl.BlockSpec(memory_space=pltpu.SMEM), pl.BlockSpec(memory_space=pltpu.VMEM)],
         out_specs=pl.BlockSpec(memory_space=pltpu.VMEM),
         out_shape=jax.ShapeDtypeStruct(v.shape, F32),
         compiler_params=params(4),
         name="scan_states",
-    )(back, v, *after)
+    )(back, v)
 
 
 def local_body(qkv_ref, sg_ref, kv_ref, qg_ref, o_ref):
@@ -214,57 +212,59 @@
     return (mine, second), (first, far)
 
 
-def finish_body(at_ref, w_ref, a_ref, b_ref, sa_ref, sb_ref, kx_ref, sx_ref, ky_ref, sy_ref, s_ref):
-    j = pl.program_id(0)
+def finish_body(at_ref, w_hbm, a_hbm, b_hbm, sa_ref, sb_ref, kx_ref, sx_ref, ky_ref, sy_ref, w_ref, a_ref, b_ref, s_ref, sems):
     core = at_ref[0]
-
-    def add(kind, dims):
+    copies = []
+    for j in range(3):
+        cols = pl.ds(j * 256, 256)
+        copies.append(
+            (
+                pltpu.make_async_copy(w_hbm.at[:, cols], w_ref.at[j], sems.at[0, j]),
+                pltpu.make_async_copy(a_hbm.at[:, cols], a_ref.at[j], sems.at[1, j]),
+                pltpu.make_async_copy(b_hbm.at[:, cols], b_ref.at[j], sems.at[2, j]),
+            )
+        )
+    for pair in copies:
+        for copy in pair:
+            copy.start()
+    for j, (kind, dims) in enumerate(((0, NT), (1, NT), (1, NN))):
+        for copy in copies[j]:
+            copy.wait()
         for i in range(2):
             cols = slice(i * HD, (i + 1) * HD)
             h = 2 * core + i
-            term = dot(a_ref[:, cols], sa_ref[kind, h].astype(BF16), dims)
-            term += dot(b_ref[:, cols].astype(BF16), sb_ref[kind, h].astype(BF16), dims)
-            s_ref[:, :, :, :, cols] = (w_ref[:, cols] + term).reshape(8, 4, 4, 8, HD)
-
-    @pl.when(j == 0)
-    def _():
-        add(0, NT)
-
-    @pl.when(j == 1)
-    def _():
-        add(1, NT)
-
-    @pl.when(j == 2)
-    def _():
-        add(1, NN)
-
-    kept, sent = pick(at_ref, 0)
-    for i in range(2):
-        kx_ref[:, :, i] = s_ref[:, :, kept[i], :, 0:128]
-        sx_ref[:, :, i] = s_ref[:, :, sent[i], :, 0:128]
-    kept, sent = pick(at_ref, 1)
-    for i in range(2):
-        ky_ref[:, i] = s_ref[:, kept[i], :, :, 128:256]
-        sy_ref[:, i] = s_ref[:, sent[i], :, :, 128:256]
+            far = b_ref[j, :, cols].astype(BF16)
+            term = dot(a_ref[j, :, cols], sa_ref[kind, h].astype(BF16), dims)
+            term += dot(far, sb_ref[kind, h].astype(BF16), dims)
+            s_ref[j, :, :, :, :, cols] = (w_ref[j, :, cols] + term).reshape(8, 4, 4, 8, HD)
+        lanes = slice(j * HD, (j + 1) * HD)
+        kept, sent = pick(at_ref, 0)
+        for i in range(2):
+            kx_ref[:, :, i, :, lanes] = s_ref[j, :, :, kept[i], :, 0:128]
+            sx_ref[:, :, i, :, lanes] = s_ref[j, :, :, sent[i], :, 0:128]
+        kept, sent = pick(at_ref, 1)
+        for i in range(2):
+            ky_ref[:, i, :, :, lanes] = s_ref[j, :, kept[i], :, :, 128:256]
+            sy_ref[:, i, :, :, lanes] = s_ref[j, :, sent[i], :, :, 128:256]
 
 
 def finish(at, w, a, b, sa, sb):
-    bx = pl.BlockSpec((8, 4, 2, 8, 128), lambda j, s: (0, 0, 0, 0, j))
-    by = pl.BlockSpec((8, 2, 4, 8, 128), lambda j, s: (0, 0, 0, 0, j))
-    cols = pl.BlockSpec((DM, 256), lambda j, s: (0, j))
-    states = pl.BlockSpec((2, H, HD, HD), lambda j, s: (0, 0, 0, 0))
+    vmem = pl.BlockSpec(memory_space=pltpu.VMEM)
+    hbm = pl.BlockSpec(memory_space=pltpu.HBM)
     return pl.pallas_call(
         finish_body,
-        grid_spec=pltpu.PrefetchScalarGridSpec(
-            num_scalar_prefetch=1,
-            grid=(3,),
-            in_specs=[cols, cols, cols, states, states],
-            out_specs=[bx, bx, by, by],
-            scratch_shapes=[pltpu.VMEM((8, 4, 4, 8, 256), F32)],
-        ),
+        in_specs=[pl.BlockSpec(memory_space=pltpu.SMEM), hbm, hbm, hbm, vmem, vmem],
+        out_specs=[vmem] * 4,
         out_shape=[jax.ShapeDtypeStruct((8, 4, 2, 8, 384), F32)] * 2
         + [jax.ShapeDtypeStruct((8, 2, 4, 8, 384), F32)] * 2,
-        compiler_params=params(24),
+        scratch_shapes=[
+            pltpu.VMEM((3, DM, 256), F32),
+            pltpu.VMEM((3, DM, 256), BF16),
+            pltpu.VMEM((3, DM, 256), F32),
+            pltpu.VMEM((3, 8, 4, 4, 8, 256), F32),
+            pltpu.SemaphoreType.DMA((3, 3)),
+        ],
+        compiler_params=params(49),
         cost_estimate=cost(1e9, 12e6),
         name="finish",
     )(at, w, a, b, sa, sb)
@@ -299,7 +299,7 @@
         out_specs=block(DM),
         out_shape=jax.ShapeDtypeStruct((TOK, DM), BF16),
         scratch_shapes=[pltpu.VMEM((CH, 3 * D), BF16)],
-        compiler_params=params(24),
+        compiler_params=params(48),
         cost_estimate=cost(5e9, 14e6),
         name="inputs_grad",
     )(loc, qkv, sg, states, weights)
@@ -391,7 +391,7 @@
     factors_in = lax.ppermute(factors_out, "core", SWAP)
     local_in = lax.ppermute(local_out, "core", SWAP)
 
-    scanned = scan_states(back, slices, [])
+    scanned = scan_states(back, slices)
     states = lax.all_to_all(scanned, ("z", "y"), 0, 0, tiled=True)
     mine = factors(at, x, sg, qkv, True, BF16, "factors_keep")
     both = local_part(at, x, loc, local_in, "local_keep")
@@ -403,6 +403,7 @@
     rx = exchange(sx, "x", 0)
     ry = exchange(sy, "y", 0)
     record_grad = inputs_grad(loc, qkv, sg, states, weights)
+    rx, ry, record_grad = lax.optimization_barrier((rx, ry, record_grad))
     kx, sx, ky, sy = whole_call(add1_body, "add1", [(8, 4, 8, 384)] * 4, kx, rx, ky, ry)
     rx = exchange(sx, "x", 1)
     ry = exchange(sy, "y", 1)

time: 157 us -> 140 us (0.89)
  local copies, waits for them, and re-layouts: 30.8 us -> 13.2 us
  blocking collectives: 12.5 us -> 27.1 us
  starting transfers between devices: 43.6 us -> 32.8 us
  waiting for transfers between devices: 28.7 us -> 20.9 us
  Pallas kernels: 39.7 us -> 44.2 us
    unnamed x58 -> x32, local copies, waits for them, and re-layouts: 30.7 us -> 13.1 us
    all_to_all x0 -> x1, blocking collectives: none -> 14.7 us  [shards(): rows = lax.all_to_all(mine, ('x', 'core'), 0, 0, tiled=True)]
    all_to_all x1 -> x0, starting transfers between devices: 10.7 us -> none  [shards(): rows = lax.all_to_all(mine, ('x', 'core'), 0, 0, tiled=True)]
    ppermute x8, waiting for transfers between devices: 25.2 us -> 17.4 us  [exchange(): return lax.ppermute(value, (axis, 'core'), pairs)]
    pallas_call x1, Pallas kernels: 5.87 us -> 9.32 us  [project(): pl.pallas_call(project_body, grid_spec=pltpu.PrefetchScalarGridSpec(num_s...]
  transfers between devices with their start and end apart: 14 -> 13, of which waited for: 10 -> 9; matrix products, arithmetic and copies ran while one was open for 0% -> 0% of each run, Pallas kernels for 17% -> 20%
where the time goes in v3:
time: 140 us; the launch traced here: 139 us
  Pallas kernels  44.2 us (32%)
  starting transfers between devices  32.8 us (23%)
  blocking collectives  27.1 us (19%)
  waiting for transfers between devices  20.9 us (15%)
  local copies, waits for them, and re-layouts  13.2 us (9%)
    ppermute x8, waiting for transfers between devices, exchange(): return lax.ppermute(value, (axis, 'core'), pairs)  17.4 us
    all_to_all x1, blocking collectives, shards(): rows = lax.all_to_all(mine, ('x', 'core'), 0, 0, tiled=True)  14.7 us
    unnamed x32, local copies, waits for them, and re-layouts  13.1 us
    all_to_all x1, blocking collectives, shards(): part = lax.all_to_all(part, 'z', 0, 0, tiled=True)  12.4 us
    all_to_all x1, starting transfers between devices, shards(): lax.all_to_all(total.reshape(32, 32, HD), ('z', 'y'), 0, 0, tiled=True)  12.2 us
    pallas_call x1, Pallas kernels, project(): pl.pallas_call(project_body, grid_spec=pltpu.PrefetchScalarGridSpec(num_s...  9.32 us
    all_to_all x1, starting transfers between devices, shards(): states = lax.all_to_all(scanned, ('z', 'y'), 0, 0, tiled=True)  8.59 us
    pallas_call x1, Pallas kernels, inputs_grad(): pl.pallas_call(inputs_body, grid=(NB,), in_specs=[block(3 * D), block(3 *...  8.28 us
  transfers between devices with their start and end apart: 13, of which 9 were waited for; matrix products, arithmetic and copies ran while one was open for 0% of the time, Pallas kernels for 20%

profile of v3, /device:TPU:1, one launch (start us, length us, event | category | flops | bytes accessed | tf_op | source)
XLA Modules:
  0.0 139.2 jit_solution(4826842411908937091)
XLA Ops:
  0.6 0.0 copy-start
  0.7 9.3 %project.1 = (bf16[1024,1536]{1,0:T(8,128)(2,1)}, bf16[1024,512]{1,0:T(8,128)(2,1)}, f32[4,4,128,128]{3,2,1,0:T(8,128)}, f32[4,4,128,128]{3,2,1,0:T(8,128)}, f32[2,4,128,128]{3,2,1,0:T(8,128)}) custom-call(s32[1]{0:T(128)} %bitcast.10.pos_ref, bf16[1024,1024]{1,0:T(8,128)(2,1)} %bitcast.16, bf16[1024,1536]{1,0:T(8,128)(2,1)} %w_ref.3, bf16[1024,512]{1,0:T(8,128)(2,1)} %bitcast.21), custom_call_target="tpu_custom_call" | custom-call | tf_op jit(solution)/shard_map/project/pallas_call | solution.py:68
  10.0 12.2 %all-to-all-start = ((f32[32,32,128]{2,1,0:T(8,128)}), f32[32,32,128]{2,1,0:T(8,128)}, u32[]{:S(2)}, u32[]{:S(2)}) async-start(f32[32,32,128]{2,1,0:T(8,128)} %bitcast.22), calls=%async_computation | async-start | bytes 1048576 | tf_op jit(solution)/shard_map/all_to_all | solution.py:386
  22.2 0.1 stack.39.at_ref.at
  22.3 0.0 copy-done
  22.3 0.0 copy-start.4
  22.3 1.9 %copy-done.4 = bf16[1024,1536]{1,0:T(8,128)(2,1)S(1)} copy-done((bf16[1024,1536]{1,0:T(8,128)(2,1)S(1)}, bf16[1024,1536]{1,0:T(8,128)(2,1)}, u32[]{:S(2)}) %copy-start.4) | copy-done | bytes 3145752
  24.2 1.2 copy-done.11
  25.4 2.9 %factors_give.1 = f32[1024,768]{1,0:T(8,128)S(1)} custom-call(s32[9]{0:T(128)S(1)} %stack.39.at_ref.at, bf16[1024,1024]{1,0:T(8,128)(2,1)S(1)} %bitcast.17, bf16[1024,512]{1,0:T(8,128)(2,1)S(1)} %copy-done.11, bf16[1024,1536]{1,0:T(8,128)(2,1)S(1)} %copy-done.4, bf16[1024,1536]{1,0:T(8,128)(2,1)S(1)} %copy-done.4), custom_call_target="tpu_custom_call" | custom-call | flops 3000000000 | bytes 12000000 | tf_op jit(solution)/shard_map/factors_give/pallas_call | solution.py:161
  28.3 0.0 copy-start.7
  28.4 0.0 copy-done.5
  28.4 0.0 copy-done.14
  28.4 0.0 copy-done.15
  28.4 0.0 copy-start.1
  28.4 5.8 %local.1.q_ref.k_ref.v_ref.loc_ref = bf16[1024,1536]{1,0:T(8,128)(2,1)S(1)} custom-call(bf16[1024,1536]{1,0:T(8,128)(2,1)S(1)} %copy-done.5, bf16[1024,512]{1,0:T(8,128)(2,1)S(1)} %copy-done.11, f32[4,4,128,128]{3,2,1,0:T(8,128)S(1)} %copy-done.14, f32[4,4,128,128]{3,2,1,0:T(8,128)S(1)} %copy-done.15), custom_call_target="tpu_custom_call" | custom-call | flops 4000000000 | bytes 20000000 | tf_op jit(solution)/shard_map/local/pallas_call | solution.py:140
  34.2 0.0 copy-done.7
  34.2 2.9 %local_give.1 = f32[1024,768]{1,0:T(8,128)S(1)} custom-call(s32[9]{0:T(128)S(1)} %stack.39.at_ref.at, bf16[1024,1024]{1,0:T(8,128)(2,1)S(1)} %bitcast.18, bf16[1024,1536]{1,0:T(8,128)(2,1)S(1)} %local.1.q_ref.k_ref.v_ref.loc_ref, bf16[1024,1536]{1,0:T(8,128)(2,1)S(1)} %local.1.q_ref.k_ref.v_ref.loc_ref, bf16[1024,1536]{1,0:T(8,128)(2,1)S(1)} %local.1.q_ref.k_ref.v_ref.loc_ref), custom_call_target="tpu_custom_call" | custom-call | flops 3000000000 | bytes 12000000 | tf_op jit(solution)/shard_map/local_give/pallas_call | solution.py:194
  37.2 1.7 %copy-done.8 = f32[1024,768]{1,0:T(8,128)} copy-done((f32[1024,768]{1,0:T(8,128)}, f32[1024,768]{1,0:T(8,128)S(1)}, u32[]{:S(2)}) %copy-start.8) | copy-done | bytes 3145752
  38.9 0.0 all-to-all-done.v_ref
  38.9 1.9 %collective-permute-start = (f32[1024,768]{1,0:T(8,128)}, f32[1024,768]{1,0:T(8,128)}, u32[]{:S(2)}, u32[]{:S(2)}) collective-permute-start(f32[1024,768]{1,0:T(8,128)} %copy-done.8), channel_id=1, source_target_pairs={{0,1},{1,0},{2,3},{3,2},{4,5},{5,4},{6,7},{7,6},{8,9},{9,8},{10,11... | collective-permute-start | bytes 9437192 | tf_op jit(solution)/shard_map/ppermute | solution.py:392
  40.8 0.0 collective-permute-start.1
  40.8 1.3 scan_states.1
  42.1 0.0 copy-start.9
  42.1 0.8 copy-done.9
  42.9 8.6 %all-to-all-start.1 = ((f32[32,32,128]{2,1,0:T(8,128)}), f32[32,32,128]{2,1,0:T(8,128)}, u32[]{:S(2)}, u32[]{:S(2)}) async-start(f32[32,32,128]{2,1,0:T(8,128)} %copy-done.9), calls=%async_computation.1 | async-start | bytes 1048576 | tf_op jit(solution)/shard_map/all_to_all | solution.py:395
  51.5 0.0 copy-start.2
  51.5 1.6 %copy-done.2 = bf16[1,1024,1024]{2,1,0:T(8,128)(2,1)S(1)} copy-done((bf16[1,1024,1024]{2,1,0:T(8,128)(2,1)S(1)}, bf16[1,1024,1024]{2,1,0:T(8,128)(2,1)}, u32[]{:S(2)}) %copy-start.2) | copy-done | bytes 2097176
  53.1 1.9 %copy-done.6 = bf16[1024,1536]{1,0:T(8,128)(2,1)S(1)} copy-done((bf16[1024,1536]{1,0:T(8,128)(2,1)S(1)}, bf16[1024,1536]{1,0:T(8,128)(2,1)}, u32[]{:S(2)}) %copy-start.6) | copy-done | bytes 3145752
  55.0 1.2 copy-done.12
  56.2 2.9 %factors_keep.1.a_hbm = bf16[1024,768]{1,0:T(8,128)(2,1)S(1)} custom-call(s32[9]{0:T(128)S(1)} %stack.39.at_ref.at, bf16[1024,1024]{1,0:T(8,128)(2,1)S(1)} %bitcast.19, bf16[1024,512]{1,0:T(8,128)(2,1)S(1)} %copy-done.12, bf16[1024,1536]{1,0:T(8,128)(2,1)S(1)} %copy-done.6, bf16[1024,1536]{1,0:T(8,128)(2,1)S(1)} %copy-done.6), custom_call_target="tpu_custom_call" | custom-call | flops 3000000000 | bytes 12000000 | tf_op jit(solution)/shard_map/factors_keep/pallas_call | solution.py:161
  59.2 0.0 copy-start.10
  59.2 1.1 copy-done.10
  60.3 0.0 collective-permute-done.r_ref
  60.3 4.2 %local_keep.1.w_hbm = f32[1024,768]{1,0:T(8,128)S(1)} custom-call(s32[9]{0:T(128)S(1)} %stack.39.at_ref.at, bf16[1024,1024]{1,0:T(8,128)(2,1)S(1)} %bitcast.20, bf16[1024,1536]{1,0:T(8,128)(2,1)S(1)} %local.1.q_ref.k_ref.v_ref.loc_ref, bf16[1024,1536]{1,0:T(8,128)(2,1)S(1)} %local.1.q_ref.k_ref.v_ref.loc_ref, ...), custom_call_target="tpu_custom_call" | custom-call | flops 3000000000 | bytes 12000000 | tf_op jit(solution)/shard_map/local_keep/pallas_call | solution.py:194
  64.5 0.0 copy-start.3
  64.5 1.7 %copy-done.3 = f32[1024,768]{1,0:T(8,128)} copy-done((f32[1024,768]{1,0:T(8,128)}, f32[1024,768]{1,0:T(8,128)S(1)}, u32[]{:S(2)}) %copy-start.3) | copy-done | bytes 3145752
  66.2 1.8 %all-to-all-done.1 = f32[32,32,128]{2,1,0:T(8,128)} async-done(((f32[32,32,128]{2,1,0:T(8,128)}), f32[32,32,128]{2,1,0:T(8,128)}, u32[]{:S(2)}, u32[]{:S(2)}) %all-to-all-start.1) | async-done | bytes 524320 | tf_op jit(solution)/shard_map/all_to_all | solution.py:395
  67.9 2.3 %collective-permute-start.2 = (f32[2,4,128,128]{3,2,1,0:T(8,128)}, f32[2,4,128,128]{3,2,1,0:T(8,128)S(1)}, u32[]{:S(2)}, u32[]{:S(2)}) collective-permute-start(f32[2,4,128,128]{3,2,1,0:T(8,128)} %bitcast.14.sa_ref.s_ref), channel_id=1, source_target_pairs={{0,1},{1,0},{2,3},{3,2},{4,5},{5,4},{6,7},{7,6},{8,9},{9,8},{10,11... | collective-permute-start | bytes 1572872 | tf_op jit(solution)/shard_map/ppermute | solution.py:401
  70.2 0.0 collective-permute-done.1.b_hbm
  70.2 1.7 %collective-permute-done.2.sb_ref = f32[2,4,128,128]{3,2,1,0:T(8,128)S(1)} collective-permute-done((f32[2,4,128,128]{3,2,1,0:T(8,128)}, f32[2,4,128,128]{3,2,1,0:T(8,128)S(1)}, u32[]{:S(2)}, u32[]{:S(2)}) %collective-permute-start.2) | collective-permute-done | bytes 524320 | tf_op jit(solution)/shard_map/ppermute | solution.py:401
  72.0 5.0 %finish.1 = (f32[8,4,2,8,384]{4,3,2,1,0:T(8,128)S(1)}, f32[8,4,2,8,384]{4,3,2,1,0:T(8,128)S(1)}, f32[8,2,4,8,384]{4,3,2,1,0:T(8,128)S(1)}, f32[8,2,4,8,384]{4,3,2,1,0:T(8,128)S(1)}) custom-call(s32[9]{0:T(128)S(1)} %stack.39.at_ref.at, f32[1024,768]{1,0:T(8,128)} %copy-done.3, bf16[1024,768]{1,0:T(8,128)(2,1)} %copy-done.10, ...), custom_call_target="tpu_custom_call" | custom-call | flops 1000000000 | bytes 12000000 | tf_op jit(solution)/shard_map/finish/pallas_call | solution.py:254
  76.9 2.7 %collective-permute-start.3 = (f32[8,4,2,8,384]{4,3,2,1,0:T(8,128)S(1)}, f32[8,4,2,8,384]{4,3,2,1,0:T(8,128)S(1)}, u32[]{:S(2)}, u32[]{:S(2)}) collective-permute-start(f32[8,4,2,8,384]{4,3,2,1,0:T(8,128)S(1)} %get-tuple-element.43), channel_id=1, source_target_pairs={{0,2},{1,7},{2,0},{3,5},{4,6},{5,3},{6,4},{7,1},{8,10},{9,15},{10,... | collective-permute-start | bytes 2359304 | tf_op jit(solution)/shard_map/ppermute | solution.py:369
  79.7 1.8 %collective-permute-start.4 = (f32[8,2,4,8,384]{4,3,2,1,0:T(8,128)S(1)}, f32[8,2,4,8,384]{4,3,2,1,0:T(8,128)S(1)}, u32[]{:S(2)}, u32[]{:S(2)}) collective-permute-start(f32[8,2,4,8,384]{4,3,2,1,0:T(8,128)S(1)} %get-tuple-element.44), channel_id=1, source_target_pairs={{0,8},{1,25},{8,0},{9,17},{16,24},{17,9},{24,16},{25,1},{2,10},{3,... | collective-permute-start | bytes 2359304 | tf_op jit(solution)/shard_map/ppermute | solution.py:369
  81.5 0.0 copy-done.13
  81.5 8.3 %inputs_grad.1 = bf16[1024,1024]{1,0:T(8,128)(2,1)} custom-call(bf16[1024,1536]{1,0:T(8,128)(2,1)S(1)} %local.1.q_ref.k_ref.v_ref.loc_ref, bf16[1024,1536]{1,0:T(8,128)(2,1)} %get-tuple-element.34.k_ref.v_ref.qkv_ref, bf16[1024,512]{1,0:T(8,128)(2,1)S(1)} %copy-done.13, f32[2,4,128,128]{3,2,1,0:T(8,128)} %bitcast.14.sa_ref.s_ref, bf16[1024,1536]{1,0:T(8,128)(2,1)} %w_ref.3), custom_call_target="tpu_custom_call" | custom-call | flops 5000000000 | bytes 14000000 | tf_op jit(solution)/shard_map/inputs_grad/pallas_call | solution.py:289
  89.8 0.0 collective-permute-done.3.rx
  89.8 2.0 %collective-permute-done.4.ry = f32[8,2,4,8,384]{4,3,2,1,0:T(8,128)S(1)} collective-permute-done((f32[8,2,4,8,384]{4,3,2,1,0:T(8,128)S(1)}, f32[8,2,4,8,384]{4,3,2,1,0:T(8,128)S(1)}, u32[]{:S(2)}, u32[]{:S(2)}) %collective-permute-start.4) | collective-permute-done | bytes 786464 | tf_op jit(solution)/shard_map/ppermute | solution.py:369
  91.7 0.2 add1.1
  91.9 0.1 collective-permute-start.5
  92.0 0.1 collective-permute-start.6
  92.1 6.8 %collective-permute-done.5.rx = f32[8,4,8,384]{3,2,1,0:T(8,128)S(1)} collective-permute-done((f32[8,4,8,384]{3,2,1,0:T(8,128)S(1)}, f32[8,4,8,384]{3,2,1,0:T(8,128)S(1)}, u32[]{:S(2)}, u32[]{:S(2)}) %collective-permute-start.5) | collective-permute-done | bytes 393248 | tf_op jit(solution)/shard_map/ppermute | solution.py:369
  98.9 0.1 collective-permute-done.6.ry
  99.0 0.6 add2.1
  99.7 1.9 %collective-permute-start.7 = (f32[8,2,8,384]{3,2,1,0:T(8,128)S(1)}, f32[8,2,8,384]{3,2,1,0:T(8,128)S(1)}, u32[]{:S(2)}, u32[]{:S(2)}) collective-permute-start(f32[8,2,8,384]{3,2,1,0:T(8,128)S(1)} %get-tuple-element.55), channel_id=1, source_target_pairs={{0,8},{1,25},{8,0},{9,17},{16,24},{17,9},{24,16},{25,1},{2,10},{3,... | collective-permute-start | bytes 589832 | tf_op jit(solution)/shard_map/ppermute | solution.py:369
  101.5 0.7 collective-permute-start.8
  102.2 3.3 %collective-permute-done.7.rp = f32[8,2,8,384]{3,2,1,0:T(8,128)S(1)} collective-permute-done((f32[8,2,8,384]{3,2,1,0:T(8,128)S(1)}, f32[8,2,8,384]{3,2,1,0:T(8,128)S(1)}, u32[]{:S(2)}, u32[]{:S(2)}) %collective-permute-start.7) | collective-permute-done | bytes 196640 | tf_op jit(solution)/shard_map/ppermute | solution.py:369
  105.5 1.8 %collective-permute-done.8.rq = f32[8,2,8,384]{3,2,1,0:T(8,128)S(1)} collective-permute-done((f32[8,2,8,384]{3,2,1,0:T(8,128)S(1)}, f32[8,2,8,384]{3,2,1,0:T(8,128)S(1)}, u32[]{:S(2)}, u32[]{:S(2)}) %collective-permute-start.8) | collective-permute-done | bytes 196640 | tf_op jit(solution)/shard_map/ppermute | solution.py:369
  107.3 0.5 collective-permute-start.10
  107.8 0.0 collective-permute-start.9
  107.8 3.0 %collective-permute-done.10.rq = f32[8,8,384]{2,1,0:T(8,128)S(1)} collective-permute-done((f32[8,8,384]{2,1,0:T(8,128)S(1)}, f32[8,8,384]{2,1,0:T(8,128)S(1)}, u32[]{:S(2)}, u32[]{:S(2)}) %collective-permute-start.10) | collective-permute-done | bytes 98336 | tf_op jit(solution)/shard_map/ppermute | solution.py:369
  110.8 0.5 collective-permute-done.9.rp
  111.3 12.4 %all_to_all.20.v = f32[8,8,768]{2,1,0:T(8,128)S(1)} all-to-all(f32[8,8,768]{2,1,0:T(8,128)S(1)} %add4.1), channel_id=1, replica_groups=mesh['z'=8,'y'=4,'x'=4,'core'=2] {'z'}, dimensions={0} | all-to-all | bytes 393216 | tf_op jit(solution)/shard_map/all_to_all | solution.py:417
  123.8 14.7 %all_to_all.21.v = f32[8,8,768]{2,1,0:T(8,128)S(1)} all-to-all(f32[8,8,768]{2,1,0:T(8,128)S(1)} %sum_z.1), channel_id=1, replica_groups=mesh['z'=8,'y'=4,'x'=4,'core'=2] {'x','core'}, dimensions={0} | all-to-all | bytes 393216 | tf_op jit(solution)/shard_map/all_to_all | solution.py:419
  138.5 0.7 place.1
  (12 shorter events, 0.1 us)
Async XLA Ops:
  0.6 21.6 %copy-start = (bf16[1,1024,1024]{2,1,0:T(8,128)(2,1)S(1)}, bf16[1,1024,1024]{2,1,0:T(8,128)(2,1)}, u32[]{:S(2)}) copy-start(bf16[1,1024,1024]{2,1,0:T(8,128)(2,1)} %param.3) | copy-start | bytes 6291460
  10.0 28.9 %all-to-all-start = ((f32[32,32,128]{2,1,0:T(8,128)}), f32[32,32,128]{2,1,0:T(8,128)}, u32[]{:S(2)}, u32[]{:S(2)}) async-start(f32[32,32,128]{2,1,0:T(8,128)} %bitcast.22), calls=%async_computation | async-start | bytes 1048576 | tf_op jit(solution)/shard_map/all_to_all | solution.py:386
  22.3 1.9 %copy-start.4 = (bf16[1024,1536]{1,0:T(8,128)(2,1)S(1)}, bf16[1024,1536]{1,0:T(8,128)(2,1)}, u32[]{:S(2)}) copy-start(bf16[1024,1536]{1,0:T(8,128)(2,1)} %get-tuple-element.34.k_ref.v_ref.qkv_ref) | copy-start | bytes 9437188
  24.2 1.2 copy-start.11
  25.4 3.0 %copy-start.5 = (bf16[1024,1536]{1,0:T(8,128)(2,1)S(1)}, bf16[1024,1536]{1,0:T(8,128)(2,1)}, u32[]{:S(2)}) copy-start(bf16[1024,1536]{1,0:T(8,128)(2,1)} %get-tuple-element.34.k_ref.v_ref.qkv_ref) | copy-start | bytes 9437188
  25.4 3.0 %copy-start.14 = (f32[4,4,128,128]{3,2,1,0:T(8,128)S(1)}, f32[4,4,128,128]{3,2,1,0:T(8,128)}, u32[]{:S(2)}) copy-start(f32[4,4,128,128]{3,2,1,0:T(8,128)} %get-tuple-element.35.kv_ref) | copy-start | bytes 3145732
  25.4 3.0 %copy-start.15 = (f32[4,4,128,128]{3,2,1,0:T(8,128)S(1)}, f32[4,4,128,128]{3,2,1,0:T(8,128)}, u32[]{:S(2)}) copy-start(f32[4,4,128,128]{3,2,1,0:T(8,128)} %get-tuple-element.36.qg_ref) | copy-start | bytes 3145732
  28.3 5.9 %copy-start.7 = (f32[1024,768]{1,0:T(8,128)}, f32[1024,768]{1,0:T(8,128)S(1)}, u32[]{:S(2)}) copy-start(f32[1024,768]{1,0:T(8,128)S(1)} %factors_give.1) | copy-start | bytes 9437188
  28.4 5.8 %copy-start.1 = (bf16[1,1024,1024]{2,1,0:T(8,128)(2,1)S(1)}, bf16[1,1024,1024]{2,1,0:T(8,128)(2,1)}, u32[]{:S(2)}) copy-start(bf16[1,1024,1024]{2,1,0:T(8,128)(2,1)} %param.3) | copy-start | bytes 6291460
  37.2 1.7 %copy-start.8 = (f32[1024,768]{1,0:T(8,128)}, f32[1024,768]{1,0:T(8,128)S(1)}, u32[]{:S(2)}) copy-start(f32[1024,768]{1,0:T(8,128)S(1)} %local_give.1) | copy-start | bytes 9437188
  38.9 21.4 %collective-permute-start = (f32[1024,768]{1,0:T(8,128)}, f32[1024,768]{1,0:T(8,128)}, u32[]{:S(2)}, u32[]{:S(2)}) collective-permute-start(f32[1024,768]{1,0:T(8,128)} %copy-done.8), channel_id=1, source_target_pairs={{0,1},{1,0},{2,3},{3,2},{4,5},{5,4},{6,7},{7,6},{8,9},{9,8},{10,11... | collective-permute-start | bytes 9437192 | tf_op jit(solution)/shard_map/ppermute | solution.py:392
  40.8 29.4 %collective-permute-start.1 = (f32[1024,768]{1,0:T(8,128)}, f32[1024,768]{1,0:T(8,128)}, u32[]{:S(2)}, u32[]{:S(2)}) collective-permute-start(f32[1024,768]{1,0:T(8,128)} %copy-done.7), channel_id=1, source_target_pairs={{0,1},{1,0},{2,3},{3,2},{4,5},{5,4},{6,7},{7,6},{8,9},{9,8},{10,11... | collective-permute-start | bytes 9437192 | tf_op jit(solution)/shard_map/ppermute | solution.py:391
  42.1 0.8 copy-start.9
  42.9 25.0 %all-to-all-start.1 = ((f32[32,32,128]{2,1,0:T(8,128)}), f32[32,32,128]{2,1,0:T(8,128)}, u32[]{:S(2)}, u32[]{:S(2)}) async-start(f32[32,32,128]{2,1,0:T(8,128)} %copy-done.9), calls=%async_computation.1 | async-start | bytes 1048576 | tf_op jit(solution)/shard_map/all_to_all | solution.py:395
  51.5 1.6 %copy-start.2 = (bf16[1,1024,1024]{2,1,0:T(8,128)(2,1)S(1)}, bf16[1,1024,1024]{2,1,0:T(8,128)(2,1)}, u32[]{:S(2)}) copy-start(bf16[1,1024,1024]{2,1,0:T(8,128)(2,1)} %param.3) | copy-start | bytes 6291460
  53.1 1.9 %copy-start.6 = (bf16[1024,1536]{1,0:T(8,128)(2,1)S(1)}, bf16[1024,1536]{1,0:T(8,128)(2,1)}, u32[]{:S(2)}) copy-start(bf16[1024,1536]{1,0:T(8,128)(2,1)} %get-tuple-element.34.k_ref.v_ref.qkv_ref) | copy-start | bytes 9437188
  55.0 1.2 copy-start.12
  59.2 1.1 copy-start.10
  64.5 1.7 %copy-start.3 = (f32[1024,768]{1,0:T(8,128)}, f32[1024,768]{1,0:T(8,128)S(1)}, u32[]{:S(2)}) copy-start(f32[1024,768]{1,0:T(8,128)S(1)} %local_keep.1.w_hbm) | copy-start | bytes 9437188
  67.9 13.5 %copy-start.13 = (bf16[1024,512]{1,0:T(8,128)(2,1)S(1)}, bf16[1024,512]{1,0:T(8,128)(2,1)}, u32[]{:S(2)}) copy-start(bf16[1024,512]{1,0:T(8,128)(2,1)} %get-tuple-element.33.g_ref.sg_ref) | copy-start | bytes 3145732
  67.9 4.0 %collective-permute-start.2 = (f32[2,4,128,128]{3,2,1,0:T(8,128)}, f32[2,4,128,128]{3,2,1,0:T(8,128)S(1)}, u32[]{:S(2)}, u32[]{:S(2)}) collective-permute-start(f32[2,4,128,128]{3,2,1,0:T(8,128)} %bitcast.14.sa_ref.s_ref), channel_id=1, source_target_pairs={{0,1},{1,0},{2,3},{3,2},{4,5},{5,4},{6,7},{7,6},{8,9},{9,8},{10,11... | collective-permute-start | bytes 1572872 | tf_op jit(solution)/shard_map/ppermute | solution.py:401
  76.9 12.8 %collective-permute-start.3 = (f32[8,4,2,8,384]{4,3,2,1,0:T(8,128)S(1)}, f32[8,4,2,8,384]{4,3,2,1,0:T(8,128)S(1)}, u32[]{:S(2)}, u32[]{:S(2)}) collective-permute-start(f32[8,4,2,8,384]{4,3,2,1,0:T(8,128)S(1)} %get-tuple-element.43), channel_id=1, source_target_pairs={{0,2},{1,7},{2,0},{3,5},{4,6},{5,3},{6,4},{7,1},{8,10},{9,15},{10,... | collective-permute-start | bytes 2359304 | tf_op jit(solution)/shard_map/ppermute | solution.py:369
  79.7 12.1 %collective-permute-start.4 = (f32[8,2,4,8,384]{4,3,2,1,0:T(8,128)S(1)}, f32[8,2,4,8,384]{4,3,2,1,0:T(8,128)S(1)}, u32[]{:S(2)}, u32[]{:S(2)}) collective-permute-start(f32[8,2,4,8,384]{4,3,2,1,0:T(8,128)S(1)} %get-tuple-element.44), channel_id=1, source_target_pairs={{0,8},{1,25},{8,0},{9,17},{16,24},{17,9},{24,16},{25,1},{2,10},{3,... | collective-permute-start | bytes 2359304 | tf_op jit(solution)/shard_map/ppermute | solution.py:369
  91.9 7.0 %collective-permute-start.5 = (f32[8,4,8,384]{3,2,1,0:T(8,128)S(1)}, f32[8,4,8,384]{3,2,1,0:T(8,128)S(1)}, u32[]{:S(2)}, u32[]{:S(2)}) collective-permute-start(f32[8,4,8,384]{3,2,1,0:T(8,128)S(1)} %get-tuple-element.51), channel_id=1, source_target_pairs={{0,6},{1,3},{2,4},{3,1},{4,2},{5,7},{6,0},{7,5},{8,14},{9,11},{10,... | collective-permute-start | bytes 1179656 | tf_op jit(solution)/shard_map/ppermute | solution.py:369
  92.0 7.0 %collective-permute-start.6 = (f32[8,4,8,384]{3,2,1,0:T(8,128)S(1)}, f32[8,4,8,384]{3,2,1,0:T(8,128)S(1)}, u32[]{:S(2)}, u32[]{:S(2)}) collective-permute-start(f32[8,4,8,384]{3,2,1,0:T(8,128)S(1)} %get-tuple-element.53), channel_id=1, source_target_pairs={{0,24},{1,9},{8,16},{9,1},{16,8},{17,25},{24,0},{25,17},{2,26},{3,... | collective-permute-start | bytes 1179656 | tf_op jit(solution)/shard_map/ppermute | solution.py:369
  99.7 5.8 %collective-permute-start.7 = (f32[8,2,8,384]{3,2,1,0:T(8,128)S(1)}, f32[8,2,8,384]{3,2,1,0:T(8,128)S(1)}, u32[]{:S(2)}, u32[]{:S(2)}) collective-permute-start(f32[8,2,8,384]{3,2,1,0:T(8,128)S(1)} %get-tuple-element.55), channel_id=1, source_target_pairs={{0,8},{1,25},{8,0},{9,17},{16,24},{17,9},{24,16},{25,1},{2,10},{3,... | collective-permute-start | bytes 589832 | tf_op jit(solution)/shard_map/ppermute | solution.py:369
  101.5 5.7 %collective-permute-start.8 = (f32[8,2,8,384]{3,2,1,0:T(8,128)S(1)}, f32[8,2,8,384]{3,2,1,0:T(8,128)S(1)}, u32[]{:S(2)}, u32[]{:S(2)}) collective-permute-start(f32[8,2,8,384]{3,2,1,0:T(8,128)S(1)} %get-tuple-element.57), channel_id=1, source_target_pairs={{0,2},{1,7},{2,0},{3,5},{4,6},{5,3},{6,4},{7,1},{8,10},{9,15},{10,... | collective-permute-start | bytes 589832 | tf_op jit(solution)/shard_map/ppermute | solution.py:369
  107.3 3.6 %collective-permute-start.10 = (f32[8,8,384]{2,1,0:T(8,128)S(1)}, f32[8,8,384]{2,1,0:T(8,128)S(1)}, u32[]{:S(2)}, u32[]{:S(2)}) collective-permute-start(f32[8,8,384]{2,1,0:T(8,128)S(1)} %get-tuple-element.61), channel_id=1, source_target_pairs={{0,6},{1,3},{2,4},{3,1},{4,2},{5,7},{6,0},{7,5},{8,14},{9,11},{10,... | collective-permute-start | bytes 294920 | tf_op jit(solution)/shard_map/ppermute | solution.py:369
  107.8 3.5 %collective-permute-start.9 = (f32[8,8,384]{2,1,0:T(8,128)S(1)}, f32[8,8,384]{2,1,0:T(8,128)S(1)}, u32[]{:S(2)}, u32[]{:S(2)}) collective-permute-start(f32[8,8,384]{2,1,0:T(8,128)S(1)} %get-tuple-element.59), channel_id=1, source_target_pairs={{0,24},{1,9},{8,16},{9,1},{16,8},{17,25},{24,0},{25,17},{2,26},{3,... | collective-permute-start | bytes 294920 | tf_op jit(solution)/shard_map/ppermute | solution.py:369

commit v4 on v3

--- a/solution.py
+++ b/solution.py
@@ -143,68 +143,58 @@
         in_specs=[block(3 * D), block(D), sums, sums],
         out_specs=block(3 * D),
         out_shape=jax.ShapeDtypeStruct((TOK, 3 * D), BF16),
-        compiler_params=params(20),
+        compiler_params=params(60),
         cost_estimate=cost(4e9, 20e6),
         name="local",
     )(qkv, sg, kv, qg)
 
 
-def factors_body(at_ref, x_ref, g_ref, k_ref, v_ref, o_ref):
-    for j, ref in enumerate((g_ref, v_ref, k_ref)):
-        o_ref[:, j * 256 : (j + 1) * 256] = dot(x_ref[...], ref[...], TN).astype(o_ref.dtype)
-
-
-def factors(at, x, sg, qkv, mine, kind, name):
-    def cols(first):
-        return pl.BlockSpec((TOK, 256), lambda i, s: (0, first + (s[0] if mine else 1 - s[0])))
-
-    return pl.pallas_call(
-        factors_body,
+def give_body(at_ref, x_ref, *refs):
+    for j, ref in enumerate(refs[:3]):
+        refs[3][:, j * 256 : (j + 1) * 256] = dot(x_ref[...], ref[...], TN)
+
+
+def give(at, x, sources, name):
+    cols = [pl.BlockSpec((TOK, 256), lambda i, s, f=f: (0, f + 1 - s[0])) for _, f in sources]
+    return pl.pallas_call(
+        give_body,
         grid_spec=pltpu.PrefetchScalarGridSpec(
             num_scalar_prefetch=1,
-            grid=(2,),
-            in_specs=[pl.BlockSpec((TOK, DM // 2), lambda i, s: (0, i)), cols(0), cols(2), cols(4)],
-            out_specs=pl.BlockSpec((DM // 2, 768), lambda i, s: (i, 0)),
+            grid=(4,),
+            in_specs=[pl.BlockSpec((TOK, DM // 4), lambda i, s: (0, i))] + cols,
+            out_specs=pl.BlockSpec((DM // 4, 768), lambda i, s: (i, 0)),
         ),
-        out_shape=jax.ShapeDtypeStruct((DM, 768), kind),
-        compiler_params=params(24),
+        out_shape=jax.ShapeDtypeStruct((DM, 768), F32),
+        compiler_params=params(60),
         cost_estimate=cost(3e9, 12e6),
         name=name,
-    )(at, x, sg, qkv, qkv)
-
-
-def give_body(at_ref, x_ref, q_ref, k_ref, v_ref, o_ref):
-    for j, ref in enumerate((q_ref, k_ref, v_ref)):
-        o_ref[:, j * 256 : (j + 1) * 256] = dot(x_ref[...], ref[...], TN)
-
-
-def keep_body(at_ref, x_ref, q_ref, k_ref, v_ref, r_ref, o_ref):
-    for j, ref in enumerate((q_ref, k_ref, v_ref)):
+    )(at, x, *(a for a, _ in sources))
+
+
+def keep_body(at_ref, x_ref, r_ref, *refs):
+    w_ref, f_ref = refs[6:]
+    for j in range(3):
         cols = slice(j * 256, (j + 1) * 256)
-        o_ref[:, cols] = dot(x_ref[...], ref[...], TN) + r_ref[:, cols]
-
-
-def local_part(at, x, loc, arrived, name):
-    mine = arrived is not None
-
-    def cols(first):
-        return pl.BlockSpec((TOK, 256), lambda i, s: (0, first + (s[0] if mine else 1 - s[0])))
-
-    rows = pl.BlockSpec((DM // 2, 768), lambda i, s: (i, 0))
-    return pl.pallas_call(
-        keep_body if mine else give_body,
+        w_ref[:, cols] = dot(x_ref[...], refs[j][...], TN) + r_ref[:, cols]
+        f_ref[:, cols] = dot(x_ref[...], refs[3 + j][...], TN).astype(BF16)
+
+
+def keep(at, x, arrived, sources):
+    cols = [pl.BlockSpec((TOK, 256), lambda i, s, f=f: (0, f + s[0])) for _, f in sources]
+    rows = pl.BlockSpec((DM // 4, 768), lambda i, s: (i, 0))
+    return pl.pallas_call(
+        keep_body,
         grid_spec=pltpu.PrefetchScalarGridSpec(
             num_scalar_prefetch=1,
-            grid=(2,),
-            in_specs=[pl.BlockSpec((TOK, DM // 2), lambda i, s: (0, i)), cols(0), cols(2), cols(4)]
-            + ([rows] if mine else []),
-            out_specs=rows,
+            grid=(4,),
+            in_specs=[pl.BlockSpec((TOK, DM // 4), lambda i, s: (0, i)), rows] + cols,
+            out_specs=[rows, rows],
         ),
-        out_shape=jax.ShapeDtypeStruct((DM, 768), F32),
-        compiler_params=params(24),
-        cost_estimate=cost(3e9, 12e6),
-        name=name,
-    )(at, x, loc, loc, loc, *([arrived] if mine else []))
+        out_shape=[jax.ShapeDtypeStruct((DM, 768), F32), jax.ShapeDtypeStruct((DM, 768), BF16)],
+        compiler_params=params(60),
+        cost_estimate=cost(40e9, 16e6),
+        name="keep",
+    )(at, x, arrived, *(a for a, _ in sources))
 
 
 def pick(at_ref, axis):
@@ -340,24 +330,42 @@
         so[...] = k[:, 1] + r[:, 1]
 
 
-def add4_body(kp, rp, kq, rq, o):
-    o[:, :, 0:384] = kp[...] + rp[...]
-    o[:, :, 384:768] = kq[...] + rq[...]
-
-
-def sum_body(v, o):
-    total = v[0]
-    for i in range(1, v.shape[0]):
-        total = total + v[i]
-    for i in range(o.shape[0]):
-        o[i] = total
-
-
-def place_body(v, o):
-    for i in range(8):
+def add4_body(at, kp, rp, kq, rq, kz, sz):
+    for o, first in ((kz, 9), (sz, 13)):
+        for i in range(4):
+            j = at[first + i]
+            o[i, :, 0:384] = kp[j] + rp[j]
+            o[i, :, 384:768] = kq[j] + rq[j]
+
+
+def halve_body(k, r, ko, so):
+    half = ko.shape[0]
+    ko[...] = k[0:half] + r[0:half]
+    so[...] = k[half:] + r[half:]
+
+
+def add_body(k, r, o):
+    o[...] = k[0] + r[0]
+
+
+def rows_body(at, a0, a1, a2, a3, o):
+    x = at[1]
+    for d, a in enumerate((a0, a1, a2, a3)):
+        o[(x + 4 - d) % 4] = a[...]
+
+
+def place_body(at, mine, other, o):
+    def put(core, a):
         for p in range(6):
-            at = (p % 3) * 512 + (i % 2) * 256 + (p // 3) * 128
-            o[i // 2 * 8 : i // 2 * 8 + 8, at : at + 128] = v[i, :, p * 128 : (p + 1) * 128]
+            first = (p % 3) * 512 + core * 256 + (p // 3) * 128
+            o[:, first : first + 128] = a[:, p * 128 : (p + 1) * 128]
+
+    for core in range(2):
+
+        @pl.when(at[0] == core)
+        def _(core=core):
+            put(core, mine)
+            put(1 - core, other)
 
 
 def exchange(value, axis, step):
@@ -369,32 +377,50 @@
     return lax.ppermute(value, (axis, "core"), pairs)
 
 
+def along_z(z, core, step):
+    up = (z ^ 1) if (core + step) % 2 == 0 else (((z + 1) ^ 1) + 7)
+    return up % 8
+
+
+def exchange_z(value, step):
+    pairs = []
+    for z in range(8):
+        for c in range(2):
+            partner = (z + 4) % 8 if step == 2 else along_z(z, c, step)
+            pairs.append((2 * z + c, 2 * partner + c))
+    return lax.ppermute(value, ("z", "core"), pairs)
+
+
 def shards(inputs, weights, out_grad):
     x = inputs[0]
     z_at, y_at, x_at, core = (lax.axis_index(a) for a in ("z", "y", "x", "core"))
     tm_at = z_at * 4 + y_at
     first = jnp.where(core == 0, 1, 3)
     second = 4 - first
+    one, two = (z_at ^ 1) % 8, (((z_at + 1) ^ 1) + 7) % 8
+    z_first, z_second = jnp.where(core == 0, one, two), jnp.where(core == 0, two, one)
+    z_both = jnp.where(core == 0, (((z_first + 1) ^ 1) + 7) % 8, z_first ^ 1)
     at = jnp.stack(
         [core]
         + [v for i in (x_at, y_at) for v in (i, i ^ first ^ second, i ^ first, i ^ second)]
+        + [v % 8 for i in (z_at, z_second, z_first, z_both) for v in (i, i + 4)]
     ).astype(jnp.int32)
     offset = (tm_at * TOK).astype(jnp.int32)[None]
     back = (tm_at >= 16).astype(jnp.int32)[None]
 
     qkv, sg, kv, qg, total = project(offset, x, weights, out_grad[0])
     slices = lax.all_to_all(total.reshape(32, 32, HD), ("z", "y"), 0, 0, tiled=True)
-    factors_out = factors(at, x, sg, qkv, False, F32, "factors_give")
     loc = local(qkv, sg, kv, qg)
-    local_out = local_part(at, x, loc, None, "local_give")
-    slices, factors_out, local_out = lax.optimization_barrier((slices, factors_out, local_out))
+    local_out = give(at, x, [(loc, 0), (loc, 2), (loc, 4)], "local_give")
+    slices, local_out = lax.optimization_barrier((slices, local_out))
+    local_in = lax.ppermute(local_out, "core", SWAP)
+
+    scanned = scan_states(back, slices)
+    scanned, sg, qkv, loc = lax.optimization_barrier((scanned, sg, qkv, loc))
+    states = lax.all_to_all(scanned, ("z", "y"), 0, 0, tiled=True)
+    factors_out = give(at, x, [(sg, 0), (qkv, 4), (qkv, 2)], "factors_give")
     factors_in = lax.ppermute(factors_out, "core", SWAP)
-    local_in = lax.ppermute(local_out, "core", SWAP)
-
-    scanned = scan_states(back, slices)
-    states = lax.all_to_all(scanned, ("z", "y"), 0, 0, tiled=True)
-    mine = factors(at, x, sg, qkv, True, BF16, "factors_keep")
-    both = local_part(at, x, loc, local_in, "local_keep")
+    both, mine = keep(at, x, local_in, [(loc, 0), (loc, 2), (loc, 4), (sg, 0), (qkv, 4), (qkv, 2)])
     states, mine, both = lax.optimization_barrier((states, mine, both))
 
     states = states.reshape(2, H, HD, HD)
@@ -413,11 +439,17 @@
     kp, sp, kq, sq = whole_call(add3_body, "add3", [(8, 8, 384)] * 4, kp, rp, kq, rq)
     rp = exchange(sp, "y", 1)
     rq = exchange(sq, "x", 1)
-    (part,) = whole_call(add4_body, "add4", [(8, 8, 768)], kp, rp, kq, rq)
-    part = lax.all_to_all(part, "z", 0, 0, tiled=True)
-    (mine,) = whole_call(sum_body, "sum_z", [(8, 8, 768)], part)
-    rows = lax.all_to_all(mine, ("x", "core"), 0, 0, tiled=True)
-    (proj_grad,) = whole_call(place_body, "place", [(32, 3 * D)], rows)
+    kz, sz = whole_call(add4_body, "add4", [(4, 8, 768)] * 2, at, kp, rp, kq, rq)
+    kz, sz = whole_call(halve_body, "add5", [(2, 8, 768)] * 2, kz, exchange_z(sz, 0))
+    kz, sz = whole_call(halve_body, "add6", [(1, 8, 768)] * 2, kz, exchange_z(sz, 1))
+    (own,) = whole_call(add_body, "add7", [(8, 768)], kz, exchange_z(sz, 2))
+    around = [own] + [
+        lax.ppermute(own, "x", [(i, (i + d) % 4) for i in range(4)]) for d in range(1, 4)
+    ]
+    (rows,) = whole_call(rows_body, "rows", [(4, 8, 768)], at, *around)
+    rows = rows.reshape(32, 768)
+    other = lax.ppermute(rows, "core", SWAP)
+    (proj_grad,) = whole_call(place_body, "place", [(32, 3 * D)], at, rows, other)
     return record_grad[None], proj_grad
 
 

time: 140 us -> 142 us (1.014)
  blocking collectives: 27.1 us -> 0 us
  starting transfers between devices: 32.8 us -> 51 us
  local copies, waits for them, and re-layouts: 13.2 us -> 0.62 us
  Pallas kernels: 44.2 us -> 56.4 us
  waiting for transfers between devices: 20.9 us -> 32.8 us
    all_to_all x2 -> x0, blocking collectives: 27.1 us -> none  [the longest x1 14.7 us: shards(): rows = lax.all_to_all(mine, ('x', 'core'), 0, 0, tiled=True)]
    ppermute x0 -> x7, starting transfers between devices: none -> 19.2 us  [the longest x1 9.97 us: shards(): other = lax.ppermute(rows, 'core', SWAP)]
    unnamed x32 -> x6, local copies, waits for them, and re-layouts: 13.1 us -> 0.01 us
    ppermute x0 -> x7, waiting for transfers between devices: none -> 12 us  [the longest x3 10.1 us: exchange_z(): return lax.ppermute(value, ('z', 'core'), pairs)]
    pallas_call x4 -> x3, Pallas kernels: 13 us -> 21.8 us  [the longest x2 12.8 us: give(): pl.pallas_call(give_body, grid_spec=pltpu.PrefetchScalarGridSpec(num_scal...]
    pallas_call x1, Pallas kernels: 5.82 us -> 8.61 us  [local(): pl.pallas_call(local_body, grid=(NB,), in_specs=[block(3 * D), block(D),...]
    pallas_call x6 -> x9, Pallas kernels: 1.56 us -> 3.23 us  [whole_call(): pl.pallas_call(body, in_specs=[smem if a.dtype == jnp.int32 else vmem for...]
  transfers between devices with their start and end apart: 13 -> 20, of which waited for: 9 -> 16; matrix products, arithmetic and copies ran while one was open for 0% -> 0% of each run, Pallas kernels for 20% -> 28%
where the time goes in v4:
time: 142 us
  Pallas kernels  56.4 us (40%)
  starting transfers between devices  51 us (36%)
  waiting for transfers between devices  32.8 us (23%)
    ppermute x8, waiting for transfers between devices, exchange(): return lax.ppermute(value, (axis, 'core'), pairs)  17.7 us
    pallas_call x2, Pallas kernels, give(): pl.pallas_call(give_body, grid_spec=pltpu.PrefetchScalarGridSpec(num_scal...  12.8 us
    all_to_all x1, starting transfers between devices, shards(): lax.all_to_all(total.reshape(32, 32, HD), ('z', 'y'), 0, 0, tiled=True)  12 us
    ppermute x3, waiting for transfers between devices, exchange_z(): return lax.ppermute(value, ('z', 'core'), pairs)  10.1 us
    ppermute x1, starting transfers between devices, shards(): other = lax.ppermute(rows, 'core', SWAP)  9.97 us
    pallas_call x1, Pallas kernels, project(): pl.pallas_call(project_body, grid_spec=pltpu.PrefetchScalarGridSpec(num_s...  9.18 us
    pallas_call x1, Pallas kernels, keep(): pl.pallas_call(keep_body, grid_spec=pltpu.PrefetchScalarGridSpec(num_scal...  9.02 us
    pallas_call x1, Pallas kernels, local(): pl.pallas_call(local_body, grid=(NB,), in_specs=[block(3 * D), block(D),...  8.61 us
  transfers between devices with their start and end apart: 20, of which 16 were waited for; matrix products, arithmetic and copies ran while one was open for 0% of the time, Pallas kernels for 28%

profile of v4, /device:TPU:1, one launch (start us, length us, event | category | flops | bytes accessed | tf_op | source)
XLA Modules:
  0.0 141.7 jit_solution(8371678870447340263)
XLA Ops:
  0.6 9.2 %project.1 = (bf16[1024,1536]{1,0:T(8,128)(2,1)}, bf16[1024,512]{1,0:T(8,128)(2,1)}, f32[4,4,128,128]{3,2,1,0:T(8,128)}, f32[4,4,128,128]{3,2,1,0:T(8,128)}, f32[2,4,128,128]{3,2,1,0:T(8,128)}) custom-call(s32[1]{0:T(128)} %bitcast.18.pos_ref, bf16[1024,1024]{1,0:T(8,128)(2,1)} %bitcast.30, bf16[1024,1536]{1,0:T(8,128)(2,1)} %w_ref.3, bf16[1024,512]{1,0:T(8,128)(2,1)} %bitcast.34), custom_call_target="tpu_custom_call" | custom-call | tf_op jit(solution)/shard_map/project/pallas_call | solution.py:68
  9.8 12.0 %all-to-all-start = ((f32[32,32,128]{2,1,0:T(8,128)}), f32[32,32,128]{2,1,0:T(8,128)S(1)}, u32[]{:S(2)}, u32[]{:S(2)}) async-start(f32[32,32,128]{2,1,0:T(8,128)} %bitcast.35), calls=%async_computation | async-start | bytes 1048576 | tf_op jit(solution)/shard_map/all_to_all | solution.py:412
  22.1 0.6 stack.71.at_ref.at
  22.7 8.6 %local.1.refs_0_.refs_1_.refs_2_.loc_ref = bf16[1024,1536]{1,0:T(8,128)(2,1)} custom-call(bf16[1024,1536]{1,0:T(8,128)(2,1)} %get-tuple-element.53.qkv_ref.refs_4_.refs_5_.refs_1_.refs_2_, bf16[1024,512]{1,0:T(8,128)(2,1)} %get-tuple-element.52.sg_ref.refs_3_.refs_0_, f32[4,4,128,128]{3,2,1,0:T(8,128)} %get-tuple-element.46.kv_ref, ...), custom_call_target="tpu_custom_call" | custom-call | flops 4000000000 | bytes 20000000 | tf_op jit(solution)/shard_map/local/pallas_call | solution.py:140
  31.3 6.4 %local_give.1 = f32[1024,768]{1,0:T(8,128)} custom-call(s32[17]{0:T(128)} %stack.71.at_ref.at, bf16[1024,1024]{1,0:T(8,128)(2,1)} %bitcast.31, bf16[1024,1536]{1,0:T(8,128)(2,1)} %local.1.refs_0_.refs_1_.refs_2_.loc_ref, bf16[1024,1536]{1,0:T(8,128)(2,1)} %local.1.refs_0_.refs_1_.refs_2_.loc_ref, bf16[1024,1536]{1,0:T(8,128)(2,1)} %local.1.refs_0_.refs_1_.refs_2_.loc_ref), custom_call_target="tpu_custom_call" | custom-call | flops 3000000000 | bytes 12000000 | tf_op jit(solution)/shard_map/local_give/pallas_call | solution.py:159
  37.7 0.5 all-to-all-done.v_ref
  38.1 2.4 %collective-permute-start = (f32[1024,768]{1,0:T(8,128)}, f32[1024,768]{1,0:T(8,128)}, u32[]{:S(2)}, u32[]{:S(2)}) collective-permute-start(f32[1024,768]{1,0:T(8,128)} %local_give.1), channel_id=1, source_target_pairs={{0,1},{1,0},{2,3},{3,2},{4,5},{5,4},{6,7},{7,6},{8,9},{9,8},{10,11... | collective-permute-start | bytes 9437192 | tf_op jit(solution)/shard_map/ppermute | solution.py:416
  40.5 1.1 scan_states.1
  41.6 7.6 %all-to-all-start.1 = ((f32[32,32,128]{2,1,0:T(8,128)}), f32[32,32,128]{2,1,0:T(8,128)S(1)}, u32[]{:S(2)}, u32[]{:S(2)}) async-start(f32[32,32,128]{2,1,0:T(8,128)} %scan_states.1), calls=%async_computation.1 | async-start | bytes 1048576 | tf_op jit(solution)/shard_map/all_to_all | solution.py:420
  49.2 6.4 %factors_give.1 = f32[1024,768]{1,0:T(8,128)} custom-call(s32[17]{0:T(128)} %stack.71.at_ref.at, bf16[1024,1024]{1,0:T(8,128)(2,1)} %bitcast.32, bf16[1024,512]{1,0:T(8,128)(2,1)} %get-tuple-element.52.sg_ref.refs_3_.refs_0_, bf16[1024,1536]{1,0:T(8,128)(2,1)} %get-tuple-element.53.qkv_ref.refs_4_.refs_5_.refs_1_.refs_2_, ...), custom_call_target="tpu_custom_call" | custom-call | flops 3000000000 | bytes 12000000 | tf_op jit(solution)/shard_map/factors_give/pallas_call | solution.py:159
  55.6 0.0 copy-start.2
  55.6 0.3 collective-permute-start.1
  55.9 0.0 collective-permute-done.r_ref
  55.9 9.0 %keep.1 = (f32[1024,768]{1,0:T(8,128)}, bf16[1024,768]{1,0:T(8,128)(2,1)}) custom-call(s32[17]{0:T(128)} %stack.71.at_ref.at, bf16[1024,1024]{1,0:T(8,128)(2,1)} %bitcast.33, f32[1024,768]{1,0:T(8,128)} %collective-permute-done.r_ref, bf16[1024,1536]{1,0:T(8,128)(2,1)} %local.1.refs_0_.refs_1_.refs_2_.loc_ref, ...), custom_call_target="tpu_custom_call" | custom-call | flops 40000000000 | bytes 16000000 | tf_op jit(solution)/shard_map/keep/pallas_call | solution.py:185
  64.9 1.1 all-to-all-done.1
  66.0 0.0 copy-start
  66.0 0.0 copy-start.1
  66.0 1.9 %collective-permute-start.2 = (f32[2,4,128,128]{3,2,1,0:T(8,128)S(1)}, f32[2,4,128,128]{3,2,1,0:T(8,128)S(1)}, u32[]{:S(2)}, u32[]{:S(2)}) collective-permute-start(f32[2,4,128,128]{3,2,1,0:T(8,128)S(1)} %bitcast.25), channel_id=1, source_target_pairs={{0,1},{1,0},{2,3},{3,2},{4,5},{5,4},{6,7},{7,6},{8,9},{9,8},{10,11... | collective-permute-start | bytes 1572872 | tf_op jit(solution)/shard_map/ppermute | solution.py:427
  67.9 0.0 collective-permute-done.1.b_hbm
  67.9 1.5 %collective-permute-done.2.sb_ref = f32[2,4,128,128]{3,2,1,0:T(8,128)S(1)} collective-permute-done((f32[2,4,128,128]{3,2,1,0:T(8,128)S(1)}, f32[2,4,128,128]{3,2,1,0:T(8,128)S(1)}, u32[]{:S(2)}, u32[]{:S(2)}) %collective-permute-start.2) | collective-permute-done | bytes 524320 | tf_op jit(solution)/shard_map/ppermute | solution.py:427
  69.4 0.0 copy-done.2
  69.4 4.5 %finish.1 = (f32[8,4,2,8,384]{4,3,2,1,0:T(8,128)S(1)}, f32[8,4,2,8,384]{4,3,2,1,0:T(8,128)S(1)}, f32[8,2,4,8,384]{4,3,2,1,0:T(8,128)S(1)}, f32[8,2,4,8,384]{4,3,2,1,0:T(8,128)S(1)}) custom-call(s32[17]{0:T(128)S(1)} %copy-done.2, f32[1024,768]{1,0:T(8,128)} %get-tuple-element.56.w_hbm, bf16[1024,768]{1,0:T(8,128)(2,1)} %get-tuple-element.57.a_hbm, ...), custom_call_target="tpu_custom_call" | custom-call | flops 1000000000 | bytes 12000000 | tf_op jit(solution)/shard_map/finish/pallas_call | solution.py:244
  73.9 2.6 %collective-permute-start.3 = (f32[8,4,2,8,384]{4,3,2,1,0:T(8,128)S(1)}, f32[8,4,2,8,384]{4,3,2,1,0:T(8,128)S(1)}, u32[]{:S(2)}, u32[]{:S(2)}) collective-permute-start(f32[8,4,2,8,384]{4,3,2,1,0:T(8,128)S(1)} %get-tuple-element.59), channel_id=1, source_target_pairs={{0,2},{1,7},{2,0},{3,5},{4,6},{5,3},{6,4},{7,1},{8,10},{9,15},{10,... | collective-permute-start | bytes 2359304 | tf_op jit(solution)/shard_map/ppermute | solution.py:377
  76.4 1.9 %collective-permute-start.4 = (f32[8,2,4,8,384]{4,3,2,1,0:T(8,128)S(1)}, f32[8,2,4,8,384]{4,3,2,1,0:T(8,128)S(1)}, u32[]{:S(2)}, u32[]{:S(2)}) collective-permute-start(f32[8,2,4,8,384]{4,3,2,1,0:T(8,128)S(1)} %get-tuple-element.60), channel_id=1, source_target_pairs={{0,8},{1,25},{8,0},{9,17},{16,24},{17,9},{24,16},{25,1},{2,10},{3,... | collective-permute-start | bytes 2359304 | tf_op jit(solution)/shard_map/ppermute | solution.py:377
  78.3 0.0 copy-done
  78.3 0.0 copy-done.1
  78.3 8.1 %inputs_grad.1 = bf16[1024,1024]{1,0:T(8,128)(2,1)} custom-call(bf16[1024,1536]{1,0:T(8,128)(2,1)S(1)} %copy-done, bf16[1024,1536]{1,0:T(8,128)(2,1)} %get-tuple-element.53.qkv_ref.refs_4_.refs_5_.refs_1_.refs_2_, bf16[1024,512]{1,0:T(8,128)(2,1)S(1)} %copy-done.1, f32[2,4,128,128]{3,2,1,0:T(8,128)S(1)} %bitcast.27, bf16[1024,1536]{1,0:T(8,128)(2,1)} %w_ref.3), custom_call_target="tpu_custom_call" | custom-call | flops 5000000000 | bytes 14000000 | tf_op jit(solution)/shard_map/inputs_grad/pallas_call | solution.py:279
  86.4 0.0 collective-permute-done.3.rx
  86.4 2.1 %collective-permute-done.4.ry = f32[8,2,4,8,384]{4,3,2,1,0:T(8,128)S(1)} collective-permute-done((f32[8,2,4,8,384]{4,3,2,1,0:T(8,128)S(1)}, f32[8,2,4,8,384]{4,3,2,1,0:T(8,128)S(1)}, u32[]{:S(2)}, u32[]{:S(2)}) %collective-permute-start.4) | collective-permute-done | bytes 786464 | tf_op jit(solution)/shard_map/ppermute | solution.py:377
  88.5 0.2 add1.1
  88.6 0.1 collective-permute-start.5
  88.7 0.3 collective-permute-start.6
  89.0 6.6 %collective-permute-done.5.rx = f32[8,4,8,384]{3,2,1,0:T(8,128)S(1)} collective-permute-done((f32[8,4,8,384]{3,2,1,0:T(8,128)S(1)}, f32[8,4,8,384]{3,2,1,0:T(8,128)S(1)}, u32[]{:S(2)}, u32[]{:S(2)}) %collective-permute-start.5) | collective-permute-done | bytes 393248 | tf_op jit(solution)/shard_map/ppermute | solution.py:377
  95.6 0.3 collective-permute-done.6.ry
  95.9 0.6 add2.1
  96.6 1.9 %collective-permute-start.7 = (f32[8,2,8,384]{3,2,1,0:T(8,128)S(1)}, f32[8,2,8,384]{3,2,1,0:T(8,128)S(1)}, u32[]{:S(2)}, u32[]{:S(2)}) collective-permute-start(f32[8,2,8,384]{3,2,1,0:T(8,128)S(1)} %get-tuple-element.71), channel_id=1, source_target_pairs={{0,8},{1,25},{8,0},{9,17},{16,24},{17,9},{24,16},{25,1},{2,10},{3,... | collective-permute-start | bytes 589832 | tf_op jit(solution)/shard_map/ppermute | solution.py:377
  98.5 0.5 collective-permute-start.8
  99.0 3.4 %collective-permute-done.7.rp = f32[8,2,8,384]{3,2,1,0:T(8,128)S(1)} collective-permute-done((f32[8,2,8,384]{3,2,1,0:T(8,128)S(1)}, f32[8,2,8,384]{3,2,1,0:T(8,128)S(1)}, u32[]{:S(2)}, u32[]{:S(2)}) %collective-permute-start.7) | collective-permute-done | bytes 196640 | tf_op jit(solution)/shard_map/ppermute | solution.py:377
  102.4 1.9 %collective-permute-done.8.rq = f32[8,2,8,384]{3,2,1,0:T(8,128)S(1)} collective-permute-done((f32[8,2,8,384]{3,2,1,0:T(8,128)S(1)}, f32[8,2,8,384]{3,2,1,0:T(8,128)S(1)}, u32[]{:S(2)}, u32[]{:S(2)}) %collective-permute-start.8) | collective-permute-done | bytes 196640 | tf_op jit(solution)/shard_map/ppermute | solution.py:377
  104.3 0.4 collective-permute-start.10
  104.6 0.0 collective-permute-start.9
  104.6 3.2 %collective-permute-done.10.rq = f32[8,8,384]{2,1,0:T(8,128)S(1)} collective-permute-done((f32[8,8,384]{2,1,0:T(8,128)S(1)}, f32[8,8,384]{2,1,0:T(8,128)S(1)}, u32[]{:S(2)}, u32[]{:S(2)}) %collective-permute-start.10) | collective-permute-done | bytes 98336 | tf_op jit(solution)/shard_map/ppermute | solution.py:377
  107.8 0.3 collective-permute-done.9.rp
  108.1 0.6 add4.1
  108.7 1.0 collective-permute-start.11
  109.7 3.8 %collective-permute-done.11.r = f32[4,8,768]{2,1,0:T(8,128)S(1)} collective-permute-done((f32[4,8,768]{2,1,0:T(8,128)S(1)}, f32[4,8,768]{2,1,0:T(8,128)S(1)}, u32[]{:S(2)}, u32[]{:S(2)}) %collective-permute-start.11) | collective-permute-done | bytes 98336 | tf_op jit(solution)/shard_map/ppermute | solution.py:391
  113.5 0.1 collective-permute-start.12
  113.6 3.5 %collective-permute-done.12.r = f32[2,8,768]{2,1,0:T(8,128)S(1)} collective-permute-done((f32[2,8,768]{2,1,0:T(8,128)S(1)}, f32[2,8,768]{2,1,0:T(8,128)S(1)}, u32[]{:S(2)}, u32[]{:S(2)}) %collective-permute-start.12) | collective-permute-done | bytes 49184 | tf_op jit(solution)/shard_map/ppermute | solution.py:391
  117.0 3.9 %collective-permute-start.13 = (f32[1,8,768]{2,1,0:T(8,128)S(1)}, f32[1,8,768]{2,1,0:T(8,128)S(1)}, u32[]{:S(2)}, u32[]{:S(2)}) collective-permute-start(f32[1,8,768]{2,1,0:T(8,128)S(1)} %get-tuple-element.83), channel_id=1, source_target_pairs={{0,128},{1,129},{32,160},{33,161},{64,192},{65,193},{96,224},{97,2... | collective-permute-start | bytes 73736 | tf_op jit(solution)/shard_map/ppermute | solution.py:391
  120.9 2.9 %collective-permute-done.13.r = f32[1,8,768]{2,1,0:T(8,128)S(1)} collective-permute-done((f32[1,8,768]{2,1,0:T(8,128)S(1)}, f32[1,8,768]{2,1,0:T(8,128)S(1)}, u32[]{:S(2)}, u32[]{:S(2)}) %collective-permute-start.13) | collective-permute-done | bytes 24608 | tf_op jit(solution)/shard_map/ppermute | solution.py:391
  123.8 0.9 collective-permute-start.14
  124.7 1.4 collective-permute-start.15
  126.1 2.0 %collective-permute-start.16 = (f32[8,768]{1,0:T(8,128)S(1)}, f32[8,768]{1,0:T(8,128)S(1)}, u32[]{:S(2)}, u32[]{:S(2)}) collective-permute-start(f32[8,768]{1,0:T(8,128)S(1)} %add7.1.a0), channel_id=1, source_target_pairs={{0,6},{2,0},{4,2},{6,4},{1,7},{3,1},{5,3},{7,5},{8,14},{10,8},{12,... | collective-permute-start | bytes 73736 | tf_op jit(solution)/shard_map/ppermute | solution.py:447
  128.1 0.0 collective-permute-done.14.a1
  128.1 0.8 collective-permute-done.15.a2
  128.9 0.2 collective-permute-done.16.a3
  129.0 0.6 rows.1
  129.6 10.0 %collective-permute-start.17 = (f32[32,768]{1,0:T(8,128)S(1)}, f32[32,768]{1,0:T(8,128)S(1)}, u32[]{:S(2)}, u32[]{:S(2)}) collective-permute-start(f32[32,768]{1,0:T(8,128)S(1)} %bitcast.28), channel_id=1, source_target_pairs={{0,1},{1,0},{2,3},{3,2},{4,5},{5,4},{6,7},{7,6},{8,9},{9,8},{10,11... | collective-permute-start | bytes 294920 | tf_op jit(solution)/shard_map/ppermute | solution.py:451
  139.5 0.9 collective-permute-done.17.other
  140.5 1.2 place.1
  (4 shorter events, 0.1 us)
Async XLA Ops:
  9.8 28.3 %all-to-all-start = ((f32[32,32,128]{2,1,0:T(8,128)}), f32[32,32,128]{2,1,0:T(8,128)S(1)}, u32[]{:S(2)}, u32[]{:S(2)}) async-start(f32[32,32,128]{2,1,0:T(8,128)} %bitcast.35), calls=%async_computation | async-start | bytes 1048576 | tf_op jit(solution)/shard_map/all_to_all | solution.py:412
  38.1 17.8 %collective-permute-start = (f32[1024,768]{1,0:T(8,128)}, f32[1024,768]{1,0:T(8,128)}, u32[]{:S(2)}, u32[]{:S(2)}) collective-permute-start(f32[1024,768]{1,0:T(8,128)} %local_give.1), channel_id=1, source_target_pairs={{0,1},{1,0},{2,3},{3,2},{4,5},{5,4},{6,7},{7,6},{8,9},{9,8},{10,11... | collective-permute-start | bytes 9437192 | tf_op jit(solution)/shard_map/ppermute | solution.py:416
  41.6 24.4 %all-to-all-start.1 = ((f32[32,32,128]{2,1,0:T(8,128)}), f32[32,32,128]{2,1,0:T(8,128)S(1)}, u32[]{:S(2)}, u32[]{:S(2)}) async-start(f32[32,32,128]{2,1,0:T(8,128)} %scan_states.1), calls=%async_computation.1 | async-start | bytes 1048576 | tf_op jit(solution)/shard_map/all_to_all | solution.py:420
  55.6 13.8 %copy-start.2 = (s32[17]{0:T(128)S(1)}, s32[17]{0:T(128)}, u32[]{:S(2)}) copy-start(s32[17]{0:T(128)} %stack.71.at_ref.at) | copy-start | bytes 208
  55.6 12.3 %collective-permute-start.1 = (f32[1024,768]{1,0:T(8,128)}, f32[1024,768]{1,0:T(8,128)}, u32[]{:S(2)}, u32[]{:S(2)}) collective-permute-start(f32[1024,768]{1,0:T(8,128)} %factors_give.1), channel_id=1, source_target_pairs={{0,1},{1,0},{2,3},{3,2},{4,5},{5,4},{6,7},{7,6},{8,9},{9,8},{10,11... | collective-permute-start | bytes 9437192 | tf_op jit(solution)/shard_map/ppermute | solution.py:422
  66.0 12.3 %copy-start = (bf16[1024,1536]{1,0:T(8,128)(2,1)S(1)}, bf16[1024,1536]{1,0:T(8,128)(2,1)}, u32[]{:S(2)}) copy-start(bf16[1024,1536]{1,0:T(8,128)(2,1)} %local.1.refs_0_.refs_1_.refs_2_.loc_ref) | copy-start | bytes 9437188
  66.0 12.3 %copy-start.1 = (bf16[1024,512]{1,0:T(8,128)(2,1)S(1)}, bf16[1024,512]{1,0:T(8,128)(2,1)}, u32[]{:S(2)}) copy-start(bf16[1024,512]{1,0:T(8,128)(2,1)} %get-tuple-element.52.sg_ref.refs_3_.refs_0_) | copy-start | bytes 3145732
  66.0 3.4 %collective-permute-start.2 = (f32[2,4,128,128]{3,2,1,0:T(8,128)S(1)}, f32[2,4,128,128]{3,2,1,0:T(8,128)S(1)}, u32[]{:S(2)}, u32[]{:S(2)}) collective-permute-start(f32[2,4,128,128]{3,2,1,0:T(8,128)S(1)} %bitcast.25), channel_id=1, source_target_pairs={{0,1},{1,0},{2,3},{3,2},{4,5},{5,4},{6,7},{7,6},{8,9},{9,8},{10,11... | collective-permute-start | bytes 1572872 | tf_op jit(solution)/shard_map/ppermute | solution.py:427
  73.9 12.5 %collective-permute-start.3 = (f32[8,4,2,8,384]{4,3,2,1,0:T(8,128)S(1)}, f32[8,4,2,8,384]{4,3,2,1,0:T(8,128)S(1)}, u32[]{:S(2)}, u32[]{:S(2)}) collective-permute-start(f32[8,4,2,8,384]{4,3,2,1,0:T(8,128)S(1)} %get-tuple-element.59), channel_id=1, source_target_pairs={{0,2},{1,7},{2,0},{3,5},{4,6},{5,3},{6,4},{7,1},{8,10},{9,15},{10,... | collective-permute-start | bytes 2359304 | tf_op jit(solution)/shard_map/ppermute | solution.py:377
  76.4 12.1 %collective-permute-start.4 = (f32[8,2,4,8,384]{4,3,2,1,0:T(8,128)S(1)}, f32[8,2,4,8,384]{4,3,2,1,0:T(8,128)S(1)}, u32[]{:S(2)}, u32[]{:S(2)}) collective-permute-start(f32[8,2,4,8,384]{4,3,2,1,0:T(8,128)S(1)} %get-tuple-element.60), channel_id=1, source_target_pairs={{0,8},{1,25},{8,0},{9,17},{16,24},{17,9},{24,16},{25,1},{2,10},{3,... | collective-permute-start | bytes 2359304 | tf_op jit(solution)/shard_map/ppermute | solution.py:377
  88.6 7.0 %collective-permute-start.5 = (f32[8,4,8,384]{3,2,1,0:T(8,128)S(1)}, f32[8,4,8,384]{3,2,1,0:T(8,128)S(1)}, u32[]{:S(2)}, u32[]{:S(2)}) collective-permute-start(f32[8,4,8,384]{3,2,1,0:T(8,128)S(1)} %get-tuple-element.67), channel_id=1, source_target_pairs={{0,6},{1,3},{2,4},{3,1},{4,2},{5,7},{6,0},{7,5},{8,14},{9,11},{10,... | collective-permute-start | bytes 1179656 | tf_op jit(solution)/shard_map/ppermute | solution.py:377
  88.7 7.2 %collective-permute-start.6 = (f32[8,4,8,384]{3,2,1,0:T(8,128)S(1)}, f32[8,4,8,384]{3,2,1,0:T(8,128)S(1)}, u32[]{:S(2)}, u32[]{:S(2)}) collective-permute-start(f32[8,4,8,384]{3,2,1,0:T(8,128)S(1)} %get-tuple-element.69), channel_id=1, source_target_pairs={{0,24},{1,9},{8,16},{9,1},{16,8},{17,25},{24,0},{25,17},{2,26},{3,... | collective-permute-start | bytes 1179656 | tf_op jit(solution)/shard_map/ppermute | solution.py:377
  96.6 5.8 %collective-permute-start.7 = (f32[8,2,8,384]{3,2,1,0:T(8,128)S(1)}, f32[8,2,8,384]{3,2,1,0:T(8,128)S(1)}, u32[]{:S(2)}, u32[]{:S(2)}) collective-permute-start(f32[8,2,8,384]{3,2,1,0:T(8,128)S(1)} %get-tuple-element.71), channel_id=1, source_target_pairs={{0,8},{1,25},{8,0},{9,17},{16,24},{17,9},{24,16},{25,1},{2,10},{3,... | collective-permute-start | bytes 589832 | tf_op jit(solution)/shard_map/ppermute | solution.py:377
  98.5 5.7 %collective-permute-start.8 = (f32[8,2,8,384]{3,2,1,0:T(8,128)S(1)}, f32[8,2,8,384]{3,2,1,0:T(8,128)S(1)}, u32[]{:S(2)}, u32[]{:S(2)}) collective-permute-start(f32[8,2,8,384]{3,2,1,0:T(8,128)S(1)} %get-tuple-element.73), channel_id=1, source_target_pairs={{0,2},{1,7},{2,0},{3,5},{4,6},{5,3},{6,4},{7,1},{8,10},{9,15},{10,... | collective-permute-start | bytes 589832 | tf_op jit(solution)/shard_map/ppermute | solution.py:377
  104.3 3.6 %collective-permute-start.10 = (f32[8,8,384]{2,1,0:T(8,128)S(1)}, f32[8,8,384]{2,1,0:T(8,128)S(1)}, u32[]{:S(2)}, u32[]{:S(2)}) collective-permute-start(f32[8,8,384]{2,1,0:T(8,128)S(1)} %get-tuple-element.77), channel_id=1, source_target_pairs={{0,6},{1,3},{2,4},{3,1},{4,2},{5,7},{6,0},{7,5},{8,14},{9,11},{10,... | collective-permute-start | bytes 294920 | tf_op jit(solution)/shard_map/ppermute | solution.py:377
  104.6 3.5 %collective-permute-start.9 = (f32[8,8,384]{2,1,0:T(8,128)S(1)}, f32[8,8,384]{2,1,0:T(8,128)S(1)}, u32[]{:S(2)}, u32[]{:S(2)}) collective-permute-start(f32[8,8,384]{2,1,0:T(8,128)S(1)} %get-tuple-element.75), channel_id=1, source_target_pairs={{0,24},{1,9},{8,16},{9,1},{16,8},{17,25},{24,0},{25,17},{2,26},{3,... | collective-permute-start | bytes 294920 | tf_op jit(solution)/shard_map/ppermute | solution.py:377
  108.7 4.8 %collective-permute-start.11 = (f32[4,8,768]{2,1,0:T(8,128)S(1)}, f32[4,8,768]{2,1,0:T(8,128)S(1)}, u32[]{:S(2)}, u32[]{:S(2)}) collective-permute-start(f32[4,8,768]{2,1,0:T(8,128)S(1)} %get-tuple-element.79), channel_id=1, source_target_pairs={{0,32},{1,225},{32,0},{33,65},{64,96},{65,33},{96,64},{97,129},{12... | collective-permute-start | bytes 294920 | tf_op jit(solution)/shard_map/ppermute | solution.py:391
  113.5 3.6 %collective-permute-start.12 = (f32[2,8,768]{2,1,0:T(8,128)S(1)}, f32[2,8,768]{2,1,0:T(8,128)S(1)}, u32[]{:S(2)}, u32[]{:S(2)}) collective-permute-start(f32[2,8,768]{2,1,0:T(8,128)S(1)} %get-tuple-element.81), channel_id=1, source_target_pairs={{0,224},{1,33},{32,64},{33,1},{64,32},{65,97},{96,128},{97,65},{12... | collective-permute-start | bytes 147464 | tf_op jit(solution)/shard_map/ppermute | solution.py:391
  117.0 6.8 %collective-permute-start.13 = (f32[1,8,768]{2,1,0:T(8,128)S(1)}, f32[1,8,768]{2,1,0:T(8,128)S(1)}, u32[]{:S(2)}, u32[]{:S(2)}) collective-permute-start(f32[1,8,768]{2,1,0:T(8,128)S(1)} %get-tuple-element.83), channel_id=1, source_target_pairs={{0,128},{1,129},{32,160},{33,161},{64,192},{65,193},{96,224},{97,2... | collective-permute-start | bytes 73736 | tf_op jit(solution)/shard_map/ppermute | solution.py:391
  123.8 4.2 %collective-permute-start.14 = (f32[8,768]{1,0:T(8,128)S(1)}, f32[8,768]{1,0:T(8,128)S(1)}, u32[]{:S(2)}, u32[]{:S(2)}) collective-permute-start(f32[8,768]{1,0:T(8,128)S(1)} %add7.1.a0), channel_id=1, source_target_pairs={{0,2},{2,4},{4,6},{6,0},{1,3},{3,5},{5,7},{7,1},{8,10},{10,12},{12... | collective-permute-start | bytes 73736 | tf_op jit(solution)/shard_map/ppermute | solution.py:447
  124.7 4.2 %collective-permute-start.15 = (f32[8,768]{1,0:T(8,128)S(1)}, f32[8,768]{1,0:T(8,128)S(1)}, u32[]{:S(2)}, u32[]{:S(2)}) collective-permute-start(f32[8,768]{1,0:T(8,128)S(1)} %add7.1.a0), channel_id=1, source_target_pairs={{0,4},{2,6},{4,0},{6,2},{1,5},{3,7},{5,1},{7,3},{8,12},{10,14},{12... | collective-permute-start | bytes 73736 | tf_op jit(solution)/shard_map/ppermute | solution.py:447
  126.1 2.9 %collective-permute-start.16 = (f32[8,768]{1,0:T(8,128)S(1)}, f32[8,768]{1,0:T(8,128)S(1)}, u32[]{:S(2)}, u32[]{:S(2)}) collective-permute-start(f32[8,768]{1,0:T(8,128)S(1)} %add7.1.a0), channel_id=1, source_target_pairs={{0,6},{2,0},{4,2},{6,4},{1,7},{3,1},{5,3},{7,5},{8,14},{10,8},{12,... | collective-permute-start | bytes 73736 | tf_op jit(solution)/shard_map/ppermute | solution.py:447
  129.6 10.9 %collective-permute-start.17 = (f32[32,768]{1,0:T(8,128)S(1)}, f32[32,768]{1,0:T(8,128)S(1)}, u32[]{:S(2)}, u32[]{:S(2)}) collective-permute-start(f32[32,768]{1,0:T(8,128)S(1)} %bitcast.28), channel_id=1, source_target_pairs={{0,1},{1,0},{2,3},{3,2},{4,5},{5,4},{6,7},{7,6},{8,9},{9,8},{10,11... | collective-permute-start | bytes 294920 | tf_op jit(solution)/shard_map/ppermute | solution.py:451

commit v5 on v3

--- a/solution.py
+++ b/solution.py
@@ -112,99 +112,96 @@
     )(back, v)
 
 
-def local_body(qkv_ref, sg_ref, kv_ref, qg_ref, o_ref):
+def local_body(at_ref, qkv_ref, sg_ref, kv_ref, qg_ref, x_ref, loc_ref, give_ref, from_ref):
     n = pl.program_id(0)
-    keep = lax.broadcasted_iota(jnp.int32, (CH, CH), 0) >= lax.broadcasted_iota(jnp.int32, (CH, CH), 1)
-    for h in range(H):
-        q, k, v = (qkv_ref[:, head(p, h)] for p in range(3))
-        g = sg_ref[:, pl.ds(h * HD, HD)]
-        before = jnp.zeros((HD, HD), F32)
-        after = jnp.zeros((HD, HD), F32)
-        for m in range(NB):
-            before = before + jnp.where(m < n, kv_ref[m, h], 0.0)
-            after = after + jnp.where(m > n, qg_ref[m, h], 0.0)
-        before = before.astype(BF16)
-        after = after.astype(BF16)
-        mvg = jnp.where(keep, dot(g, v, NT), 0.0).astype(BF16)
-        mqk = jnp.where(keep, dot(q, k, NT), 0.0).astype(BF16)
-        dq = dot(mvg, k, NN) + dot(g, before, NT)
-        dk = dot(mvg, q, TN) + dot(v, after, NT)
-        dv = dot(mqk, g, TN) + dot(k, after, NN)
-        for p, d in enumerate((dq, dk, dv)):
-            o_ref[:, head(p, h)] = d.astype(BF16)
-
-
-def local(qkv, sg, kv, qg):
-    block = lambda cols: pl.BlockSpec((CH, cols), lambda n: (n, 0))
-    sums = pl.BlockSpec((NB, H, HD, HD), lambda n: (0, 0, 0, 0))
+    theirs = pl.multiple_of((1 - at_ref[0]) * 256, 256)
+
+    @pl.when(n < NB)
+    def _():
+        keep = lax.broadcasted_iota(jnp.int32, (CH, CH), 0) >= lax.broadcasted_iota(jnp.int32, (CH, CH), 1)
+        for h in range(H):
+            q, k, v = (qkv_ref[:, head(p, h)] for p in range(3))
+            g = sg_ref[:, pl.ds(h * HD, HD)]
+            before = jnp.zeros((HD, HD), F32)
+            after = jnp.zeros((HD, HD), F32)
+            for m in range(NB):
+                before = before + jnp.where(m < n, kv_ref[m, h], 0.0)
+                after = after + jnp.where(m > n, qg_ref[m, h], 0.0)
+            before = before.astype(BF16)
+            after = after.astype(BF16)
+            mvg = jnp.where(keep, dot(g, v, NT), 0.0).astype(BF16)
+            mqk = jnp.where(keep, dot(q, k, NT), 0.0).astype(BF16)
+            dq = dot(mvg, k, NN) + dot(g, before, NT)
+            dk = dot(mvg, q, TN) + dot(v, after, NT)
+            dv = dot(mqk, g, TN) + dot(k, after, NN)
+            for p, d in enumerate((dq, dk, dv)):
+                loc_ref[:, head(p, h)] = d.astype(BF16)
+        rows = pl.ds(pl.multiple_of(n * CH, CH), CH)
+        for p in range(3):
+            from_ref[rows, p * 256 : (p + 1) * 256] = loc_ref[:, pl.ds(p * D + theirs, 256)]
+        from_ref[rows, 768:1024] = sg_ref[:, pl.ds(theirs, 256)]
+        from_ref[rows, 1024:1280] = qkv_ref[:, pl.ds(2 * D + theirs, 256)]
+        from_ref[rows, 1280:1536] = qkv_ref[:, pl.ds(D + theirs, 256)]
+
+    @pl.when(n >= NB)
+    def _():
+        give_ref[...] = dot(x_ref[...], from_ref[...], TN)
+
+
+def local(at, qkv, sg, kv, qg, x):
+    first = lambda n: jnp.minimum(n, NB - 1)
+    last = lambda n: jnp.maximum(n - NB, 0)
+    block = lambda cols: pl.BlockSpec((CH, cols), lambda n, s: (first(n), 0))
+    sums = pl.BlockSpec((NB, H, HD, HD), lambda n, s: (0, 0, 0, 0))
     return pl.pallas_call(
         local_body,
-        grid=(NB,),
-        in_specs=[block(3 * D), block(D), sums, sums],
-        out_specs=block(3 * D),
-        out_shape=jax.ShapeDtypeStruct((TOK, 3 * D), BF16),
-        compiler_params=params(20),
-        cost_estimate=cost(4e9, 20e6),
-        name="local",
-    )(qkv, sg, kv, qg)
-
-
-def factors_body(at_ref, x_ref, g_ref, k_ref, v_ref, o_ref):
-    for j, ref in enumerate((g_ref, v_ref, k_ref)):
-        o_ref[:, j * 256 : (j + 1) * 256] = dot(x_ref[...], ref[...], TN).astype(o_ref.dtype)
-
-
-def factors(at, x, sg, qkv, mine, kind, name):
-    def cols(first):
-        return pl.BlockSpec((TOK, 256), lambda i, s: (0, first + (s[0] if mine else 1 - s[0])))
-
-    return pl.pallas_call(
-        factors_body,
         grid_spec=pltpu.PrefetchScalarGridSpec(
             num_scalar_prefetch=1,
-            grid=(2,),
-            in_specs=[pl.BlockSpec((TOK, DM // 2), lambda i, s: (0, i)), cols(0), cols(2), cols(4)],
-            out_specs=pl.BlockSpec((DM // 2, 768), lambda i, s: (i, 0)),
+            grid=(2 * NB,),
+            in_specs=[
+                block(3 * D),
+                block(D),
+                sums,
+                sums,
+                pl.BlockSpec((TOK, DM // 4), lambda n, s: (0, last(n))),
+            ],
+            out_specs=[block(3 * D), pl.BlockSpec((DM // 4, 3 * D), lambda n, s: (last(n), 0))],
+            scratch_shapes=[pltpu.VMEM((TOK, 3 * D), BF16)],
         ),
-        out_shape=jax.ShapeDtypeStruct((DM, 768), kind),
-        compiler_params=params(24),
-        cost_estimate=cost(3e9, 12e6),
-        name=name,
-    )(at, x, sg, qkv, qkv)
-
-
-def give_body(at_ref, x_ref, q_ref, k_ref, v_ref, o_ref):
-    for j, ref in enumerate((q_ref, k_ref, v_ref)):
-        o_ref[:, j * 256 : (j + 1) * 256] = dot(x_ref[...], ref[...], TN)
-
-
-def keep_body(at_ref, x_ref, q_ref, k_ref, v_ref, r_ref, o_ref):
-    for j, ref in enumerate((q_ref, k_ref, v_ref)):
+        out_shape=[
+            jax.ShapeDtypeStruct((TOK, 3 * D), BF16),
+            jax.ShapeDtypeStruct((DM, 3 * D), F32),
+        ],
+        compiler_params=params(60),
+        cost_estimate=cost(8e9, 24e6),
+        name="local",
+    )(at, qkv, sg, kv, qg, x)
+
+
+def keep_body(at_ref, x_ref, r_ref, *refs):
+    w_ref, f_ref = refs[6:]
+    for j in range(3):
         cols = slice(j * 256, (j + 1) * 256)
-        o_ref[:, cols] = dot(x_ref[...], ref[...], TN) + r_ref[:, cols]
-
-
-def local_part(at, x, loc, arrived, name):
-    mine = arrived is not None
-
-    def cols(first):
-        return pl.BlockSpec((TOK, 256), lambda i, s: (0, first + (s[0] if mine else 1 - s[0])))
-
-    rows = pl.BlockSpec((DM // 2, 768), lambda i, s: (i, 0))
-    return pl.pallas_call(
-        keep_body if mine else give_body,
+        w_ref[:, cols] = dot(x_ref[...], refs[j][...], TN) + r_ref[:, cols]
+        f_ref[:, cols] = dot(x_ref[...], refs[3 + j][...], TN).astype(BF16)
+
+
+def keep(at, x, arrived, sources):
+    cols = [pl.BlockSpec((TOK, 256), lambda i, s, f=f: (0, f + s[0])) for _, f in sources]
+    rows = pl.BlockSpec((DM // 4, 768), lambda i, s: (i, 0))
+    return pl.pallas_call(
+        keep_body,
         grid_spec=pltpu.PrefetchScalarGridSpec(
             num_scalar_prefetch=1,
-            grid=(2,),
-            in_specs=[pl.BlockSpec((TOK, DM // 2), lambda i, s: (0, i)), cols(0), cols(2), cols(4)]
-            + ([rows] if mine else []),
-            out_specs=rows,
+            grid=(4,),
+            in_specs=[pl.BlockSpec((TOK, DM // 4), lambda i, s: (0, i)), rows] + cols,
+            out_specs=[rows, rows],
         ),
-        out_shape=jax.ShapeDtypeStruct((DM, 768), F32),
-        compiler_params=params(24),
-        cost_estimate=cost(3e9, 12e6),
-        name=name,
-    )(at, x, loc, loc, loc, *([arrived] if mine else []))
+        out_shape=[jax.ShapeDtypeStruct((DM, 768), F32), jax.ShapeDtypeStruct((DM, 768), BF16)],
+        compiler_params=params(60),
+        cost_estimate=cost(5e9, 16e6),
+        name="keep",
+    )(at, x, arrived, *(a for a, _ in sources))
 
 
 def pick(at_ref, axis):
@@ -221,7 +218,7 @@
             (
                 pltpu.make_async_copy(w_hbm.at[:, cols], w_ref.at[j], sems.at[0, j]),
                 pltpu.make_async_copy(a_hbm.at[:, cols], a_ref.at[j], sems.at[1, j]),
-                pltpu.make_async_copy(b_hbm.at[:, cols], b_ref.at[j], sems.at[2, j]),
+                pltpu.make_async_copy(b_hbm.at[:, pl.ds(768 + j * 256, 256)], b_ref.at[j], sems.at[2, j]),
             )
         )
     for pair in copies:
@@ -319,25 +316,22 @@
     )(*args)
 
 
-def add1_body(kx, rx, ky, ry, kx2, sx2, ky2, sy2):
-    kx2[...] = kx[:, :, 0] + rx[:, :, 0]
-    sx2[...] = kx[:, :, 1] + rx[:, :, 1]
-    ky2[...] = ky[:, 0] + ry[:, 0]
-    sy2[...] = ky[:, 1] + ry[:, 1]
-
-
-def add2_body(at, kx, rx, ky, ry, kp, sp, kq, sq):
-    for axis, k, r, ko, so in ((1, kx, rx, kp, sp), (0, ky, ry, kq, sq)):
-        kept, sent = pick(at, axis)
-        for i in range(2):
-            ko[:, i] = k[:, kept[i]] + r[:, kept[i]]
-            so[:, i] = k[:, sent[i]] + r[:, sent[i]]
-
-
-def add3_body(kp, rp, kq, rq, kp2, sp2, kq2, sq2):
-    for k, r, ko, so in ((kp, rp, kp2, sp2), (kq, rq, kq2, sq2)):
-        ko[...] = k[:, 0] + r[:, 0]
-        so[...] = k[:, 1] + r[:, 1]
+def add1_body(k, r, ko, so):
+    at = (slice(None), slice(None)) if k.shape[1] == 4 else (slice(None),)
+    ko[...] = k[at + (0,)] + r[at + (0,)]
+    so[...] = k[at + (1,)] + r[at + (1,)]
+
+
+def add2_body(axis, at, k, r, ko, so):
+    kept, sent = pick(at, axis)
+    for i in range(2):
+        ko[:, i] = k[:, kept[i]] + r[:, kept[i]]
+        so[:, i] = k[:, sent[i]] + r[:, sent[i]]
+
+
+def add3_body(k, r, ko, so):
+    ko[...] = k[:, 0] + r[:, 0]
+    so[...] = k[:, 1] + r[:, 1]
 
 
 def add4_body(kp, rp, kq, rq, o):
@@ -384,39 +378,38 @@
 
     qkv, sg, kv, qg, total = project(offset, x, weights, out_grad[0])
     slices = lax.all_to_all(total.reshape(32, 32, HD), ("z", "y"), 0, 0, tiled=True)
-    factors_out = factors(at, x, sg, qkv, False, F32, "factors_give")
-    loc = local(qkv, sg, kv, qg)
-    local_out = local_part(at, x, loc, None, "local_give")
-    slices, factors_out, local_out = lax.optimization_barrier((slices, factors_out, local_out))
-    factors_in = lax.ppermute(factors_out, "core", SWAP)
-    local_in = lax.ppermute(local_out, "core", SWAP)
+    loc, given = local(at, qkv, sg, kv, qg, x)
+    slices, given = lax.optimization_barrier((slices, given))
+    arrived = lax.ppermute(given, "core", SWAP)
 
     scanned = scan_states(back, slices)
     states = lax.all_to_all(scanned, ("z", "y"), 0, 0, tiled=True)
-    mine = factors(at, x, sg, qkv, True, BF16, "factors_keep")
-    both = local_part(at, x, loc, local_in, "local_keep")
+    both, mine = keep(at, x, arrived, [(loc, 0), (loc, 2), (loc, 4), (sg, 0), (qkv, 4), (qkv, 2)])
     states, mine, both = lax.optimization_barrier((states, mine, both))
 
     states = states.reshape(2, H, HD, HD)
     states_in = lax.ppermute(states, "core", SWAP)
-    kx, sx, ky, sy = finish(at, both, mine, factors_in, states, states_in)
+    kx, sx, ky, sy = finish(at, both, mine, arrived, states, states_in)
     rx = exchange(sx, "x", 0)
     ry = exchange(sy, "y", 0)
     record_grad = inputs_grad(loc, qkv, sg, states, weights)
     rx, ry, record_grad = lax.optimization_barrier((rx, ry, record_grad))
-    kx, sx, ky, sy = whole_call(add1_body, "add1", [(8, 4, 8, 384)] * 4, kx, rx, ky, ry)
-    rx = exchange(sx, "x", 1)
-    ry = exchange(sy, "y", 1)
-    kp, sp, kq, sq = whole_call(add2_body, "add2", [(8, 2, 8, 384)] * 4, at, kx, rx, ky, ry)
+    kp, sp = whole_call(add1_body, "add1x", [(8, 4, 8, 384)] * 2, kx, rx)
+    rp = exchange(sp, "x", 1)
+    kq, sq = whole_call(add1_body, "add1y", [(8, 4, 8, 384)] * 2, ky, ry)
+    rq = exchange(sq, "y", 1)
+    kp, sp = whole_call(functools.partial(add2_body, 1), "add2x", [(8, 2, 8, 384)] * 2, at, kp, rp)
     rp = exchange(sp, "y", 0)
+    kq, sq = whole_call(functools.partial(add2_body, 0), "add2y", [(8, 2, 8, 384)] * 2, at, kq, rq)
     rq = exchange(sq, "x", 0)
-    kp, sp, kq, sq = whole_call(add3_body, "add3", [(8, 8, 384)] * 4, kp, rp, kq, rq)
+    kp, sp = whole_call(add3_body, "add3x", [(8, 8, 384)] * 2, kp, rp)
     rp = exchange(sp, "y", 1)
+    kq, sq = whole_call(add3_body, "add3y", [(8, 8, 384)] * 2, kq, rq)
     rq = exchange(sq, "x", 1)
     (part,) = whole_call(add4_body, "add4", [(8, 8, 768)], kp, rp, kq, rq)
     part = lax.all_to_all(part, "z", 0, 0, tiled=True)
-    (mine,) = whole_call(sum_body, "sum_z", [(8, 8, 768)], part)
-    rows = lax.all_to_all(mine, ("x", "core"), 0, 0, tiled=True)
+    (own,) = whole_call(sum_body, "sum_z", [(8, 8, 768)], part)
+    rows = lax.all_to_all(own, ("x", "core"), 0, 0, tiled=True)
     (proj_grad,) = whole_call(place_body, "place", [(32, 3 * D)], rows)
     return record_grad[None], proj_grad
 

time: 140 us -> 135 us (0.964)
  local copies, waits for them, and re-layouts: 13.2 us -> 0.59 us
  Pallas kernels: 44.2 us -> 49.1 us
  waiting for transfers between devices: 20.9 us -> 25.7 us
  starting transfers between devices: 32.8 us -> 30.9 us
    unnamed x32 -> x6, local copies, waits for them, and re-layouts: 13.1 us -> 0.01 us
    pallas_call x5 -> x2, Pallas kernels: 18.8 us -> 24.3 us  [the longest x1 15.1 us: local(): pl.pallas_call(local_body, grid_spec=pltpu.PrefetchScalarGridSpec(num_sca...]
    all_to_all x1, waiting for transfers between devices: 1.75 us -> 6.17 us  [shards(): states = lax.all_to_all(scanned, ('z', 'y'), 0, 0, tiled=True)]
    ppermute x2 -> x1, waiting for transfers between devices: 0.01 us -> 1.47 us  [shards(): arrived = lax.ppermute(given, 'core', SWAP)]
  transfers between devices with their start and end apart: 13 -> 12, of which waited for: 9 -> 10; matrix products, arithmetic and copies ran while one was open for 0% -> 0% of each run, Pallas kernels for 20% -> 26%
where the time goes in v5:
time: 135 us; the launch traced here: 134 us
  Pallas kernels  49.1 us (36%)
  starting transfers between devices  30.9 us (23%)
  blocking collectives  26.9 us (20%)
  waiting for transfers between devices  25.7 us (19%)
    ppermute x8, waiting for transfers between devices, exchange(): return lax.ppermute(value, (axis, 'core'), pairs)  16 us
    all_to_all x1, blocking collectives, shards(): rows = lax.all_to_all(own, ('x', 'core'), 0, 0, tiled=True)  15.4 us
    pallas_call x1, Pallas kernels, local(): pl.pallas_call(local_body, grid_spec=pltpu.PrefetchScalarGridSpec(num_sca...  15.1 us
    all_to_all x1, starting transfers between devices, shards(): lax.all_to_all(total.reshape(32, 32, HD), ('z', 'y'), 0, 0, tiled=True)  12 us
    all_to_all x1, blocking collectives, shards(): part = lax.all_to_all(part, 'z', 0, 0, tiled=True)  11.4 us
    pallas_call x1, Pallas kernels, project(): pl.pallas_call(project_body, grid_spec=pltpu.PrefetchScalarGridSpec(num_s...  9.16 us
    pallas_call x1, Pallas kernels, keep(): pl.pallas_call(keep_body, grid_spec=pltpu.PrefetchScalarGridSpec(num_scal...  9.13 us
    pallas_call x1, Pallas kernels, inputs_grad(): pl.pallas_call(inputs_body, grid=(NB,), in_specs=[block(3 * D), block(3 *...  8.08 us
  transfers between devices with their start and end apart: 12, of which 10 were waited for; matrix products, arithmetic and copies ran while one was open for 0% of the time, Pallas kernels for 26%

profile of v5, /device:TPU:1, one launch (start us, length us, event | category | flops | bytes accessed | tf_op | source)
XLA Modules:
  0.0 134.0 jit_solution(4700421067725514399)
XLA Ops:
  0.6 9.2 %project.1 = (bf16[1024,1536]{1,0:T(8,128)(2,1)}, bf16[1024,512]{1,0:T(8,128)(2,1)}, f32[4,4,128,128]{3,2,1,0:T(8,128)}, f32[4,4,128,128]{3,2,1,0:T(8,128)}, f32[2,4,128,128]{3,2,1,0:T(8,128)}) custom-call(s32[1]{0:T(128)} %bitcast.10.pos_ref, bf16[1024,1024]{1,0:T(8,128)(2,1)} %bitcast.19, bf16[1024,1536]{1,0:T(8,128)(2,1)} %w_ref.3, bf16[1024,512]{1,0:T(8,128)(2,1)} %bitcast.22), custom_call_target="tpu_custom_call" | custom-call | tf_op jit(solution)/shard_map/project/pallas_call | solution.py:68
  9.8 12.0 %all-to-all-start = ((f32[32,32,128]{2,1,0:T(8,128)}), f32[32,32,128]{2,1,0:T(8,128)S(1)}, u32[]{:S(2)}, u32[]{:S(2)}) async-start(f32[32,32,128]{2,1,0:T(8,128)} %bitcast.23), calls=%async_computation | async-start | bytes 1048576 | tf_op jit(solution)/shard_map/all_to_all | solution.py:380
  21.9 0.6 stack.39.at_ref.at
  22.5 15.1 %local.1 = (bf16[1024,1536]{1,0:T(8,128)(2,1)}, f32[1024,1536]{1,0:T(8,128)}) custom-call(s32[9]{0:T(128)} %stack.39.at_ref.at, bf16[1024,1536]{1,0:T(8,128)(2,1)} %get-tuple-element.36.qkv_ref.refs_4_.refs_5_, bf16[1024,512]{1,0:T(8,128)(2,1)} %get-tuple-element.37.sg_ref.refs_3_, f32[4,4,128,128]{3,2,1,0:T(8,128)} %get-tuple-element.38.kv_ref, ...), custom_call_target="tpu_custom_call" | custom-call | flops 8000000000 | bytes 24000000 | tf_op jit(solution)/shard_map/local/pallas_call | solution.py:156
  37.6 0.5 all-to-all-done.v_ref
  38.1 2.4 %collective-permute-start = (f32[1024,1536]{1,0:T(8,128)}, f32[1024,1536]{1,0:T(8,128)}, u32[]{:S(2)}, u32[]{:S(2)}) collective-permute-start(f32[1024,1536]{1,0:T(8,128)} %get-tuple-element.42), channel_id=1, source_target_pairs={{0,1},{1,0},{2,3},{3,2},{4,5},{5,4},{6,7},{7,6},{8,9},{9,8},{10,11... | collective-permute-start | bytes 18874376 | tf_op jit(solution)/shard_map/ppermute | solution.py:383
  40.5 1.1 scan_states.1
  41.6 7.6 %all-to-all-start.1 = ((f32[32,32,128]{2,1,0:T(8,128)}), f32[32,32,128]{2,1,0:T(8,128)S(1)}, u32[]{:S(2)}, u32[]{:S(2)}) async-start(f32[32,32,128]{2,1,0:T(8,128)} %scan_states.1), calls=%async_computation.1 | async-start | bytes 1048576 | tf_op jit(solution)/shard_map/all_to_all | solution.py:386
  49.2 1.5 %collective-permute-done.r_ref.b_hbm = f32[1024,1536]{1,0:T(8,128)} collective-permute-done((f32[1024,1536]{1,0:T(8,128)}, f32[1024,1536]{1,0:T(8,128)}, u32[]{:S(2)}, u32[]{:S(2)}) %collective-permute-start) | collective-permute-done | bytes 6291488 | tf_op jit(solution)/shard_map/ppermute | solution.py:383
  50.7 0.0 copy-start.2
  50.7 9.1 %keep.1 = (f32[1024,768]{1,0:T(8,128)}, bf16[1024,768]{1,0:T(8,128)(2,1)}) custom-call(s32[9]{0:T(128)} %stack.39.at_ref.at, bf16[1024,1024]{1,0:T(8,128)(2,1)} %bitcast.21, f32[1024,1536]{1,0:T(8,128)} %collective-permute-done.r_ref.b_hbm, bf16[1024,1536]{1,0:T(8,128)(2,1)} %get-tuple-element.43.refs_0_.refs_1_.refs_2_.loc_ref, ...), custom_call_target="tpu_custom_call" | custom-call | flops 5000000000 | bytes 16000000 | tf_op jit(solution)/shard_map/keep/pallas_call | solution.py:192
  59.8 6.2 %all-to-all-done.1 = f32[32,32,128]{2,1,0:T(8,128)S(1)} async-done(((f32[32,32,128]{2,1,0:T(8,128)}), f32[32,32,128]{2,1,0:T(8,128)S(1)}, u32[]{:S(2)}, u32[]{:S(2)}) %all-to-all-start.1) | async-done | bytes 524320 | tf_op jit(solution)/shard_map/all_to_all | solution.py:386
  66.0 0.0 copy-start
  66.0 0.0 copy-start.1
  66.0 1.9 %collective-permute-start.1 = (f32[2,4,128,128]{3,2,1,0:T(8,128)S(1)}, f32[2,4,128,128]{3,2,1,0:T(8,128)S(1)}, u32[]{:S(2)}, u32[]{:S(2)}) collective-permute-start(f32[2,4,128,128]{3,2,1,0:T(8,128)S(1)} %bitcast.16), channel_id=1, source_target_pairs={{0,1},{1,0},{2,3},{3,2},{4,5},{5,4},{6,7},{7,6},{8,9},{9,8},{10,11... | collective-permute-start | bytes 1572872 | tf_op jit(solution)/shard_map/ppermute | solution.py:391
  67.8 1.5 %collective-permute-done.1.sb_ref = f32[2,4,128,128]{3,2,1,0:T(8,128)S(1)} collective-permute-done((f32[2,4,128,128]{3,2,1,0:T(8,128)S(1)}, f32[2,4,128,128]{3,2,1,0:T(8,128)S(1)}, u32[]{:S(2)}, u32[]{:S(2)}) %collective-permute-start.1) | collective-permute-done | bytes 524320 | tf_op jit(solution)/shard_map/ppermute | solution.py:391
  69.4 0.0 copy-done.2
  69.4 4.5 %finish.1 = (f32[8,4,2,8,384]{4,3,2,1,0:T(8,128)S(1)}, f32[8,4,2,8,384]{4,3,2,1,0:T(8,128)S(1)}, f32[8,2,4,8,384]{4,3,2,1,0:T(8,128)S(1)}, f32[8,2,4,8,384]{4,3,2,1,0:T(8,128)S(1)}) custom-call(s32[9]{0:T(128)S(1)} %copy-done.2, f32[1024,768]{1,0:T(8,128)} %get-tuple-element.46.w_hbm, bf16[1024,768]{1,0:T(8,128)(2,1)} %get-tuple-element.47.a_hbm, ...), custom_call_target="tpu_custom_call" | custom-call | flops 1000000000 | bytes 12000000 | tf_op jit(solution)/shard_map/finish/pallas_call | solution.py:251
  73.8 2.6 %collective-permute-start.2 = (f32[8,4,2,8,384]{4,3,2,1,0:T(8,128)S(1)}, f32[8,4,2,8,384]{4,3,2,1,0:T(8,128)S(1)}, u32[]{:S(2)}, u32[]{:S(2)}) collective-permute-start(f32[8,4,2,8,384]{4,3,2,1,0:T(8,128)S(1)} %get-tuple-element.49), channel_id=1, source_target_pairs={{0,2},{1,7},{2,0},{3,5},{4,6},{5,3},{6,4},{7,1},{8,10},{9,15},{10,... | collective-permute-start | bytes 2359304 | tf_op jit(solution)/shard_map/ppermute | solution.py:363
  76.4 1.9 %collective-permute-start.3 = (f32[8,2,4,8,384]{4,3,2,1,0:T(8,128)S(1)}, f32[8,2,4,8,384]{4,3,2,1,0:T(8,128)S(1)}, u32[]{:S(2)}, u32[]{:S(2)}) collective-permute-start(f32[8,2,4,8,384]{4,3,2,1,0:T(8,128)S(1)} %get-tuple-element.50), channel_id=1, source_target_pairs={{0,8},{1,25},{8,0},{9,17},{16,24},{17,9},{24,16},{25,1},{2,10},{3,... | collective-permute-start | bytes 2359304 | tf_op jit(solution)/shard_map/ppermute | solution.py:363
  78.3 0.0 copy-done
  78.3 0.0 copy-done.1
  78.3 8.1 %inputs_grad.1 = bf16[1024,1024]{1,0:T(8,128)(2,1)} custom-call(bf16[1024,1536]{1,0:T(8,128)(2,1)S(1)} %copy-done, bf16[1024,1536]{1,0:T(8,128)(2,1)} %get-tuple-element.36.qkv_ref.refs_4_.refs_5_, bf16[1024,512]{1,0:T(8,128)(2,1)S(1)} %copy-done.1, f32[2,4,128,128]{3,2,1,0:T(8,128)S(1)} %bitcast.18, bf16[1024,1536]{1,0:T(8,128)(2,1)} %w_ref.3), custom_call_target="tpu_custom_call" | custom-call | flops 5000000000 | bytes 14000000 | tf_op jit(solution)/shard_map/inputs_grad/pallas_call | solution.py:286
  86.4 0.0 collective-permute-done.2.r
  86.4 2.1 %collective-permute-done.3.r = f32[8,2,4,8,384]{4,3,2,1,0:T(8,128)S(1)} collective-permute-done((f32[8,2,4,8,384]{4,3,2,1,0:T(8,128)S(1)}, f32[8,2,4,8,384]{4,3,2,1,0:T(8,128)S(1)}, u32[]{:S(2)}, u32[]{:S(2)}) %collective-permute-start.3) | collective-permute-done | bytes 786464 | tf_op jit(solution)/shard_map/ppermute | solution.py:363
  88.5 0.1 add1y.1
  88.5 0.1 collective-permute-start.7
  88.6 0.1 add1x.1
  88.7 0.1 collective-permute-start.4
  88.8 6.7 %collective-permute-done.7.r = f32[8,4,8,384]{3,2,1,0:T(8,128)S(1)} collective-permute-done((f32[8,4,8,384]{3,2,1,0:T(8,128)S(1)}, f32[8,4,8,384]{3,2,1,0:T(8,128)S(1)}, u32[]{:S(2)}, u32[]{:S(2)}) %collective-permute-start.7) | collective-permute-done | bytes 393248 | tf_op jit(solution)/shard_map/ppermute | solution.py:363
  95.6 0.6 add2y.1
  96.1 0.3 collective-permute-start.8
  96.4 0.0 collective-permute-done.4.r
  96.4 0.6 add2x.1
  97.0 1.9 %collective-permute-start.5 = (f32[8,2,8,384]{3,2,1,0:T(8,128)S(1)}, f32[8,2,8,384]{3,2,1,0:T(8,128)S(1)}, u32[]{:S(2)}, u32[]{:S(2)}) collective-permute-start(f32[8,2,8,384]{3,2,1,0:T(8,128)S(1)} %get-tuple-element.57), channel_id=1, source_target_pairs={{0,8},{1,25},{8,0},{9,17},{16,24},{17,9},{24,16},{25,1},{2,10},{3,... | collective-permute-start | bytes 589832 | tf_op jit(solution)/shard_map/ppermute | solution.py:363
  99.0 3.0 %collective-permute-done.8.r = f32[8,2,8,384]{3,2,1,0:T(8,128)S(1)} collective-permute-done((f32[8,2,8,384]{3,2,1,0:T(8,128)S(1)}, f32[8,2,8,384]{3,2,1,0:T(8,128)S(1)}, u32[]{:S(2)}, u32[]{:S(2)}) %collective-permute-start.8) | collective-permute-done | bytes 196640 | tf_op jit(solution)/shard_map/ppermute | solution.py:363
  102.0 0.1 collective-permute-start.9
  102.1 0.8 collective-permute-done.5.r
  102.9 0.1 collective-permute-start.6
  103.0 2.6 %collective-permute-done.9.rq = f32[8,8,384]{2,1,0:T(8,128)S(1)} collective-permute-done((f32[8,8,384]{2,1,0:T(8,128)S(1)}, f32[8,8,384]{2,1,0:T(8,128)S(1)}, u32[]{:S(2)}, u32[]{:S(2)}) %collective-permute-start.9) | collective-permute-done | bytes 98336 | tf_op jit(solution)/shard_map/ppermute | solution.py:363
  105.5 0.9 collective-permute-done.6.rp
  106.5 11.4 %all_to_all.20.v = f32[8,8,768]{2,1,0:T(8,128)S(1)} all-to-all(f32[8,8,768]{2,1,0:T(8,128)S(1)} %add4.1), channel_id=1, replica_groups=mesh['z'=8,'y'=4,'x'=4,'core'=2] {'z'}, dimensions={0} | all-to-all | bytes 393216 | tf_op jit(solution)/shard_map/all_to_all | solution.py:410
  117.9 15.4 %all_to_all.21.v = f32[8,8,768]{2,1,0:T(8,128)S(1)} all-to-all(f32[8,8,768]{2,1,0:T(8,128)S(1)} %sum_z.1), channel_id=1, replica_groups=mesh['z'=8,'y'=4,'x'=4,'core'=2] {'x','core'}, dimensions={0} | all-to-all | bytes 393216 | tf_op jit(solution)/shard_map/all_to_all | solution.py:412
  133.3 0.7 place.1
  (4 shorter events, 0.1 us)
Async XLA Ops:
  9.8 28.3 %all-to-all-start = ((f32[32,32,128]{2,1,0:T(8,128)}), f32[32,32,128]{2,1,0:T(8,128)S(1)}, u32[]{:S(2)}, u32[]{:S(2)}) async-start(f32[32,32,128]{2,1,0:T(8,128)} %bitcast.23), calls=%async_computation | async-start | bytes 1048576 | tf_op jit(solution)/shard_map/all_to_all | solution.py:380
  38.1 12.5 %collective-permute-start = (f32[1024,1536]{1,0:T(8,128)}, f32[1024,1536]{1,0:T(8,128)}, u32[]{:S(2)}, u32[]{:S(2)}) collective-permute-start(f32[1024,1536]{1,0:T(8,128)} %get-tuple-element.42), channel_id=1, source_target_pairs={{0,1},{1,0},{2,3},{3,2},{4,5},{5,4},{6,7},{7,6},{8,9},{9,8},{10,11... | collective-permute-start | bytes 18874376 | tf_op jit(solution)/shard_map/ppermute | solution.py:383
  41.6 24.4 %all-to-all-start.1 = ((f32[32,32,128]{2,1,0:T(8,128)}), f32[32,32,128]{2,1,0:T(8,128)S(1)}, u32[]{:S(2)}, u32[]{:S(2)}) async-start(f32[32,32,128]{2,1,0:T(8,128)} %scan_states.1), calls=%async_computation.1 | async-start | bytes 1048576 | tf_op jit(solution)/shard_map/all_to_all | solution.py:386
  50.7 18.7 %copy-start.2 = (s32[9]{0:T(128)S(1)}, s32[9]{0:T(128)}, u32[]{:S(2)}) copy-start(s32[9]{0:T(128)} %stack.39.at_ref.at) | copy-start | bytes 112
  66.0 12.3 %copy-start = (bf16[1024,1536]{1,0:T(8,128)(2,1)S(1)}, bf16[1024,1536]{1,0:T(8,128)(2,1)}, u32[]{:S(2)}) copy-start(bf16[1024,1536]{1,0:T(8,128)(2,1)} %get-tuple-element.43.refs_0_.refs_1_.refs_2_.loc_ref) | copy-start | bytes 9437188
  66.0 12.3 %copy-start.1 = (bf16[1024,512]{1,0:T(8,128)(2,1)S(1)}, bf16[1024,512]{1,0:T(8,128)(2,1)}, u32[]{:S(2)}) copy-start(bf16[1024,512]{1,0:T(8,128)(2,1)} %get-tuple-element.37.sg_ref.refs_3_) | copy-start | bytes 3145732
  66.0 3.4 %collective-permute-start.1 = (f32[2,4,128,128]{3,2,1,0:T(8,128)S(1)}, f32[2,4,128,128]{3,2,1,0:T(8,128)S(1)}, u32[]{:S(2)}, u32[]{:S(2)}) collective-permute-start(f32[2,4,128,128]{3,2,1,0:T(8,128)S(1)} %bitcast.16), channel_id=1, source_target_pairs={{0,1},{1,0},{2,3},{3,2},{4,5},{5,4},{6,7},{7,6},{8,9},{9,8},{10,11... | collective-permute-start | bytes 1572872 | tf_op jit(solution)/shard_map/ppermute | solution.py:391
  73.8 12.5 %collective-permute-start.2 = (f32[8,4,2,8,384]{4,3,2,1,0:T(8,128)S(1)}, f32[8,4,2,8,384]{4,3,2,1,0:T(8,128)S(1)}, u32[]{:S(2)}, u32[]{:S(2)}) collective-permute-start(f32[8,4,2,8,384]{4,3,2,1,0:T(8,128)S(1)} %get-tuple-element.49), channel_id=1, source_target_pairs={{0,2},{1,7},{2,0},{3,5},{4,6},{5,3},{6,4},{7,1},{8,10},{9,15},{10,... | collective-permute-start | bytes 2359304 | tf_op jit(solution)/shard_map/ppermute | solution.py:363
  76.4 12.1 %collective-permute-start.3 = (f32[8,2,4,8,384]{4,3,2,1,0:T(8,128)S(1)}, f32[8,2,4,8,384]{4,3,2,1,0:T(8,128)S(1)}, u32[]{:S(2)}, u32[]{:S(2)}) collective-permute-start(f32[8,2,4,8,384]{4,3,2,1,0:T(8,128)S(1)} %get-tuple-element.50), channel_id=1, source_target_pairs={{0,8},{1,25},{8,0},{9,17},{16,24},{17,9},{24,16},{25,1},{2,10},{3,... | collective-permute-start | bytes 2359304 | tf_op jit(solution)/shard_map/ppermute | solution.py:363
  88.5 7.0 %collective-permute-start.7 = (f32[8,4,8,384]{3,2,1,0:T(8,128)S(1)}, f32[8,4,8,384]{3,2,1,0:T(8,128)S(1)}, u32[]{:S(2)}, u32[]{:S(2)}) collective-permute-start(f32[8,4,8,384]{3,2,1,0:T(8,128)S(1)} %get-tuple-element.63), channel_id=1, source_target_pairs={{0,24},{1,9},{8,16},{9,1},{16,8},{17,25},{24,0},{25,17},{2,26},{3,... | collective-permute-start | bytes 1179656 | tf_op jit(solution)/shard_map/ppermute | solution.py:363
  88.7 7.7 %collective-permute-start.4 = (f32[8,4,8,384]{3,2,1,0:T(8,128)S(1)}, f32[8,4,8,384]{3,2,1,0:T(8,128)S(1)}, u32[]{:S(2)}, u32[]{:S(2)}) collective-permute-start(f32[8,4,8,384]{3,2,1,0:T(8,128)S(1)} %get-tuple-element.55), channel_id=1, source_target_pairs={{0,6},{1,3},{2,4},{3,1},{4,2},{5,7},{6,0},{7,5},{8,14},{9,11},{10,... | collective-permute-start | bytes 1179656 | tf_op jit(solution)/shard_map/ppermute | solution.py:363
  96.1 5.8 %collective-permute-start.8 = (f32[8,2,8,384]{3,2,1,0:T(8,128)S(1)}, f32[8,2,8,384]{3,2,1,0:T(8,128)S(1)}, u32[]{:S(2)}, u32[]{:S(2)}) collective-permute-start(f32[8,2,8,384]{3,2,1,0:T(8,128)S(1)} %get-tuple-element.65), channel_id=1, source_target_pairs={{0,2},{1,7},{2,0},{3,5},{4,6},{5,3},{6,4},{7,1},{8,10},{9,15},{10,... | collective-permute-start | bytes 589832 | tf_op jit(solution)/shard_map/ppermute | solution.py:363
  97.0 5.8 %collective-permute-start.5 = (f32[8,2,8,384]{3,2,1,0:T(8,128)S(1)}, f32[8,2,8,384]{3,2,1,0:T(8,128)S(1)}, u32[]{:S(2)}, u32[]{:S(2)}) collective-permute-start(f32[8,2,8,384]{3,2,1,0:T(8,128)S(1)} %get-tuple-element.57), channel_id=1, source_target_pairs={{0,8},{1,25},{8,0},{9,17},{16,24},{17,9},{24,16},{25,1},{2,10},{3,... | collective-permute-start | bytes 589832 | tf_op jit(solution)/shard_map/ppermute | solution.py:363
  102.0 3.6 %collective-permute-start.9 = (f32[8,8,384]{2,1,0:T(8,128)S(1)}, f32[8,8,384]{2,1,0:T(8,128)S(1)}, u32[]{:S(2)}, u32[]{:S(2)}) collective-permute-start(f32[8,8,384]{2,1,0:T(8,128)S(1)} %get-tuple-element.67), channel_id=1, source_target_pairs={{0,6},{1,3},{2,4},{3,1},{4,2},{5,7},{6,0},{7,5},{8,14},{9,11},{10,... | collective-permute-start | bytes 294920 | tf_op jit(solution)/shard_map/ppermute | solution.py:363
  102.9 3.6 %collective-permute-start.6 = (f32[8,8,384]{2,1,0:T(8,128)S(1)}, f32[8,8,384]{2,1,0:T(8,128)S(1)}, u32[]{:S(2)}, u32[]{:S(2)}) collective-permute-start(f32[8,8,384]{2,1,0:T(8,128)S(1)} %get-tuple-element.59), channel_id=1, source_target_pairs={{0,24},{1,9},{8,16},{9,1},{16,8},{17,25},{24,0},{25,17},{2,26},{3,... | collective-permute-start | bytes 294920 | tf_op jit(solution)/shard_map/ppermute | solution.py:363

commit v6 on v5

--- a/solution.py
+++ b/solution.py
@@ -42,10 +42,10 @@
     return pl.ds(part * D + h * HD, HD)
 
 
-def project_body(pos_ref, x_ref, w_ref, g_ref, qkv_ref, sg_ref, kv_ref, qg_ref, total_ref):
+def project_body(at_ref, x_ref, w_ref, g_ref, qkv_ref, sg_ref, kv_ref, qg_ref, total_ref):
     n = pl.program_id(0)
     qkv_ref[...] = dot(x_ref[...], w_ref[...], NN).astype(BF16)
-    pos = (pos_ref[0] + n * CH + lax.broadcasted_iota(jnp.int32, (CH, 1), 0)).astype(F32)
+    pos = (at_ref[9] + n * CH + lax.broadcasted_iota(jnp.int32, (CH, 1), 0)).astype(F32)
     factor = 1.0 / jnp.sqrt(jnp.float32(HD) * (pos + 1.0))
     sg_ref[...] = (g_ref[...].astype(F32) * factor).astype(BF16)
 
@@ -62,7 +62,7 @@
         total_ref[1, h] += qg
 
 
-def project(offset, x, w, g):
+def project(at, x, w, g):
     block = lambda cols: pl.BlockSpec((CH, cols), lambda n, s: (n, 0))
     sums = pl.BlockSpec((1, H, HD, HD), lambda n, s: (n, 0, 0, 0))
     return pl.pallas_call(
@@ -88,20 +88,20 @@
         ],
         compiler_params=params(60),
         name="project",
-    )(offset, x, w, g)
-
-
-def scan_body(count, back_ref, v_ref, o_ref):
+    )(at, x, w, g)
+
+
+def scan_body(count, at_ref, v_ref, o_ref):
 
     def step(t, so_far):
-        i = jnp.where(back_ref[0] == 1, count - 1 - t, t)
+        i = jnp.where(at_ref[10] == 1, count - 1 - t, t)
         o_ref[i] = so_far
         return so_far + v_ref[i]
 
     lax.fori_loop(0, count, step, jnp.zeros(v_ref.shape[1:], F32))
 
 
-def scan_states(back, v):
+def scan_states(at, v):
     return pl.pallas_call(
         functools.partial(scan_body, v.shape[0]),
         in_specs=[pl.BlockSpec(memory_space=pltpu.SMEM), pl.BlockSpec(memory_space=pltpu.VMEM)],
@@ -109,12 +109,17 @@
         out_shape=jax.ShapeDtypeStruct(v.shape, F32),
         compiler_params=params(4),
         name="scan_states",
-    )(back, v)
-
-
-def local_body(at_ref, qkv_ref, sg_ref, kv_ref, qg_ref, x_ref, loc_ref, give_ref, from_ref):
+    )(at, v)
+
+
+def local_body(at_ref, qkv_ref, sg_ref, kv_ref, qg_ref, x_hbm, loc_ref, give_ref, from_ref, x_ref, sem):
     n = pl.program_id(0)
+    copy = pltpu.make_async_copy(x_hbm, x_ref, sem)
     theirs = pl.multiple_of((1 - at_ref[0]) * 256, 256)
+
+    @pl.when(n == 0)
+    def _():
+        copy.start()
 
     @pl.when(n < NB)
     def _():
@@ -139,13 +144,15 @@
         rows = pl.ds(pl.multiple_of(n * CH, CH), CH)
         for p in range(3):
             from_ref[rows, p * 256 : (p + 1) * 256] = loc_ref[:, pl.ds(p * D + theirs, 256)]
-        from_ref[rows, 768:1024] = sg_ref[:, pl.ds(theirs, 256)]
-        from_ref[rows, 1024:1280] = qkv_ref[:, pl.ds(2 * D + theirs, 256)]
-        from_ref[rows, 1280:1536] = qkv_ref[:, pl.ds(D + theirs, 256)]
+
+    @pl.when(n == NB)
+    def _():
+        copy.wait()
 
     @pl.when(n >= NB)
     def _():
-        give_ref[...] = dot(x_ref[...], from_ref[...], TN)
+        half = pl.ds(pl.multiple_of((n - NB) * (DM // 2), DM // 2), DM // 2)
+        give_ref[...] = dot(x_ref[:, half], from_ref[...], TN)
 
 
 def local(at, qkv, sg, kv, qg, x):
@@ -157,25 +164,51 @@
         local_body,
         grid_spec=pltpu.PrefetchScalarGridSpec(
             num_scalar_prefetch=1,
-            grid=(2 * NB,),
+            grid=(NB + 2,),
             in_specs=[
                 block(3 * D),
                 block(D),
                 sums,
                 sums,
-                pl.BlockSpec((TOK, DM // 4), lambda n, s: (0, last(n))),
+                pl.BlockSpec(memory_space=pltpu.HBM),
             ],
-            out_specs=[block(3 * D), pl.BlockSpec((DM // 4, 3 * D), lambda n, s: (last(n), 0))],
-            scratch_shapes=[pltpu.VMEM((TOK, 3 * D), BF16)],
+            out_specs=[block(3 * D), pl.BlockSpec((DM // 2, 768), lambda n, s: (last(n), 0))],
+            scratch_shapes=[
+                pltpu.VMEM((TOK, 768), BF16),
+                pltpu.VMEM((TOK, DM), BF16),
+                pltpu.SemaphoreType.DMA,
+            ],
         ),
         out_shape=[
             jax.ShapeDtypeStruct((TOK, 3 * D), BF16),
-            jax.ShapeDtypeStruct((DM, 3 * D), F32),
+            jax.ShapeDtypeStruct((DM, 768), F32),
         ],
         compiler_params=params(60),
         cost_estimate=cost(8e9, 24e6),
         name="local",
     )(at, qkv, sg, kv, qg, x)
+
+
+def factors_body(at_ref, x_ref, *refs):
+    for j, ref in enumerate(refs[:3]):
+        refs[3][:, j * 256 : (j + 1) * 256] = dot(x_ref[...], ref[...], TN)
+
+
+def factors(at, x, sources):
+    cols = [pl.BlockSpec((TOK, 256), lambda i, s, f=f: (0, f + 1 - s[0])) for _, f in sources]
+    return pl.pallas_call(
+        factors_body,
+        grid_spec=pltpu.PrefetchScalarGridSpec(
+            num_scalar_prefetch=1,
+            grid=(2,),
+            in_specs=[pl.BlockSpec((TOK, DM // 2), lambda i, s: (0, i))] + cols,
+            out_specs=pl.BlockSpec((DM // 2, 768), lambda i, s: (i, 0)),
+        ),
+        out_shape=jax.ShapeDtypeStruct((DM, 768), F32),
+        compiler_params=params(60),
+        cost_estimate=cost(3e9, 12e6),
+        name="factors",
+    )(at, x, *(a for a, _ in sources))
 
 
 def keep_body(at_ref, x_ref, r_ref, *refs):
@@ -188,18 +221,18 @@
 
 def keep(at, x, arrived, sources):
     cols = [pl.BlockSpec((TOK, 256), lambda i, s, f=f: (0, f + s[0])) for _, f in sources]
-    rows = pl.BlockSpec((DM // 4, 768), lambda i, s: (i, 0))
+    rows = pl.BlockSpec((DM // 2, 768), lambda i, s: (i, 0))
     return pl.pallas_call(
         keep_body,
         grid_spec=pltpu.PrefetchScalarGridSpec(
             num_scalar_prefetch=1,
-            grid=(4,),
-            in_specs=[pl.BlockSpec((TOK, DM // 4), lambda i, s: (0, i)), rows] + cols,
+            grid=(2,),
+            in_specs=[pl.BlockSpec((TOK, DM // 2), lambda i, s: (0, i)), rows] + cols,
             out_specs=[rows, rows],
         ),
         out_shape=[jax.ShapeDtypeStruct((DM, 768), F32), jax.ShapeDtypeStruct((DM, 768), BF16)],
         compiler_params=params(60),
-        cost_estimate=cost(5e9, 16e6),
+        cost_estimate=cost(40e9, 16e6),
         name="keep",
     )(at, x, arrived, *(a for a, _ in sources))
 
@@ -218,7 +251,7 @@
             (
                 pltpu.make_async_copy(w_hbm.at[:, cols], w_ref.at[j], sems.at[0, j]),
                 pltpu.make_async_copy(a_hbm.at[:, cols], a_ref.at[j], sems.at[1, j]),
-                pltpu.make_async_copy(b_hbm.at[:, pl.ds(768 + j * 256, 256)], b_ref.at[j], sems.at[2, j]),
+                pltpu.make_async_copy(b_hbm.at[:, cols], b_ref.at[j], sems.at[2, j]),
             )
         )
     for pair in copies:
@@ -372,24 +405,26 @@
     at = jnp.stack(
         [core]
         + [v for i in (x_at, y_at) for v in (i, i ^ first ^ second, i ^ first, i ^ second)]
+        + [tm_at * TOK, (tm_at >= 16).astype(jnp.int32)]
     ).astype(jnp.int32)
-    offset = (tm_at * TOK).astype(jnp.int32)[None]
-    back = (tm_at >= 16).astype(jnp.int32)[None]
-
-    qkv, sg, kv, qg, total = project(offset, x, weights, out_grad[0])
+
+    qkv, sg, kv, qg, total = project(at, x, weights, out_grad[0])
     slices = lax.all_to_all(total.reshape(32, 32, HD), ("z", "y"), 0, 0, tiled=True)
     loc, given = local(at, qkv, sg, kv, qg, x)
     slices, given = lax.optimization_barrier((slices, given))
-    arrived = lax.ppermute(given, "core", SWAP)
-
-    scanned = scan_states(back, slices)
+    local_in = lax.ppermute(given, "core", SWAP)
+
+    scanned = scan_states(at, slices)
+    scanned, sg, qkv, loc = lax.optimization_barrier((scanned, sg, qkv, loc))
     states = lax.all_to_all(scanned, ("z", "y"), 0, 0, tiled=True)
-    both, mine = keep(at, x, arrived, [(loc, 0), (loc, 2), (loc, 4), (sg, 0), (qkv, 4), (qkv, 2)])
+    given = factors(at, x, [(sg, 0), (qkv, 4), (qkv, 2)])
+    factors_in = lax.ppermute(given, "core", SWAP)
+    both, mine = keep(at, x, local_in, [(loc, 0), (loc, 2), (loc, 4), (sg, 0), (qkv, 4), (qkv, 2)])
     states, mine, both = lax.optimization_barrier((states, mine, both))
 
     states = states.reshape(2, H, HD, HD)
     states_in = lax.ppermute(states, "core", SWAP)
-    kx, sx, ky, sy = finish(at, both, mine, arrived, states, states_in)
+    kx, sx, ky, sy = finish(at, both, mine, factors_in, states, states_in)
     rx = exchange(sx, "x", 0)
     ry = exchange(sy, "y", 0)
     record_grad = inputs_grad(loc, qkv, sg, states, weights)

time: 135 us -> 134 us (level)
  Pallas kernels: 49.1 us -> 52.9 us
  starting transfers between devices: 30.9 us -> 28.1 us
  waiting for transfers between devices: 25.7 us -> 23.7 us
    pallas_call x0 -> x1, Pallas kernels: none -> 5.64 us  [factors(): pl.pallas_call(factors_body, grid_spec=pltpu.PrefetchScalarGridSpec(num_s...]
    all_to_all x1, waiting for transfers between devices: 6.17 us -> 2.26 us  [shards(): states = lax.all_to_all(scanned, ('z', 'y'), 0, 0, tiled=True)]
    all_to_all x1, waiting for transfers between devices: 0.54 us -> 3.77 us  [shards(): lax.all_to_all(total.reshape(32, 32, HD), ('z', 'y'), 0, 0, tiled=True)]
    all_to_all x1, starting transfers between devices: 7.58 us -> 4.41 us  [shards(): states = lax.all_to_all(scanned, ('z', 'y'), 0, 0, tiled=True)]
    pallas_call x1, Pallas kernels: 15.1 us -> 12.5 us  [local(): pl.pallas_call(local_body, grid_spec=pltpu.PrefetchScalarGridSpec(num_sca...]
    ppermute x1 -> x2, waiting for transfers between devices: 1.47 us -> 0.01 us  [the longest x1 0.01 us: shards(): local_in = lax.ppermute(given, 'core', SWAP)]
  transfers between devices with their start and end apart: 12 -> 13, of which waited for: 10 -> 9; matrix products, arithmetic and copies ran while one was open for 0% -> 0% of each run, Pallas kernels for 26% -> 28%
where the time goes in v6:
time: 134 us
  Pallas kernels  52.9 us (39%)
  starting transfers between devices  28.1 us (21%)
  blocking collectives  27.9 us (21%)
  waiting for transfers between devices  23.7 us (18%)
    all_to_all x1, blocking collectives, shards(): rows = lax.all_to_all(own, ('x', 'core'), 0, 0, tiled=True)  16.4 us
    ppermute x8, waiting for transfers between devices, exchange(): return lax.ppermute(value, (axis, 'core'), pairs)  16.1 us
    pallas_call x1, Pallas kernels, local(): pl.pallas_call(local_body, grid_spec=pltpu.PrefetchScalarGridSpec(num_sca...  12.5 us
    all_to_all x1, starting transfers between devices, shards(): lax.all_to_all(total.reshape(32, 32, HD), ('z', 'y'), 0, 0, tiled=True)  12 us
    all_to_all x1, blocking collectives, shards(): part = lax.all_to_all(part, 'z', 0, 0, tiled=True)  11.5 us
    pallas_call x1, Pallas kernels, project(): pl.pallas_call(project_body, grid_spec=pltpu.PrefetchScalarGridSpec(num_s...  9.82 us
    pallas_call x1, Pallas kernels, keep(): pl.pallas_call(keep_body, grid_spec=pltpu.PrefetchScalarGridSpec(num_scal...  8.62 us
    pallas_call x1, Pallas kernels, inputs_grad(): pl.pallas_call(inputs_body, grid=(NB,), in_specs=[block(3 * D), block(3 *...  8.09 us
  transfers between devices with their start and end apart: 13, of which 9 were waited for; matrix products, arithmetic and copies ran while one was open for 0% of the time, Pallas kernels for 28%

profile of v6, /device:TPU:1, one launch (start us, length us, event | category | flops | bytes accessed | tf_op | source)
XLA Modules:
  0.0 133.9 jit_solution(17134799600278528893)
XLA Ops:
  0.6 0.7 stack.51.at_ref.at
  1.3 9.8 %project.1 = (bf16[1024,1536]{1,0:T(8,128)(2,1)}, bf16[1024,512]{1,0:T(8,128)(2,1)}, f32[4,4,128,128]{3,2,1,0:T(8,128)}, f32[4,4,128,128]{3,2,1,0:T(8,128)}, f32[2,4,128,128]{3,2,1,0:T(8,128)}) custom-call(s32[11]{0:T(128)} %stack.51.at_ref.at, bf16[1024,1024]{1,0:T(8,128)(2,1)} %bitcast.19, bf16[1024,1536]{1,0:T(8,128)(2,1)} %w_ref.3, ...), custom_call_target="tpu_custom_call" | custom-call | tf_op jit(solution)/shard_map/project/pallas_call | solution.py:68
  11.2 12.0 %all-to-all-start = ((f32[32,32,128]{2,1,0:T(8,128)}), f32[32,32,128]{2,1,0:T(8,128)S(1)}, u32[]{:S(2)}, u32[]{:S(2)}) async-start(f32[32,32,128]{2,1,0:T(8,128)} %bitcast.24), calls=%async_computation | async-start | bytes 1048576 | tf_op jit(solution)/shard_map/all_to_all | solution.py:412
  23.2 0.0 copy-start.1
  23.2 12.5 %local.1 = (bf16[1024,1536]{1,0:T(8,128)(2,1)}, f32[1024,768]{1,0:T(8,128)}) custom-call(s32[11]{0:T(128)} %stack.51.at_ref.at, bf16[1024,1536]{1,0:T(8,128)(2,1)} %get-tuple-element.51.qkv_ref.refs_4_.refs_5_.refs_1_.refs_2_, bf16[1024,512]{1,0:T(8,128)(2,1)} %get-tuple-element.50.sg_ref.refs_3_.refs_0_, f32[4,4,128,128]{3,2,1,0:T(8,128)} %get-tuple-element.42.kv_ref, ...), custom_call_target="tpu_custom_call" | custom-call | flops 8000000000 | bytes 24000000 | tf_op jit(solution)/shard_map/local/pallas_call | solution.py:163
  35.7 3.8 %all-to-all-done.v_ref = f32[32,32,128]{2,1,0:T(8,128)S(1)} async-done(((f32[32,32,128]{2,1,0:T(8,128)}), f32[32,32,128]{2,1,0:T(8,128)S(1)}, u32[]{:S(2)}, u32[]{:S(2)}) %all-to-all-start) | async-done | bytes 524320 | tf_op jit(solution)/shard_map/all_to_all | solution.py:412
  39.5 2.4 %collective-permute-start = (f32[1024,768]{1,0:T(8,128)}, f32[1024,768]{1,0:T(8,128)}, u32[]{:S(2)}, u32[]{:S(2)}) collective-permute-start(f32[1024,768]{1,0:T(8,128)} %get-tuple-element.48), channel_id=1, source_target_pairs={{0,1},{1,0},{2,3},{3,2},{4,5},{5,4},{6,7},{7,6},{8,9},{9,8},{10,11... | collective-permute-start | bytes 9437192 | tf_op jit(solution)/shard_map/ppermute | solution.py:415
  41.9 0.0 copy-done.1
  41.9 1.7 %scan_states.1 = f32[32,32,128]{2,1,0:T(8,128)} custom-call(s32[11]{0:T(128)S(1)} %copy-done.1, f32[32,32,128]{2,1,0:T(8,128)S(1)} %all-to-all-done.v_ref), custom_call_target="tpu_custom_call" | custom-call | tf_op jit(solution)/shard_map/scan_states/pallas_call | solution.py:105
  43.5 4.4 %all-to-all-start.1 = ((f32[32,32,128]{2,1,0:T(8,128)}), f32[32,32,128]{2,1,0:T(8,128)S(1)}, u32[]{:S(2)}, u32[]{:S(2)}) async-start(f32[32,32,128]{2,1,0:T(8,128)} %scan_states.1), calls=%async_computation.1 | async-start | bytes 1048576 | tf_op jit(solution)/shard_map/all_to_all | solution.py:419
  47.9 5.6 %factors.1 = f32[1024,768]{1,0:T(8,128)} custom-call(s32[11]{0:T(128)} %stack.51.at_ref.at, bf16[1024,1024]{1,0:T(8,128)(2,1)} %bitcast.21, bf16[1024,512]{1,0:T(8,128)(2,1)} %get-tuple-element.50.sg_ref.refs_3_.refs_0_, bf16[1024,1536]{1,0:T(8,128)(2,1)} %get-tuple-element.51.qkv_ref.refs_4_.refs_5_.refs_1_.refs_2_, ...), custom_call_target="tpu_custom_call" | custom-call | flops 3000000000 | bytes 12000000 | tf_op jit(solution)/shard_map/factors/pallas_call | solution.py:199
  53.6 0.0 copy-start.2
  53.6 0.3 collective-permute-start.1
  53.9 0.0 collective-permute-done.r_ref
  53.9 8.6 %keep.1 = (f32[1024,768]{1,0:T(8,128)}, bf16[1024,768]{1,0:T(8,128)(2,1)}) custom-call(s32[11]{0:T(128)} %stack.51.at_ref.at, bf16[1024,1024]{1,0:T(8,128)(2,1)} %bitcast.22, f32[1024,768]{1,0:T(8,128)} %collective-permute-done.r_ref, bf16[1024,1536]{1,0:T(8,128)(2,1)} %get-tuple-element.49.refs_0_.refs_1_.refs_2_.loc_ref, ...), custom_call_target="tpu_custom_call" | custom-call | flops 40000000000 | bytes 16000000 | tf_op jit(solution)/shard_map/keep/pallas_call | solution.py:225
  62.5 2.3 %all-to-all-done.1 = f32[32,32,128]{2,1,0:T(8,128)S(1)} async-done(((f32[32,32,128]{2,1,0:T(8,128)}), f32[32,32,128]{2,1,0:T(8,128)S(1)}, u32[]{:S(2)}, u32[]{:S(2)}) %all-to-all-start.1) | async-done | bytes 524320 | tf_op jit(solution)/shard_map/all_to_all | solution.py:419
  64.7 0.0 copy-start
  64.8 0.0 copy-start.3
  64.8 1.9 %collective-permute-start.2 = (f32[2,4,128,128]{3,2,1,0:T(8,128)S(1)}, f32[2,4,128,128]{3,2,1,0:T(8,128)S(1)}, u32[]{:S(2)}, u32[]{:S(2)}) collective-permute-start(f32[2,4,128,128]{3,2,1,0:T(8,128)S(1)} %bitcast.16), channel_id=1, source_target_pairs={{0,1},{1,0},{2,3},{3,2},{4,5},{5,4},{6,7},{7,6},{8,9},{9,8},{10,11... | collective-permute-start | bytes 1572872 | tf_op jit(solution)/shard_map/ppermute | solution.py:426
  66.6 0.0 collective-permute-done.1.b_hbm
  66.6 1.5 %collective-permute-done.2.sb_ref = f32[2,4,128,128]{3,2,1,0:T(8,128)S(1)} collective-permute-done((f32[2,4,128,128]{3,2,1,0:T(8,128)S(1)}, f32[2,4,128,128]{3,2,1,0:T(8,128)S(1)}, u32[]{:S(2)}, u32[]{:S(2)}) %collective-permute-start.2) | collective-permute-done | bytes 524320 | tf_op jit(solution)/shard_map/ppermute | solution.py:426
  68.2 0.0 copy-done.2
  68.2 4.5 %finish.1 = (f32[8,4,2,8,384]{4,3,2,1,0:T(8,128)S(1)}, f32[8,4,2,8,384]{4,3,2,1,0:T(8,128)S(1)}, f32[8,2,4,8,384]{4,3,2,1,0:T(8,128)S(1)}, f32[8,2,4,8,384]{4,3,2,1,0:T(8,128)S(1)}) custom-call(s32[11]{0:T(128)S(1)} %copy-done.2, f32[1024,768]{1,0:T(8,128)} %get-tuple-element.54.w_hbm, bf16[1024,768]{1,0:T(8,128)(2,1)} %get-tuple-element.55.a_hbm, ...), custom_call_target="tpu_custom_call" | custom-call | flops 1000000000 | bytes 12000000 | tf_op jit(solution)/shard_map/finish/pallas_call | solution.py:284
  72.6 2.6 %collective-permute-start.3 = (f32[8,4,2,8,384]{4,3,2,1,0:T(8,128)S(1)}, f32[8,4,2,8,384]{4,3,2,1,0:T(8,128)S(1)}, u32[]{:S(2)}, u32[]{:S(2)}) collective-permute-start(f32[8,4,2,8,384]{4,3,2,1,0:T(8,128)S(1)} %get-tuple-element.57), channel_id=1, source_target_pairs={{0,2},{1,7},{2,0},{3,5},{4,6},{5,3},{6,4},{7,1},{8,10},{9,15},{10,... | collective-permute-start | bytes 2359304 | tf_op jit(solution)/shard_map/ppermute | solution.py:396
  75.2 1.8 %collective-permute-start.4 = (f32[8,2,4,8,384]{4,3,2,1,0:T(8,128)S(1)}, f32[8,2,4,8,384]{4,3,2,1,0:T(8,128)S(1)}, u32[]{:S(2)}, u32[]{:S(2)}) collective-permute-start(f32[8,2,4,8,384]{4,3,2,1,0:T(8,128)S(1)} %get-tuple-element.58), channel_id=1, source_target_pairs={{0,8},{1,25},{8,0},{9,17},{16,24},{17,9},{24,16},{25,1},{2,10},{3,... | collective-permute-start | bytes 2359304 | tf_op jit(solution)/shard_map/ppermute | solution.py:396
  77.0 0.0 copy-done
  77.0 0.0 copy-done.3
  77.0 8.1 %inputs_grad.1 = bf16[1024,1024]{1,0:T(8,128)(2,1)} custom-call(bf16[1024,1536]{1,0:T(8,128)(2,1)S(1)} %copy-done.3, bf16[1024,1536]{1,0:T(8,128)(2,1)} %get-tuple-element.51.qkv_ref.refs_4_.refs_5_.refs_1_.refs_2_, bf16[1024,512]{1,0:T(8,128)(2,1)S(1)} %copy-done, f32[2,4,128,128]{3,2,1,0:T(8,128)S(1)} %bitcast.18, bf16[1024,1536]{1,0:T(8,128)(2,1)} %w_ref.3), custom_call_target="tpu_custom_call" | custom-call | flops 5000000000 | bytes 14000000 | tf_op jit(solution)/shard_map/inputs_grad/pallas_call | solution.py:319
  85.1 0.0 collective-permute-done.3.r
  85.1 2.1 %collective-permute-done.4.r = f32[8,2,4,8,384]{4,3,2,1,0:T(8,128)S(1)} collective-permute-done((f32[8,2,4,8,384]{4,3,2,1,0:T(8,128)S(1)}, f32[8,2,4,8,384]{4,3,2,1,0:T(8,128)S(1)}, u32[]{:S(2)}, u32[]{:S(2)}) %collective-permute-start.4) | collective-permute-done | bytes 786464 | tf_op jit(solution)/shard_map/ppermute | solution.py:396
  87.3 0.1 add1y.1
  87.3 0.1 collective-permute-start.8
  87.4 0.1 add1x.1
  87.5 0.1 collective-permute-start.5
  87.6 6.7 %collective-permute-done.8.r = f32[8,4,8,384]{3,2,1,0:T(8,128)S(1)} collective-permute-done((f32[8,4,8,384]{3,2,1,0:T(8,128)S(1)}, f32[8,4,8,384]{3,2,1,0:T(8,128)S(1)}, u32[]{:S(2)}, u32[]{:S(2)}) %collective-permute-start.8) | collective-permute-done | bytes 393248 | tf_op jit(solution)/shard_map/ppermute | solution.py:396
  94.4 0.6 add2y.1
  94.9 0.4 collective-permute-start.9
  95.3 0.0 collective-permute-done.5.r
  95.3 0.6 add2x.1
  95.9 1.9 %collective-permute-start.6 = (f32[8,2,8,384]{3,2,1,0:T(8,128)S(1)}, f32[8,2,8,384]{3,2,1,0:T(8,128)S(1)}, u32[]{:S(2)}, u32[]{:S(2)}) collective-permute-start(f32[8,2,8,384]{3,2,1,0:T(8,128)S(1)} %get-tuple-element.65), channel_id=1, source_target_pairs={{0,8},{1,25},{8,0},{9,17},{16,24},{17,9},{24,16},{25,1},{2,10},{3,... | collective-permute-start | bytes 589832 | tf_op jit(solution)/shard_map/ppermute | solution.py:396
  97.8 2.9 %collective-permute-done.9.r = f32[8,2,8,384]{3,2,1,0:T(8,128)S(1)} collective-permute-done((f32[8,2,8,384]{3,2,1,0:T(8,128)S(1)}, f32[8,2,8,384]{3,2,1,0:T(8,128)S(1)}, u32[]{:S(2)}, u32[]{:S(2)}) %collective-permute-start.9) | collective-permute-done | bytes 196640 | tf_op jit(solution)/shard_map/ppermute | solution.py:396
  100.8 0.1 collective-permute-start.10
  100.9 0.8 collective-permute-done.6.r
  101.8 0.1 collective-permute-start.7
  101.9 2.5 %collective-permute-done.10.rq = f32[8,8,384]{2,1,0:T(8,128)S(1)} collective-permute-done((f32[8,8,384]{2,1,0:T(8,128)S(1)}, f32[8,8,384]{2,1,0:T(8,128)S(1)}, u32[]{:S(2)}, u32[]{:S(2)}) %collective-permute-start.10) | collective-permute-done | bytes 98336 | tf_op jit(solution)/shard_map/ppermute | solution.py:396
  104.3 1.0 collective-permute-done.7.rp
  105.3 11.5 %all_to_all.20.v = f32[8,8,768]{2,1,0:T(8,128)S(1)} all-to-all(f32[8,8,768]{2,1,0:T(8,128)S(1)} %add4.1), channel_id=1, replica_groups=mesh['z'=8,'y'=4,'x'=4,'core'=2] {'z'}, dimensions={0} | all-to-all | bytes 393216 | tf_op jit(solution)/shard_map/all_to_all | solution.py:445
  116.8 16.4 %all_to_all.21.v = f32[8,8,768]{2,1,0:T(8,128)S(1)} all-to-all(f32[8,8,768]{2,1,0:T(8,128)S(1)} %sum_z.1), channel_id=1, replica_groups=mesh['z'=8,'y'=4,'x'=4,'core'=2] {'x','core'}, dimensions={0} | all-to-all | bytes 393216 | tf_op jit(solution)/shard_map/all_to_all | solution.py:447
  133.2 0.7 place.1
  (4 shorter events, 0.1 us)
Async XLA Ops:
  11.2 28.3 %all-to-all-start = ((f32[32,32,128]{2,1,0:T(8,128)}), f32[32,32,128]{2,1,0:T(8,128)S(1)}, u32[]{:S(2)}, u32[]{:S(2)}) async-start(f32[32,32,128]{2,1,0:T(8,128)} %bitcast.24), calls=%async_computation | async-start | bytes 1048576 | tf_op jit(solution)/shard_map/all_to_all | solution.py:412
  23.2 18.7 %copy-start.1 = (s32[11]{0:T(128)S(1)}, s32[11]{0:T(128)}, u32[]{:S(2)}) copy-start(s32[11]{0:T(128)} %stack.51.at_ref.at) | copy-start | bytes 136
  39.5 14.4 %collective-permute-start = (f32[1024,768]{1,0:T(8,128)}, f32[1024,768]{1,0:T(8,128)}, u32[]{:S(2)}, u32[]{:S(2)}) collective-permute-start(f32[1024,768]{1,0:T(8,128)} %get-tuple-element.48), channel_id=1, source_target_pairs={{0,1},{1,0},{2,3},{3,2},{4,5},{5,4},{6,7},{7,6},{8,9},{9,8},{10,11... | collective-permute-start | bytes 9437192 | tf_op jit(solution)/shard_map/ppermute | solution.py:415
  43.5 21.2 %all-to-all-start.1 = ((f32[32,32,128]{2,1,0:T(8,128)}), f32[32,32,128]{2,1,0:T(8,128)S(1)}, u32[]{:S(2)}, u32[]{:S(2)}) async-start(f32[32,32,128]{2,1,0:T(8,128)} %scan_states.1), calls=%async_computation.1 | async-start | bytes 1048576 | tf_op jit(solution)/shard_map/all_to_all | solution.py:419
  53.6 14.6 %copy-start.2 = (s32[11]{0:T(128)S(1)}, s32[11]{0:T(128)}, u32[]{:S(2)}) copy-start(s32[11]{0:T(128)} %stack.51.at_ref.at) | copy-start | bytes 136
  53.6 13.1 %collective-permute-start.1 = (f32[1024,768]{1,0:T(8,128)}, f32[1024,768]{1,0:T(8,128)}, u32[]{:S(2)}, u32[]{:S(2)}) collective-permute-start(f32[1024,768]{1,0:T(8,128)} %factors.1), channel_id=1, source_target_pairs={{0,1},{1,0},{2,3},{3,2},{4,5},{5,4},{6,7},{7,6},{8,9},{9,8},{10,11... | collective-permute-start | bytes 9437192 | tf_op jit(solution)/shard_map/ppermute | solution.py:421
  64.7 12.3 %copy-start = (bf16[1024,512]{1,0:T(8,128)(2,1)S(1)}, bf16[1024,512]{1,0:T(8,128)(2,1)}, u32[]{:S(2)}) copy-start(bf16[1024,512]{1,0:T(8,128)(2,1)} %get-tuple-element.50.sg_ref.refs_3_.refs_0_) | copy-start | bytes 3145732
  64.8 12.3 %copy-start.3 = (bf16[1024,1536]{1,0:T(8,128)(2,1)S(1)}, bf16[1024,1536]{1,0:T(8,128)(2,1)}, u32[]{:S(2)}) copy-start(bf16[1024,1536]{1,0:T(8,128)(2,1)} %get-tuple-element.49.refs_0_.refs_1_.refs_2_.loc_ref) | copy-start | bytes 9437188
  64.8 3.4 %collective-permute-start.2 = (f32[2,4,128,128]{3,2,1,0:T(8,128)S(1)}, f32[2,4,128,128]{3,2,1,0:T(8,128)S(1)}, u32[]{:S(2)}, u32[]{:S(2)}) collective-permute-start(f32[2,4,128,128]{3,2,1,0:T(8,128)S(1)} %bitcast.16), channel_id=1, source_target_pairs={{0,1},{1,0},{2,3},{3,2},{4,5},{5,4},{6,7},{7,6},{8,9},{9,8},{10,11... | collective-permute-start | bytes 1572872 | tf_op jit(solution)/shard_map/ppermute | solution.py:426
  72.6 12.5 %collective-permute-start.3 = (f32[8,4,2,8,384]{4,3,2,1,0:T(8,128)S(1)}, f32[8,4,2,8,384]{4,3,2,1,0:T(8,128)S(1)}, u32[]{:S(2)}, u32[]{:S(2)}) collective-permute-start(f32[8,4,2,8,384]{4,3,2,1,0:T(8,128)S(1)} %get-tuple-element.57), channel_id=1, source_target_pairs={{0,2},{1,7},{2,0},{3,5},{4,6},{5,3},{6,4},{7,1},{8,10},{9,15},{10,... | collective-permute-start | bytes 2359304 | tf_op jit(solution)/shard_map/ppermute | solution.py:396
  75.2 12.1 %collective-permute-start.4 = (f32[8,2,4,8,384]{4,3,2,1,0:T(8,128)S(1)}, f32[8,2,4,8,384]{4,3,2,1,0:T(8,128)S(1)}, u32[]{:S(2)}, u32[]{:S(2)}) collective-permute-start(f32[8,2,4,8,384]{4,3,2,1,0:T(8,128)S(1)} %get-tuple-element.58), channel_id=1, source_target_pairs={{0,8},{1,25},{8,0},{9,17},{16,24},{17,9},{24,16},{25,1},{2,10},{3,... | collective-permute-start | bytes 2359304 | tf_op jit(solution)/shard_map/ppermute | solution.py:396
  87.3 7.0 %collective-permute-start.8 = (f32[8,4,8,384]{3,2,1,0:T(8,128)S(1)}, f32[8,4,8,384]{3,2,1,0:T(8,128)S(1)}, u32[]{:S(2)}, u32[]{:S(2)}) collective-permute-start(f32[8,4,8,384]{3,2,1,0:T(8,128)S(1)} %get-tuple-element.71), channel_id=1, source_target_pairs={{0,24},{1,9},{8,16},{9,1},{16,8},{17,25},{24,0},{25,17},{2,26},{3,... | collective-permute-start | bytes 1179656 | tf_op jit(solution)/shard_map/ppermute | solution.py:396
  87.5 7.8 %collective-permute-start.5 = (f32[8,4,8,384]{3,2,1,0:T(8,128)S(1)}, f32[8,4,8,384]{3,2,1,0:T(8,128)S(1)}, u32[]{:S(2)}, u32[]{:S(2)}) collective-permute-start(f32[8,4,8,384]{3,2,1,0:T(8,128)S(1)} %get-tuple-element.63), channel_id=1, source_target_pairs={{0,6},{1,3},{2,4},{3,1},{4,2},{5,7},{6,0},{7,5},{8,14},{9,11},{10,... | collective-permute-start | bytes 1179656 | tf_op jit(solution)/shard_map/ppermute | solution.py:396
  94.9 5.8 %collective-permute-start.9 = (f32[8,2,8,384]{3,2,1,0:T(8,128)S(1)}, f32[8,2,8,384]{3,2,1,0:T(8,128)S(1)}, u32[]{:S(2)}, u32[]{:S(2)}) collective-permute-start(f32[8,2,8,384]{3,2,1,0:T(8,128)S(1)} %get-tuple-element.73), channel_id=1, source_target_pairs={{0,2},{1,7},{2,0},{3,5},{4,6},{5,3},{6,4},{7,1},{8,10},{9,15},{10,... | collective-permute-start | bytes 589832 | tf_op jit(solution)/shard_map/ppermute | solution.py:396
  95.9 5.8 %collective-permute-start.6 = (f32[8,2,8,384]{3,2,1,0:T(8,128)S(1)}, f32[8,2,8,384]{3,2,1,0:T(8,128)S(1)}, u32[]{:S(2)}, u32[]{:S(2)}) collective-permute-start(f32[8,2,8,384]{3,2,1,0:T(8,128)S(1)} %get-tuple-element.65), channel_id=1, source_target_pairs={{0,8},{1,25},{8,0},{9,17},{16,24},{17,9},{24,16},{25,1},{2,10},{3,... | collective-permute-start | bytes 589832 | tf_op jit(solution)/shard_map/ppermute | solution.py:396
  100.8 3.6 %collective-permute-start.10 = (f32[8,8,384]{2,1,0:T(8,128)S(1)}, f32[8,8,384]{2,1,0:T(8,128)S(1)}, u32[]{:S(2)}, u32[]{:S(2)}) collective-permute-start(f32[8,8,384]{2,1,0:T(8,128)S(1)} %get-tuple-element.75), channel_id=1, source_target_pairs={{0,6},{1,3},{2,4},{3,1},{4,2},{5,7},{6,0},{7,5},{8,14},{9,11},{10,... | collective-permute-start | bytes 294920 | tf_op jit(solution)/shard_map/ppermute | solution.py:396
  101.8 3.6 %collective-permute-start.7 = (f32[8,8,384]{2,1,0:T(8,128)S(1)}, f32[8,8,384]{2,1,0:T(8,128)S(1)}, u32[]{:S(2)}, u32[]{:S(2)}) collective-permute-start(f32[8,8,384]{2,1,0:T(8,128)S(1)} %get-tuple-element.67), channel_id=1, source_target_pairs={{0,24},{1,9},{8,16},{9,1},{16,8},{17,25},{24,0},{25,17},{2,26},{3,... | collective-permute-start | bytes 294920 | tf_op jit(solution)/shard_map/ppermute | solution.py:396

commit v7 on v6

--- a/solution.py
+++ b/solution.py
@@ -42,10 +42,11 @@
     return pl.ds(part * D + h * HD, HD)
 
 
-def project_body(at_ref, x_ref, w_ref, g_ref, qkv_ref, sg_ref, kv_ref, qg_ref, total_ref):
+def project_body(x_ref, w_ref, g_ref, qkv_ref, sg_ref, kv_ref, qg_ref, total_ref):
     n = pl.program_id(0)
+    first = (lax.axis_index("z") * 4 + lax.axis_index("y")) * TOK
     qkv_ref[...] = dot(x_ref[...], w_ref[...], NN).astype(BF16)
-    pos = (at_ref[9] + n * CH + lax.broadcasted_iota(jnp.int32, (CH, 1), 0)).astype(F32)
+    pos = (first + n * CH + lax.broadcasted_iota(jnp.int32, (CH, 1), 0)).astype(F32)
     factor = 1.0 / jnp.sqrt(jnp.float32(HD) * (pos + 1.0))
     sg_ref[...] = (g_ref[...].astype(F32) * factor).astype(BF16)
 
@@ -62,23 +63,20 @@
         total_ref[1, h] += qg
 
 
-def project(at, x, w, g):
-    block = lambda cols: pl.BlockSpec((CH, cols), lambda n, s: (n, 0))
-    sums = pl.BlockSpec((1, H, HD, HD), lambda n, s: (n, 0, 0, 0))
+def project(x, w, g):
+    block = lambda cols: pl.BlockSpec((CH, cols), lambda n: (n, 0))
+    sums = pl.BlockSpec((1, H, HD, HD), lambda n: (n, 0, 0, 0))
     return pl.pallas_call(
         project_body,
-        grid_spec=pltpu.PrefetchScalarGridSpec(
-            num_scalar_prefetch=1,
             grid=(NB,),
-            in_specs=[block(DM), pl.BlockSpec((DM, 3 * D), lambda n, s: (0, 0)), block(D)],
+            in_specs=[block(DM), pl.BlockSpec((DM, 3 * D), lambda n: (0, 0)), block(D)],
             out_specs=[
                 block(3 * D),
                 block(D),
                 sums,
                 sums,
-                pl.BlockSpec((2, H, HD, HD), lambda n, s: (0, 0, 0, 0)),
+                pl.BlockSpec((2, H, HD, HD), lambda n: (0, 0, 0, 0)),
             ],
-        ),
         out_shape=[
             jax.ShapeDtypeStruct((TOK, 3 * D), BF16),
             jax.ShapeDtypeStruct((TOK, D), BF16),
@@ -88,28 +86,30 @@
         ],
         compiler_params=params(60),
         name="project",
-    )(at, x, w, g)
-
-
-def scan_body(count, at_ref, v_ref, o_ref):
+    )(x, w, g)
+
+
+def scan_body(count, v_ref, o_ref):
+    back = lax.axis_index("z") >= 4
+
 
     def step(t, so_far):
-        i = jnp.where(at_ref[10] == 1, count - 1 - t, t)
+        i = jnp.where(back, count - 1 - t, t)
         o_ref[i] = so_far
         return so_far + v_ref[i]
 
     lax.fori_loop(0, count, step, jnp.zeros(v_ref.shape[1:], F32))
 
 
-def scan_states(at, v):
+def scan_states(v):
     return pl.pallas_call(
         functools.partial(scan_body, v.shape[0]),
-        in_specs=[pl.BlockSpec(memory_space=pltpu.SMEM), pl.BlockSpec(memory_space=pltpu.VMEM)],
+        in_specs=[pl.BlockSpec(memory_space=pltpu.VMEM)],
         out_specs=pl.BlockSpec(memory_space=pltpu.VMEM),
         out_shape=jax.ShapeDtypeStruct(v.shape, F32),
         compiler_params=params(4),
         name="scan_states",
-    )(at, v)
+    )(v)
 
 
 def local_body(at_ref, qkv_ref, sg_ref, kv_ref, qg_ref, x_hbm, loc_ref, give_ref, from_ref, x_ref, sem):
@@ -206,7 +206,7 @@
         ),
         out_shape=jax.ShapeDtypeStruct((DM, 768), F32),
         compiler_params=params(60),
-        cost_estimate=cost(3e9, 12e6),
+        cost_estimate=cost(60e9, 12e6),
         name="factors",
     )(at, x, *(a for a, _ in sources))
 
@@ -237,13 +237,15 @@
     )(at, x, arrived, *(a for a, _ in sources))
 
 
-def pick(at_ref, axis):
-    mine, far, first, second = (at_ref[1 + 4 * axis + i] for i in range(4))
-    return (mine, second), (first, far)
-
-
-def finish_body(at_ref, w_hbm, a_hbm, b_hbm, sa_ref, sb_ref, kx_ref, sx_ref, ky_ref, sy_ref, w_ref, a_ref, b_ref, s_ref, sems):
-    core = at_ref[0]
+def pick(axis):
+    mine = lax.axis_index(axis)
+    first = jnp.where(lax.axis_index("core") == 0, 1, 3)
+    second = 4 - first
+    return (mine, mine ^ second), (mine ^ first, mine ^ first ^ second)
+
+
+def finish_body(w_hbm, a_hbm, b_hbm, sa_ref, sb_ref, kx_ref, sx_ref, ky_ref, sy_ref, w_ref, a_ref, b_ref, s_ref, sems):
+    core = lax.axis_index("core")
     copies = []
     for j in range(3):
         cols = pl.ds(j * 256, 256)
@@ -268,22 +270,22 @@
             term += dot(far, sb_ref[kind, h].astype(BF16), dims)
             s_ref[j, :, :, :, :, cols] = (w_ref[j, :, cols] + term).reshape(8, 4, 4, 8, HD)
         lanes = slice(j * HD, (j + 1) * HD)
-        kept, sent = pick(at_ref, 0)
+        kept, sent = pick("x")
         for i in range(2):
             kx_ref[:, :, i, :, lanes] = s_ref[j, :, :, kept[i], :, 0:128]
             sx_ref[:, :, i, :, lanes] = s_ref[j, :, :, sent[i], :, 0:128]
-        kept, sent = pick(at_ref, 1)
+        kept, sent = pick("y")
         for i in range(2):
             ky_ref[:, i, :, :, lanes] = s_ref[j, :, kept[i], :, :, 128:256]
             sy_ref[:, i, :, :, lanes] = s_ref[j, :, sent[i], :, :, 128:256]
 
 
-def finish(at, w, a, b, sa, sb):
+def finish(w, a, b, sa, sb):
     vmem = pl.BlockSpec(memory_space=pltpu.VMEM)
     hbm = pl.BlockSpec(memory_space=pltpu.HBM)
     return pl.pallas_call(
         finish_body,
-        in_specs=[pl.BlockSpec(memory_space=pltpu.SMEM), hbm, hbm, hbm, vmem, vmem],
+        in_specs=[hbm, hbm, hbm, vmem, vmem],
         out_specs=[vmem] * 4,
         out_shape=[jax.ShapeDtypeStruct((8, 4, 2, 8, 384), F32)] * 2
         + [jax.ShapeDtypeStruct((8, 2, 4, 8, 384), F32)] * 2,
@@ -297,7 +299,7 @@
         compiler_params=params(49),
         cost_estimate=cost(1e9, 12e6),
         name="finish",
-    )(at, w, a, b, sa, sb)
+    )(w, a, b, sa, sb)
 
 
 def inputs_body(loc_ref, qkv_ref, sg_ref, s_ref, w_ref, o_ref, d_ref):
@@ -355,8 +357,8 @@
     so[...] = k[at + (1,)] + r[at + (1,)]
 
 
-def add2_body(axis, at, k, r, ko, so):
-    kept, sent = pick(at, axis)
+def add2_body(axis, k, r, ko, so):
+    kept, sent = pick(axis)
     for i in range(2):
         ko[:, i] = k[:, kept[i]] + r[:, kept[i]]
         so[:, i] = k[:, sent[i]] + r[:, sent[i]]
@@ -398,23 +400,14 @@
 
 def shards(inputs, weights, out_grad):
     x = inputs[0]
-    z_at, y_at, x_at, core = (lax.axis_index(a) for a in ("z", "y", "x", "core"))
-    tm_at = z_at * 4 + y_at
-    first = jnp.where(core == 0, 1, 3)
-    second = 4 - first
-    at = jnp.stack(
-        [core]
-        + [v for i in (x_at, y_at) for v in (i, i ^ first ^ second, i ^ first, i ^ second)]
-        + [tm_at * TOK, (tm_at >= 16).astype(jnp.int32)]
-    ).astype(jnp.int32)
-
-    qkv, sg, kv, qg, total = project(at, x, weights, out_grad[0])
+    at = lax.axis_index("core").astype(jnp.int32)[None]
+
+    qkv, sg, kv, qg, total = project(x, weights, out_grad[0])
     slices = lax.all_to_all(total.reshape(32, 32, HD), ("z", "y"), 0, 0, tiled=True)
     loc, given = local(at, qkv, sg, kv, qg, x)
-    slices, given = lax.optimization_barrier((slices, given))
     local_in = lax.ppermute(given, "core", SWAP)
-
-    scanned = scan_states(at, slices)
+    slices, loc = lax.optimization_barrier((slices, loc))
+    scanned = scan_states(slices)
     scanned, sg, qkv, loc = lax.optimization_barrier((scanned, sg, qkv, loc))
     states = lax.all_to_all(scanned, ("z", "y"), 0, 0, tiled=True)
     given = factors(at, x, [(sg, 0), (qkv, 4), (qkv, 2)])
@@ -424,7 +417,7 @@
 
     states = states.reshape(2, H, HD, HD)
     states_in = lax.ppermute(states, "core", SWAP)
-    kx, sx, ky, sy = finish(at, both, mine, factors_in, states, states_in)
+    kx, sx, ky, sy = finish(both, mine, factors_in, states, states_in)
     rx = exchange(sx, "x", 0)
     ry = exchange(sy, "y", 0)
     record_grad = inputs_grad(loc, qkv, sg, states, weights)
@@ -433,9 +426,9 @@
     rp = exchange(sp, "x", 1)
     kq, sq = whole_call(add1_body, "add1y", [(8, 4, 8, 384)] * 2, ky, ry)
     rq = exchange(sq, "y", 1)
-    kp, sp = whole_call(functools.partial(add2_body, 1), "add2x", [(8, 2, 8, 384)] * 2, at, kp, rp)
+    kp, sp = whole_call(functools.partial(add2_body, "y"), "add2x", [(8, 2, 8, 384)] * 2, kp, rp)
     rp = exchange(sp, "y", 0)
-    kq, sq = whole_call(functools.partial(add2_body, 0), "add2y", [(8, 2, 8, 384)] * 2, at, kq, rq)
+    kq, sq = whole_call(functools.partial(add2_body, "x"), "add2y", [(8, 2, 8, 384)] * 2, kq, rq)
     rq = exchange(sq, "x", 0)
     kp, sp = whole_call(add3_body, "add3x", [(8, 8, 384)] * 2, kp, rp)
     rp = exchange(sp, "y", 1)

time: 134 us -> 130 us (0.970)
  Pallas kernels: 52.9 us -> 47.9 us
  waiting for transfers between devices: 23.7 us -> 21.1 us
  starting transfers between devices: 28.1 us -> 30.1 us
    unnamed x8 -> x4, local copies, waits for them, and re-layouts: 0.02 us -> 1.89 us
    ppermute x8, waiting for transfers between devices: 16.1 us -> 14.2 us  [exchange(): return lax.ppermute(value, (axis, 'core'), pairs)]
    all_to_all x1, starting transfers between devices: 4.41 us -> 6.03 us  [shards(): states = lax.all_to_all(scanned, ('z', 'y'), 0, 0, tiled=True)]
    ppermute x1, starting transfers between devices: 2.41 us -> 1.05 us  [shards(): local_in = lax.ppermute(given, 'core', SWAP)]
  transfers between devices with their start and end apart: 13 -> 13, of which waited for: 9 -> 9; matrix products, arithmetic and copies ran while one was open for 0% -> 0% of each run, Pallas kernels for 28% -> 26%
where the time goes in v7:
time: 130 us
  Pallas kernels  47.9 us (37%)
  starting transfers between devices  30.1 us (23%)
  blocking collectives  28.1 us (22%)
  waiting for transfers between devices  21.1 us (16%)
  local copies, waits for them, and re-layouts  1.89 us (1%)
    all_to_all x1, blocking collectives, shards(): rows = lax.all_to_all(own, ('x', 'core'), 0, 0, tiled=True)  16.7 us
    ppermute x8, waiting for transfers between devices, exchange(): return lax.ppermute(value, (axis, 'core'), pairs)  14.2 us
    all_to_all x1, starting transfers between devices, shards(): lax.all_to_all(total.reshape(32, 32, HD), ('z', 'y'), 0, 0, tiled=True)  12 us
    pallas_call x1, Pallas kernels, local(): pl.pallas_call(local_body, grid_spec=pltpu.PrefetchScalarGridSpec(num_sca...  11.8 us
    all_to_all x1, blocking collectives, shards(): part = lax.all_to_all(part, 'z', 0, 0, tiled=True)  11.4 us
    pallas_call x1, Pallas kernels, project(): pl.pallas_call(project_body, grid=(NB,), in_specs=[block(DM), pl.BlockSpe...  9.22 us
    pallas_call x1, Pallas kernels, inputs_grad(): pl.pallas_call(inputs_body, grid=(NB,), in_specs=[block(3 * D), block(3 *...  8.06 us
    pallas_call x1, Pallas kernels, keep(): pl.pallas_call(keep_body, grid_spec=pltpu.PrefetchScalarGridSpec(num_scal...  7.97 us
  transfers between devices with their start and end apart: 13, of which 9 were waited for; matrix products, arithmetic and copies ran while one was open for 0% of the time, Pallas kernels for 26%

profile of v7, /device:TPU:1, one launch (start us, length us, event | category | flops | bytes accessed | tf_op | source)
XLA Modules:
  0.0 129.8 jit_solution(2948542286311645414)
XLA Ops:
  0.6 9.2 %project.1 = (bf16[1024,1536]{1,0:T(8,128)(2,1)}, bf16[1024,512]{1,0:T(8,128)(2,1)}, f32[4,4,128,128]{3,2,1,0:T(8,128)}, f32[4,4,128,128]{3,2,1,0:T(8,128)}, f32[2,4,128,128]{3,2,1,0:T(8,128)}) custom-call(bf16[1024,1024]{1,0:T(8,128)(2,1)} %bitcast.9, bf16[1024,1536]{1,0:T(8,128)(2,1)} %w_ref.3, bf16[1024,512]{1,0:T(8,128)(2,1)} %bitcast.13), custom_call_target="tpu_custom_call" | custom-call | tf_op jit(solution)/shard_map/project/pallas_call | solution.py:69
  9.9 12.0 %all-to-all-start = ((f32[32,32,128]{2,1,0:T(8,128)}), f32[32,32,128]{2,1,0:T(8,128)S(1)}, u32[]{:S(2)}, u32[]{:S(2)}) async-start(f32[32,32,128]{2,1,0:T(8,128)} %bitcast.14), calls=%async_computation | async-start | bytes 1048576 | tf_op jit(solution)/shard_map/all_to_all | solution.py:406
  21.9 11.8 %local.1 = (bf16[1024,1536]{1,0:T(8,128)(2,1)}, f32[1024,768]{1,0:T(8,128)}) custom-call(s32[1]{0:T(128)} %bitcast.3.at_ref, bf16[1024,1536]{1,0:T(8,128)(2,1)} %get-tuple-element.51.qkv_ref.refs_4_.refs_5_.refs_1_.refs_2_, bf16[1024,512]{1,0:T(8,128)(2,1)} %get-tuple-element.50.sg_ref.refs_3_.refs_0_, f32[4,4,128,128]{3,2,1,0:T(8,128)} %get-tuple-element.42.kv_ref, ...), custom_call_target="tpu_custom_call" | custom-call | flops 8000000000 | bytes 24000000 | tf_op jit(solution)/shard_map/local/pallas_call | solution.py:163
  33.7 1.0 collective-permute-start
  34.7 3.5 %all-to-all-done.v_ref = f32[32,32,128]{2,1,0:T(8,128)S(1)} async-done(((f32[32,32,128]{2,1,0:T(8,128)}), f32[32,32,128]{2,1,0:T(8,128)S(1)}, u32[]{:S(2)}, u32[]{:S(2)}) %all-to-all-start) | async-done | bytes 524320 | tf_op jit(solution)/shard_map/all_to_all | solution.py:406
  38.2 1.0 scan_states.1
  39.2 6.0 %all-to-all-start.1 = ((f32[32,32,128]{2,1,0:T(8,128)}), f32[32,32,128]{2,1,0:T(8,128)S(1)}, u32[]{:S(2)}, u32[]{:S(2)}) async-start(f32[32,32,128]{2,1,0:T(8,128)} %scan_states.1), calls=%async_computation.1 | async-start | bytes 1048576 | tf_op jit(solution)/shard_map/all_to_all | solution.py:412
  45.2 5.0 %factors.1 = f32[1024,768]{1,0:T(8,128)} custom-call(s32[1]{0:T(128)} %bitcast.3.at_ref, bf16[1024,1024]{1,0:T(8,128)(2,1)} %bitcast.11, bf16[1024,512]{1,0:T(8,128)(2,1)} %get-tuple-element.50.sg_ref.refs_3_.refs_0_, bf16[1024,1536]{1,0:T(8,128)(2,1)} %get-tuple-element.51.qkv_ref.refs_4_.refs_5_.refs_1_.refs_2_, ...), custom_call_target="tpu_custom_call" | custom-call | flops 60000002048 | bytes 12000000 | tf_op jit(solution)/shard_map/factors/pallas_call | solution.py:199
  50.2 1.0 collective-permute-start.1
  51.2 0.0 collective-permute-done.r_ref
  51.2 8.0 %keep.1 = (f32[1024,768]{1,0:T(8,128)}, bf16[1024,768]{1,0:T(8,128)(2,1)}) custom-call(s32[1]{0:T(128)} %bitcast.3.at_ref, bf16[1024,1024]{1,0:T(8,128)(2,1)} %bitcast.12, f32[1024,768]{1,0:T(8,128)} %collective-permute-done.r_ref, bf16[1024,1536]{1,0:T(8,128)(2,1)} %get-tuple-element.49.refs_0_.refs_1_.refs_2_.loc_ref, ...), custom_call_target="tpu_custom_call" | custom-call | flops 40000000000 | bytes 16000000 | tf_op jit(solution)/shard_map/keep/pallas_call | solution.py:225
  59.2 1.9 %all-to-all-done.1 = f32[32,32,128]{2,1,0:T(8,128)S(1)} async-done(((f32[32,32,128]{2,1,0:T(8,128)}), f32[32,32,128]{2,1,0:T(8,128)S(1)}, u32[]{:S(2)}, u32[]{:S(2)}) %all-to-all-start.1) | async-done | bytes 524320 | tf_op jit(solution)/shard_map/all_to_all | solution.py:412
  61.1 0.0 copy-start
  61.1 2.8 %collective-permute-start.2 = (f32[2,4,128,128]{3,2,1,0:T(8,128)S(1)}, f32[2,4,128,128]{3,2,1,0:T(8,128)S(1)}, u32[]{:S(2)}, u32[]{:S(2)}) collective-permute-start(f32[2,4,128,128]{3,2,1,0:T(8,128)S(1)} %bitcast.6), channel_id=1, source_target_pairs={{0,1},{1,0},{2,3},{3,2},{4,5},{5,4},{6,7},{7,6},{8,9},{9,8},{10,11... | collective-permute-start | bytes 1572872 | tf_op jit(solution)/shard_map/ppermute | solution.py:419
  63.9 1.5 %collective-permute-done.2.sb_ref = f32[2,4,128,128]{3,2,1,0:T(8,128)S(1)} collective-permute-done((f32[2,4,128,128]{3,2,1,0:T(8,128)S(1)}, f32[2,4,128,128]{3,2,1,0:T(8,128)S(1)}, u32[]{:S(2)}, u32[]{:S(2)}) %collective-permute-start.2) | collective-permute-done | bytes 524320 | tf_op jit(solution)/shard_map/ppermute | solution.py:419
  65.4 0.0 collective-permute-done.1.b_hbm
  65.4 3.9 %finish.1 = (f32[8,4,2,8,384]{4,3,2,1,0:T(8,128)S(1)}, f32[8,4,2,8,384]{4,3,2,1,0:T(8,128)S(1)}, f32[8,2,4,8,384]{4,3,2,1,0:T(8,128)S(1)}, f32[8,2,4,8,384]{4,3,2,1,0:T(8,128)S(1)}) custom-call(f32[1024,768]{1,0:T(8,128)} %get-tuple-element.54.w_hbm, bf16[1024,768]{1,0:T(8,128)(2,1)} %get-tuple-element.55.a_hbm, f32[1024,768]{1,0:T(8,128)} %collective-permute-done.1.b_hbm, ...), custom_call_target="tpu_custom_call" | custom-call | flops 1000000000 | bytes 12000000 | tf_op jit(solution)/shard_map/finish/pallas_call | solution.py:286
  69.4 2.6 %collective-permute-start.3 = (f32[8,4,2,8,384]{4,3,2,1,0:T(8,128)S(1)}, f32[8,4,2,8,384]{4,3,2,1,0:T(8,128)S(1)}, u32[]{:S(2)}, u32[]{:S(2)}) collective-permute-start(f32[8,4,2,8,384]{4,3,2,1,0:T(8,128)S(1)} %get-tuple-element.57), channel_id=1, source_target_pairs={{0,2},{1,7},{2,0},{3,5},{4,6},{5,3},{6,4},{7,1},{8,10},{9,15},{10,... | collective-permute-start | bytes 2359304 | tf_op jit(solution)/shard_map/ppermute | solution.py:398
  72.0 1.8 %collective-permute-start.4 = (f32[8,2,4,8,384]{4,3,2,1,0:T(8,128)S(1)}, f32[8,2,4,8,384]{4,3,2,1,0:T(8,128)S(1)}, u32[]{:S(2)}, u32[]{:S(2)}) collective-permute-start(f32[8,2,4,8,384]{4,3,2,1,0:T(8,128)S(1)} %get-tuple-element.58), channel_id=1, source_target_pairs={{0,8},{1,25},{8,0},{9,17},{16,24},{17,9},{24,16},{25,1},{2,10},{3,... | collective-permute-start | bytes 2359304 | tf_op jit(solution)/shard_map/ppermute | solution.py:398
  73.8 0.0 copy-done
  73.8 0.0 copy-start.1
  73.8 1.9 %copy-done.1 = bf16[1024,1536]{1,0:T(8,128)(2,1)S(1)} copy-done((bf16[1024,1536]{1,0:T(8,128)(2,1)S(1)}, bf16[1024,1536]{1,0:T(8,128)(2,1)}, u32[]{:S(2)}) %copy-start.1) | copy-done | bytes 3145752
  75.7 8.1 %inputs_grad.1 = bf16[1024,1024]{1,0:T(8,128)(2,1)} custom-call(bf16[1024,1536]{1,0:T(8,128)(2,1)S(1)} %copy-done.1, bf16[1024,1536]{1,0:T(8,128)(2,1)} %get-tuple-element.51.qkv_ref.refs_4_.refs_5_.refs_1_.refs_2_, bf16[1024,512]{1,0:T(8,128)(2,1)S(1)} %copy-done, f32[2,4,128,128]{3,2,1,0:T(8,128)S(1)} %bitcast.8, bf16[1024,1536]{1,0:T(8,128)(2,1)} %w_ref.3), custom_call_target="tpu_custom_call" | custom-call | flops 5000000000 | bytes 14000000 | tf_op jit(solution)/shard_map/inputs_grad/pallas_call | solution.py:321
  83.7 0.0 collective-permute-done.3.r
  83.7 0.3 collective-permute-done.4.r
  84.0 0.1 add1y.1
  84.1 0.1 collective-permute-start.8
  84.2 0.1 add1x.1
  84.3 0.1 collective-permute-start.5
  84.4 6.7 %collective-permute-done.8.r = f32[8,4,8,384]{3,2,1,0:T(8,128)S(1)} collective-permute-done((f32[8,4,8,384]{3,2,1,0:T(8,128)S(1)}, f32[8,4,8,384]{3,2,1,0:T(8,128)S(1)}, u32[]{:S(2)}, u32[]{:S(2)}) %collective-permute-start.8) | collective-permute-done | bytes 393248 | tf_op jit(solution)/shard_map/ppermute | solution.py:398
  91.1 0.4 collective-permute-start.9
  91.5 0.0 collective-permute-done.5.r
  91.6 1.9 %collective-permute-start.6 = (f32[8,2,8,384]{3,2,1,0:T(8,128)S(1)}, f32[8,2,8,384]{3,2,1,0:T(8,128)S(1)}, u32[]{:S(2)}, u32[]{:S(2)}) collective-permute-start(f32[8,2,8,384]{3,2,1,0:T(8,128)S(1)} %get-tuple-element.65), channel_id=1, source_target_pairs={{0,8},{1,25},{8,0},{9,17},{16,24},{17,9},{24,16},{25,1},{2,10},{3,... | collective-permute-start | bytes 589832 | tf_op jit(solution)/shard_map/ppermute | solution.py:398
  93.5 3.5 %collective-permute-done.9.r = f32[8,2,8,384]{3,2,1,0:T(8,128)S(1)} collective-permute-done((f32[8,2,8,384]{3,2,1,0:T(8,128)S(1)}, f32[8,2,8,384]{3,2,1,0:T(8,128)S(1)}, u32[]{:S(2)}, u32[]{:S(2)}) %collective-permute-start.9) | collective-permute-done | bytes 196640 | tf_op jit(solution)/shard_map/ppermute | solution.py:398
  97.0 0.1 collective-permute-start.10
  97.1 0.3 collective-permute-done.6.r
  97.4 0.1 collective-permute-start.7
  97.5 3.0 %collective-permute-done.10.rq = f32[8,8,384]{2,1,0:T(8,128)S(1)} collective-permute-done((f32[8,8,384]{2,1,0:T(8,128)S(1)}, f32[8,8,384]{2,1,0:T(8,128)S(1)}, u32[]{:S(2)}, u32[]{:S(2)}) %collective-permute-start.10) | collective-permute-done | bytes 98336 | tf_op jit(solution)/shard_map/ppermute | solution.py:398
  100.5 0.4 collective-permute-done.7.rp
  101.0 11.4 %all_to_all.20.v = f32[8,8,768]{2,1,0:T(8,128)S(1)} all-to-all(f32[8,8,768]{2,1,0:T(8,128)S(1)} %add4.1), channel_id=1, replica_groups=mesh['z'=8,'y'=4,'x'=4,'core'=2] {'z'}, dimensions={0} | all-to-all | bytes 393216 | tf_op jit(solution)/shard_map/all_to_all | solution.py:438
  112.4 16.7 %all_to_all.21.v = f32[8,8,768]{2,1,0:T(8,128)S(1)} all-to-all(f32[8,8,768]{2,1,0:T(8,128)S(1)} %sum_z.1), channel_id=1, replica_groups=mesh['z'=8,'y'=4,'x'=4,'core'=2] {'x','core'}, dimensions={0} | all-to-all | bytes 393216 | tf_op jit(solution)/shard_map/all_to_all | solution.py:440
  129.1 0.7 place.1
  (6 shorter events, 0.2 us)
Async XLA Ops:
  9.9 28.3 %all-to-all-start = ((f32[32,32,128]{2,1,0:T(8,128)}), f32[32,32,128]{2,1,0:T(8,128)S(1)}, u32[]{:S(2)}, u32[]{:S(2)}) async-start(f32[32,32,128]{2,1,0:T(8,128)} %bitcast.14), calls=%async_computation | async-start | bytes 1048576 | tf_op jit(solution)/shard_map/all_to_all | solution.py:406
  33.7 17.5 %collective-permute-start = (f32[1024,768]{1,0:T(8,128)}, f32[1024,768]{1,0:T(8,128)}, u32[]{:S(2)}, u32[]{:S(2)}) collective-permute-start(f32[1024,768]{1,0:T(8,128)} %get-tuple-element.48), channel_id=1, source_target_pairs={{0,1},{1,0},{2,3},{3,2},{4,5},{5,4},{6,7},{7,6},{8,9},{9,8},{10,11... | collective-permute-start | bytes 9437192 | tf_op jit(solution)/shard_map/ppermute | solution.py:408
  39.2 21.9 %all-to-all-start.1 = ((f32[32,32,128]{2,1,0:T(8,128)}), f32[32,32,128]{2,1,0:T(8,128)S(1)}, u32[]{:S(2)}, u32[]{:S(2)}) async-start(f32[32,32,128]{2,1,0:T(8,128)} %scan_states.1), calls=%async_computation.1 | async-start | bytes 1048576 | tf_op jit(solution)/shard_map/all_to_all | solution.py:412
  50.2 15.2 %collective-permute-start.1 = (f32[1024,768]{1,0:T(8,128)}, f32[1024,768]{1,0:T(8,128)}, u32[]{:S(2)}, u32[]{:S(2)}) collective-permute-start(f32[1024,768]{1,0:T(8,128)} %factors.1), channel_id=1, source_target_pairs={{0,1},{1,0},{2,3},{3,2},{4,5},{5,4},{6,7},{7,6},{8,9},{9,8},{10,11... | collective-permute-start | bytes 9437192 | tf_op jit(solution)/shard_map/ppermute | solution.py:414
  61.1 12.7 %copy-start = (bf16[1024,512]{1,0:T(8,128)(2,1)S(1)}, bf16[1024,512]{1,0:T(8,128)(2,1)}, u32[]{:S(2)}) copy-start(bf16[1024,512]{1,0:T(8,128)(2,1)} %get-tuple-element.50.sg_ref.refs_3_.refs_0_) | copy-start | bytes 3145732
  61.1 4.4 %collective-permute-start.2 = (f32[2,4,128,128]{3,2,1,0:T(8,128)S(1)}, f32[2,4,128,128]{3,2,1,0:T(8,128)S(1)}, u32[]{:S(2)}, u32[]{:S(2)}) collective-permute-start(f32[2,4,128,128]{3,2,1,0:T(8,128)S(1)} %bitcast.6), channel_id=1, source_target_pairs={{0,1},{1,0},{2,3},{3,2},{4,5},{5,4},{6,7},{7,6},{8,9},{9,8},{10,11... | collective-permute-start | bytes 1572872 | tf_op jit(solution)/shard_map/ppermute | solution.py:419
  69.4 14.4 %collective-permute-start.3 = (f32[8,4,2,8,384]{4,3,2,1,0:T(8,128)S(1)}, f32[8,4,2,8,384]{4,3,2,1,0:T(8,128)S(1)}, u32[]{:S(2)}, u32[]{:S(2)}) collective-permute-start(f32[8,4,2,8,384]{4,3,2,1,0:T(8,128)S(1)} %get-tuple-element.57), channel_id=1, source_target_pairs={{0,2},{1,7},{2,0},{3,5},{4,6},{5,3},{6,4},{7,1},{8,10},{9,15},{10,... | collective-permute-start | bytes 2359304 | tf_op jit(solution)/shard_map/ppermute | solution.py:398
  72.0 12.1 %collective-permute-start.4 = (f32[8,2,4,8,384]{4,3,2,1,0:T(8,128)S(1)}, f32[8,2,4,8,384]{4,3,2,1,0:T(8,128)S(1)}, u32[]{:S(2)}, u32[]{:S(2)}) collective-permute-start(f32[8,2,4,8,384]{4,3,2,1,0:T(8,128)S(1)} %get-tuple-element.58), channel_id=1, source_target_pairs={{0,8},{1,25},{8,0},{9,17},{16,24},{17,9},{24,16},{25,1},{2,10},{3,... | collective-permute-start | bytes 2359304 | tf_op jit(solution)/shard_map/ppermute | solution.py:398
  73.8 1.9 %copy-start.1 = (bf16[1024,1536]{1,0:T(8,128)(2,1)S(1)}, bf16[1024,1536]{1,0:T(8,128)(2,1)}, u32[]{:S(2)}) copy-start(bf16[1024,1536]{1,0:T(8,128)(2,1)} %get-tuple-element.49.refs_0_.refs_1_.refs_2_.loc_ref) | copy-start | bytes 9437188
  84.1 7.0 %collective-permute-start.8 = (f32[8,4,8,384]{3,2,1,0:T(8,128)S(1)}, f32[8,4,8,384]{3,2,1,0:T(8,128)S(1)}, u32[]{:S(2)}, u32[]{:S(2)}) collective-permute-start(f32[8,4,8,384]{3,2,1,0:T(8,128)S(1)} %get-tuple-element.71), channel_id=1, source_target_pairs={{0,24},{1,9},{8,16},{9,1},{16,8},{17,25},{24,0},{25,17},{2,26},{3,... | collective-permute-start | bytes 1179656 | tf_op jit(solution)/shard_map/ppermute | solution.py:398
  84.3 7.2 %collective-permute-start.5 = (f32[8,4,8,384]{3,2,1,0:T(8,128)S(1)}, f32[8,4,8,384]{3,2,1,0:T(8,128)S(1)}, u32[]{:S(2)}, u32[]{:S(2)}) collective-permute-start(f32[8,4,8,384]{3,2,1,0:T(8,128)S(1)} %get-tuple-element.63), channel_id=1, source_target_pairs={{0,6},{1,3},{2,4},{3,1},{4,2},{5,7},{6,0},{7,5},{8,14},{9,11},{10,... | collective-permute-start | bytes 1179656 | tf_op jit(solution)/shard_map/ppermute | solution.py:398
  91.1 5.8 %collective-permute-start.9 = (f32[8,2,8,384]{3,2,1,0:T(8,128)S(1)}, f32[8,2,8,384]{3,2,1,0:T(8,128)S(1)}, u32[]{:S(2)}, u32[]{:S(2)}) collective-permute-start(f32[8,2,8,384]{3,2,1,0:T(8,128)S(1)} %get-tuple-element.73), channel_id=1, source_target_pairs={{0,2},{1,7},{2,0},{3,5},{4,6},{5,3},{6,4},{7,1},{8,10},{9,15},{10,... | collective-permute-start | bytes 589832 | tf_op jit(solution)/shard_map/ppermute | solution.py:398
  91.6 5.8 %collective-permute-start.6 = (f32[8,2,8,384]{3,2,1,0:T(8,128)S(1)}, f32[8,2,8,384]{3,2,1,0:T(8,128)S(1)}, u32[]{:S(2)}, u32[]{:S(2)}) collective-permute-start(f32[8,2,8,384]{3,2,1,0:T(8,128)S(1)} %get-tuple-element.65), channel_id=1, source_target_pairs={{0,8},{1,25},{8,0},{9,17},{16,24},{17,9},{24,16},{25,1},{2,10},{3,... | collective-permute-start | bytes 589832 | tf_op jit(solution)/shard_map/ppermute | solution.py:398
  97.0 3.6 %collective-permute-start.10 = (f32[8,8,384]{2,1,0:T(8,128)S(1)}, f32[8,8,384]{2,1,0:T(8,128)S(1)}, u32[]{:S(2)}, u32[]{:S(2)}) collective-permute-start(f32[8,8,384]{2,1,0:T(8,128)S(1)} %get-tuple-element.75), channel_id=1, source_target_pairs={{0,6},{1,3},{2,4},{3,1},{4,2},{5,7},{6,0},{7,5},{8,14},{9,11},{10,... | collective-permute-start | bytes 294920 | tf_op jit(solution)/shard_map/ppermute | solution.py:398
  97.4 3.6 %collective-permute-start.7 = (f32[8,8,384]{2,1,0:T(8,128)S(1)}, f32[8,8,384]{2,1,0:T(8,128)S(1)}, u32[]{:S(2)}, u32[]{:S(2)}) collective-permute-start(f32[8,8,384]{2,1,0:T(8,128)S(1)} %get-tuple-element.67), channel_id=1, source_target_pairs={{0,24},{1,9},{8,16},{9,1},{16,8},{17,25},{24,0},{25,17},{2,26},{3,... | collective-permute-start | bytes 294920 | tf_op jit(solution)/shard_map/ppermute | solution.py:398

commit v8 on v7

--- a/solution.py
+++ b/solution.py
@@ -244,7 +244,7 @@
     return (mine, mine ^ second), (mine ^ first, mine ^ first ^ second)
 
 
-def finish_body(w_hbm, a_hbm, b_hbm, sa_ref, sb_ref, kx_ref, sx_ref, ky_ref, sy_ref, w_ref, a_ref, b_ref, s_ref, sems):
+def own_body(w_hbm, a_hbm, b_hbm, s_ref, o_ref, far_ref, w_ref, a_ref, b_ref, sems):
     core = lax.axis_index("core")
     copies = []
     for j in range(3):
@@ -256,50 +256,73 @@
                 pltpu.make_async_copy(b_hbm.at[:, cols], b_ref.at[j], sems.at[2, j]),
             )
         )
-    for pair in copies:
-        for copy in pair:
+    for group in copies:
+        for copy in group:
             copy.start()
     for j, (kind, dims) in enumerate(((0, NT), (1, NT), (1, NN))):
         for copy in copies[j]:
             copy.wait()
         for i in range(2):
             cols = slice(i * HD, (i + 1) * HD)
-            h = 2 * core + i
-            far = b_ref[j, :, cols].astype(BF16)
-            term = dot(a_ref[j, :, cols], sa_ref[kind, h].astype(BF16), dims)
-            term += dot(far, sb_ref[kind, h].astype(BF16), dims)
-            s_ref[j, :, :, :, :, cols] = (w_ref[j, :, cols] + term).reshape(8, 4, 4, 8, HD)
-        lanes = slice(j * HD, (j + 1) * HD)
-        kept, sent = pick("x")
-        for i in range(2):
-            kx_ref[:, :, i, :, lanes] = s_ref[j, :, :, kept[i], :, 0:128]
-            sx_ref[:, :, i, :, lanes] = s_ref[j, :, :, sent[i], :, 0:128]
-        kept, sent = pick("y")
-        for i in range(2):
-            ky_ref[:, i, :, :, lanes] = s_ref[j, :, kept[i], :, :, 128:256]
-            sy_ref[:, i, :, :, lanes] = s_ref[j, :, sent[i], :, :, 128:256]
-
-
-def finish(w, a, b, sa, sb):
+            term = dot(a_ref[j, :, cols], s_ref[kind, 2 * core + i].astype(BF16), dims)
+            o_ref[j, :, cols] = w_ref[j, :, cols] + term
+        far_ref[j] = b_ref[j].astype(BF16)
+
+
+def own_states(w, a, b, states):
     vmem = pl.BlockSpec(memory_space=pltpu.VMEM)
     hbm = pl.BlockSpec(memory_space=pltpu.HBM)
     return pl.pallas_call(
-        finish_body,
-        in_specs=[hbm, hbm, hbm, vmem, vmem],
-        out_specs=[vmem] * 4,
-        out_shape=[jax.ShapeDtypeStruct((8, 4, 2, 8, 384), F32)] * 2
-        + [jax.ShapeDtypeStruct((8, 2, 4, 8, 384), F32)] * 2,
+        own_body,
+        in_specs=[hbm, hbm, hbm, vmem],
+        out_specs=[vmem, vmem],
+        out_shape=[
+            jax.ShapeDtypeStruct((3, DM, 256), F32),
+            jax.ShapeDtypeStruct((3, DM, 256), BF16),
+        ],
         scratch_shapes=[
             pltpu.VMEM((3, DM, 256), F32),
             pltpu.VMEM((3, DM, 256), BF16),
             pltpu.VMEM((3, DM, 256), F32),
-            pltpu.VMEM((3, 8, 4, 4, 8, 256), F32),
             pltpu.SemaphoreType.DMA((3, 3)),
         ],
-        compiler_params=params(49),
+        compiler_params=params(47),
+        cost_estimate=cost(5e9, 12e6),
+        name="own_states",
+    )(w, a, b, states)
+
+
+def finish_body(w_ref, b_ref, s_ref, kx_ref, sx_ref, ky_ref, sy_ref, t_ref):
+    core = lax.axis_index("core")
+    for j, (kind, dims) in enumerate(((0, NT), (1, NT), (1, NN))):
+        for i in range(2):
+            cols = slice(i * HD, (i + 1) * HD)
+            term = dot(b_ref[j, :, cols], s_ref[kind, 2 * core + i].astype(BF16), dims)
+            t_ref[j, :, :, :, :, cols] = (w_ref[j, :, cols] + term).reshape(8, 4, 4, 8, HD)
+        lanes = slice(j * HD, (j + 1) * HD)
+        kept, sent = pick("x")
+        for i in range(2):
+            kx_ref[:, :, i, :, lanes] = t_ref[j, :, :, kept[i], :, 0:128]
+            sx_ref[:, :, i, :, lanes] = t_ref[j, :, :, sent[i], :, 0:128]
+        kept, sent = pick("y")
+        for i in range(2):
+            ky_ref[:, i, :, :, lanes] = t_ref[j, :, kept[i], :, :, 128:256]
+            sy_ref[:, i, :, :, lanes] = t_ref[j, :, sent[i], :, :, 128:256]
+
+
+def finish(w, b, states):
+    vmem = pl.BlockSpec(memory_space=pltpu.VMEM)
+    return pl.pallas_call(
+        finish_body,
+        in_specs=[vmem] * 3,
+        out_specs=[vmem] * 4,
+        out_shape=[jax.ShapeDtypeStruct((8, 4, 2, 8, 384), F32)] * 2
+        + [jax.ShapeDtypeStruct((8, 2, 4, 8, 384), F32)] * 2,
+        scratch_shapes=[pltpu.VMEM((3, 8, 4, 4, 8, 256), F32)],
+        compiler_params=params(44),
         cost_estimate=cost(1e9, 12e6),
         name="finish",
-    )(w, a, b, sa, sb)
+    )(w, b, states)
 
 
 def inputs_body(loc_ref, qkv_ref, sg_ref, s_ref, w_ref, o_ref, d_ref):
@@ -331,7 +354,7 @@
         out_specs=block(DM),
         out_shape=jax.ShapeDtypeStruct((TOK, DM), BF16),
         scratch_shapes=[pltpu.VMEM((CH, 3 * D), BF16)],
-        compiler_params=params(48),
+        compiler_params=params(50),
         cost_estimate=cost(5e9, 14e6),
         name="inputs_grad",
     )(loc, qkv, sg, states, weights)
@@ -417,7 +440,8 @@
 
     states = states.reshape(2, H, HD, HD)
     states_in = lax.ppermute(states, "core", SWAP)
-    kx, sx, ky, sy = finish(both, mine, factors_in, states, states_in)
+    both, far = own_states(both, mine, factors_in, states)
+    kx, sx, ky, sy = finish(both, far, states_in)
     rx = exchange(sx, "x", 0)
     ry = exchange(sy, "y", 0)
     record_grad = inputs_grad(loc, qkv, sg, states, weights)

time: 130 us -> 130 us (level)
    ppermute x1, waiting for transfers between devices: 1.54 us -> 0.01 us  [shards(): states_in = lax.ppermute(states, 'core', SWAP)]
    ppermute x8, waiting for transfers between devices: 14.2 us -> 15.5 us  [exchange(): return lax.ppermute(value, (axis, 'core'), pairs)]
    pallas_call x1 -> x2, Pallas kernels: 3.92 us -> 4.33 us  [the longest x1 3.28 us: own_states(): pl.pallas_call(own_body, in_specs=[hbm, hbm, hbm, vmem], out_specs=[vmem,...]
  transfers between devices with their start and end apart: 13 -> 13, of which waited for: 9 -> 8; matrix products, arithmetic and copies ran while one was open for 0% -> 0% of each run, Pallas kernels for 26% -> 29%
where the time goes in v8:
time: 130 us
  Pallas kernels  48.8 us (38%)
  starting transfers between devices  30.3 us (23%)
  blocking collectives  28 us (22%)
  waiting for transfers between devices  20.7 us (16%)
  local copies, waits for them, and re-layouts  1.41 us (1%)
    all_to_all x1, blocking collectives, shards(): rows = lax.all_to_all(own, ('x', 'core'), 0, 0, tiled=True)  16.6 us
    ppermute x8, waiting for transfers between devices, exchange(): return lax.ppermute(value, (axis, 'core'), pairs)  15.5 us
    all_to_all x1, starting transfers between devices, shards(): lax.all_to_all(total.reshape(32, 32, HD), ('z', 'y'), 0, 0, tiled=True)  12 us
    pallas_call x1, Pallas kernels, local(): pl.pallas_call(local_body, grid_spec=pltpu.PrefetchScalarGridSpec(num_sca...  11.8 us
    all_to_all x1, blocking collectives, shards(): part = lax.all_to_all(part, 'z', 0, 0, tiled=True)  11.4 us
    pallas_call x1, Pallas kernels, project(): pl.pallas_call(project_body, grid=(NB,), in_specs=[block(DM), pl.BlockSpe...  9.22 us
    pallas_call x1, Pallas kernels, inputs_grad(): pl.pallas_call(inputs_body, grid=(NB,), in_specs=[block(3 * D), block(3 *...  8.6 us
    pallas_call x1, Pallas kernels, keep(): pl.pallas_call(keep_body, grid_spec=pltpu.PrefetchScalarGridSpec(num_scal...  7.96 us
  transfers between devices with their start and end apart: 13, of which 8 were waited for; matrix products, arithmetic and copies ran while one was open for 0% of the time, Pallas kernels for 29%

profile of v8, /device:TPU:1, one launch (start us, length us, event | category | flops | bytes accessed | tf_op | source)
XLA Modules:
  0.0 130.0 jit_solution(15265649868162125946)
XLA Ops:
  0.6 9.2 %project.1 = (bf16[1024,1536]{1,0:T(8,128)(2,1)}, bf16[1024,512]{1,0:T(8,128)(2,1)}, f32[4,4,128,128]{3,2,1,0:T(8,128)}, f32[4,4,128,128]{3,2,1,0:T(8,128)}, f32[2,4,128,128]{3,2,1,0:T(8,128)}) custom-call(bf16[1024,1024]{1,0:T(8,128)(2,1)} %bitcast.9, bf16[1024,1536]{1,0:T(8,128)(2,1)} %w_ref.3, bf16[1024,512]{1,0:T(8,128)(2,1)} %bitcast.13), custom_call_target="tpu_custom_call" | custom-call | tf_op jit(solution)/shard_map/project/pallas_call | solution.py:69
  9.9 12.0 %all-to-all-start = ((f32[32,32,128]{2,1,0:T(8,128)}), f32[32,32,128]{2,1,0:T(8,128)S(1)}, u32[]{:S(2)}, u32[]{:S(2)}) async-start(f32[32,32,128]{2,1,0:T(8,128)} %bitcast.14), calls=%async_computation | async-start | bytes 1048576 | tf_op jit(solution)/shard_map/all_to_all | solution.py:429
  21.9 11.8 %local.1 = (bf16[1024,1536]{1,0:T(8,128)(2,1)}, f32[1024,768]{1,0:T(8,128)}) custom-call(s32[1]{0:T(128)} %bitcast.3.at_ref, bf16[1024,1536]{1,0:T(8,128)(2,1)} %get-tuple-element.53.qkv_ref.refs_4_.refs_5_.refs_1_.refs_2_, bf16[1024,512]{1,0:T(8,128)(2,1)} %get-tuple-element.52.sg_ref.refs_3_.refs_0_, f32[4,4,128,128]{3,2,1,0:T(8,128)} %get-tuple-element.44.kv_ref, ...), custom_call_target="tpu_custom_call" | custom-call | flops 8000000000 | bytes 24000000 | tf_op jit(solution)/shard_map/local/pallas_call | solution.py:163
  33.7 1.0 collective-permute-start
  34.7 3.5 %all-to-all-done.v_ref = f32[32,32,128]{2,1,0:T(8,128)S(1)} async-done(((f32[32,32,128]{2,1,0:T(8,128)}), f32[32,32,128]{2,1,0:T(8,128)S(1)}, u32[]{:S(2)}, u32[]{:S(2)}) %all-to-all-start) | async-done | bytes 524320 | tf_op jit(solution)/shard_map/all_to_all | solution.py:429
  38.2 1.0 scan_states.1
  39.1 6.0 %all-to-all-start.1 = ((f32[32,32,128]{2,1,0:T(8,128)}), f32[32,32,128]{2,1,0:T(8,128)S(1)}, u32[]{:S(2)}, u32[]{:S(2)}) async-start(f32[32,32,128]{2,1,0:T(8,128)} %scan_states.1), calls=%async_computation.1 | async-start | bytes 1048576 | tf_op jit(solution)/shard_map/all_to_all | solution.py:435
  45.2 5.0 %factors.1 = f32[1024,768]{1,0:T(8,128)} custom-call(s32[1]{0:T(128)} %bitcast.3.at_ref, bf16[1024,1024]{1,0:T(8,128)(2,1)} %bitcast.11, bf16[1024,512]{1,0:T(8,128)(2,1)} %get-tuple-element.52.sg_ref.refs_3_.refs_0_, bf16[1024,1536]{1,0:T(8,128)(2,1)} %get-tuple-element.53.qkv_ref.refs_4_.refs_5_.refs_1_.refs_2_, ...), custom_call_target="tpu_custom_call" | custom-call | flops 60000002048 | bytes 12000000 | tf_op jit(solution)/shard_map/factors/pallas_call | solution.py:199
  50.2 1.0 collective-permute-start.1
  51.2 0.0 collective-permute-done.r_ref
  51.2 8.0 %keep.1 = (f32[1024,768]{1,0:T(8,128)}, bf16[1024,768]{1,0:T(8,128)(2,1)}) custom-call(s32[1]{0:T(128)} %bitcast.3.at_ref, bf16[1024,1024]{1,0:T(8,128)(2,1)} %bitcast.12, f32[1024,768]{1,0:T(8,128)} %collective-permute-done.r_ref, bf16[1024,1536]{1,0:T(8,128)(2,1)} %get-tuple-element.51.refs_0_.refs_1_.refs_2_.loc_ref, ...), custom_call_target="tpu_custom_call" | custom-call | flops 40000000000 | bytes 16000000 | tf_op jit(solution)/shard_map/keep/pallas_call | solution.py:225
  59.2 1.6 %all-to-all-done.1 = f32[32,32,128]{2,1,0:T(8,128)S(1)} async-done(((f32[32,32,128]{2,1,0:T(8,128)}), f32[32,32,128]{2,1,0:T(8,128)S(1)}, u32[]{:S(2)}, u32[]{:S(2)}) %all-to-all-start.1) | async-done | bytes 524320 | tf_op jit(solution)/shard_map/all_to_all | solution.py:435
  60.8 3.1 %collective-permute-start.2 = (f32[2,4,128,128]{3,2,1,0:T(8,128)S(1)}, f32[2,4,128,128]{3,2,1,0:T(8,128)S(1)}, u32[]{:S(2)}, u32[]{:S(2)}) collective-permute-start(f32[2,4,128,128]{3,2,1,0:T(8,128)S(1)} %bitcast.6), channel_id=1, source_target_pairs={{0,1},{1,0},{2,3},{3,2},{4,5},{5,4},{6,7},{7,6},{8,9},{9,8},{10,11... | collective-permute-start | bytes 1572872 | tf_op jit(solution)/shard_map/ppermute | solution.py:442
  63.9 0.0 collective-permute-done.1.b_hbm
  63.9 0.0 copy-start.1
  63.9 1.4 %copy-done.1 = bf16[1024,768]{1,0:T(8,128)(2,1)S(1)} copy-done((bf16[1024,768]{1,0:T(8,128)(2,1)S(1)}, bf16[1024,768]{1,0:T(8,128)(2,1)}, u32[]{:S(2)}) %copy-start.1) | copy-done | bytes 1572888
  65.3 3.3 %own_states.1 = (f32[3,1024,256]{2,1,0:T(8,128)S(1)}, bf16[3,1024,256]{2,1,0:T(8,128)(2,1)S(1)}) custom-call(f32[1024,768]{1,0:T(8,128)} %get-tuple-element.56.w_hbm, bf16[1024,768]{1,0:T(8,128)(2,1)S(1)} %copy-done.1, f32[1024,768]{1,0:T(8,128)} %collective-permute-done.1.b_hbm, f32[2,4,128,128]{3,2,1,0:T(8,128)S(1)} %bitcast.7), custom_call_target="tpu_custom_call" | custom-call | flops 5000000000 | bytes 12000000 | tf_op jit(solution)/shard_map/own_states/pallas_call | solution.py:275
  68.6 0.0 copy-start
  68.6 0.0 collective-permute-done.2.s_ref
  68.6 1.0 finish.1
  69.6 2.6 %collective-permute-start.3 = (f32[8,4,2,8,384]{4,3,2,1,0:T(8,128)S(1)}, f32[8,4,2,8,384]{4,3,2,1,0:T(8,128)S(1)}, u32[]{:S(2)}, u32[]{:S(2)}) collective-permute-start(f32[8,4,2,8,384]{4,3,2,1,0:T(8,128)S(1)} %get-tuple-element.61), channel_id=1, source_target_pairs={{0,2},{1,7},{2,0},{3,5},{4,6},{5,3},{6,4},{7,1},{8,10},{9,15},{10,... | collective-permute-start | bytes 2359304 | tf_op jit(solution)/shard_map/ppermute | solution.py:421
  72.2 1.8 %collective-permute-start.4 = (f32[8,2,4,8,384]{4,3,2,1,0:T(8,128)S(1)}, f32[8,2,4,8,384]{4,3,2,1,0:T(8,128)S(1)}, u32[]{:S(2)}, u32[]{:S(2)}) collective-permute-start(f32[8,2,4,8,384]{4,3,2,1,0:T(8,128)S(1)} %get-tuple-element.62), channel_id=1, source_target_pairs={{0,8},{1,25},{8,0},{9,17},{16,24},{17,9},{24,16},{25,1},{2,10},{3,... | collective-permute-start | bytes 2359304 | tf_op jit(solution)/shard_map/ppermute | solution.py:421
  74.1 0.0 copy-done
  74.1 8.6 %inputs_grad.1 = bf16[1024,1024]{1,0:T(8,128)(2,1)} custom-call(bf16[1024,1536]{1,0:T(8,128)(2,1)} %get-tuple-element.51.refs_0_.refs_1_.refs_2_.loc_ref, bf16[1024,1536]{1,0:T(8,128)(2,1)} %get-tuple-element.53.qkv_ref.refs_4_.refs_5_.refs_1_.refs_2_, bf16[1024,512]{1,0:T(8,128)(2,1)S(1)} %copy-done, f32[2,4,128,128]{3,2,1,0:T(8,128)S(1)} %bitcast.8, ...), custom_call_target="tpu_custom_call" | custom-call | flops 5000000000 | bytes 14000000 | tf_op jit(solution)/shard_map/inputs_grad/pallas_call | solution.py:344
  82.7 0.0 collective-permute-done.3.r
  82.7 1.6 %collective-permute-done.4.r = f32[8,2,4,8,384]{4,3,2,1,0:T(8,128)S(1)} collective-permute-done((f32[8,2,4,8,384]{4,3,2,1,0:T(8,128)S(1)}, f32[8,2,4,8,384]{4,3,2,1,0:T(8,128)S(1)}, u32[]{:S(2)}, u32[]{:S(2)}) %collective-permute-start.4) | collective-permute-done | bytes 786464 | tf_op jit(solution)/shard_map/ppermute | solution.py:421
  84.3 0.1 add1y.1
  84.4 0.1 collective-permute-start.8
  84.5 0.1 add1x.1
  84.6 0.1 collective-permute-start.5
  84.7 6.7 %collective-permute-done.8.r = f32[8,4,8,384]{3,2,1,0:T(8,128)S(1)} collective-permute-done((f32[8,4,8,384]{3,2,1,0:T(8,128)S(1)}, f32[8,4,8,384]{3,2,1,0:T(8,128)S(1)}, u32[]{:S(2)}, u32[]{:S(2)}) %collective-permute-start.8) | collective-permute-done | bytes 393248 | tf_op jit(solution)/shard_map/ppermute | solution.py:421
  91.4 0.4 collective-permute-start.9
  91.8 0.0 collective-permute-done.5.r
  91.8 1.9 %collective-permute-start.6 = (f32[8,2,8,384]{3,2,1,0:T(8,128)S(1)}, f32[8,2,8,384]{3,2,1,0:T(8,128)S(1)}, u32[]{:S(2)}, u32[]{:S(2)}) collective-permute-start(f32[8,2,8,384]{3,2,1,0:T(8,128)S(1)} %get-tuple-element.69), channel_id=1, source_target_pairs={{0,8},{1,25},{8,0},{9,17},{16,24},{17,9},{24,16},{25,1},{2,10},{3,... | collective-permute-start | bytes 589832 | tf_op jit(solution)/shard_map/ppermute | solution.py:421
  93.8 3.5 %collective-permute-done.9.r = f32[8,2,8,384]{3,2,1,0:T(8,128)S(1)} collective-permute-done((f32[8,2,8,384]{3,2,1,0:T(8,128)S(1)}, f32[8,2,8,384]{3,2,1,0:T(8,128)S(1)}, u32[]{:S(2)}, u32[]{:S(2)}) %collective-permute-start.9) | collective-permute-done | bytes 196640 | tf_op jit(solution)/shard_map/ppermute | solution.py:421
  97.3 0.1 collective-permute-start.10
  97.4 0.3 collective-permute-done.6.r
  97.7 0.1 collective-permute-start.7
  97.8 3.0 %collective-permute-done.10.rq = f32[8,8,384]{2,1,0:T(8,128)S(1)} collective-permute-done((f32[8,8,384]{2,1,0:T(8,128)S(1)}, f32[8,8,384]{2,1,0:T(8,128)S(1)}, u32[]{:S(2)}, u32[]{:S(2)}) %collective-permute-start.10) | collective-permute-done | bytes 98336 | tf_op jit(solution)/shard_map/ppermute | solution.py:421
  100.8 0.4 collective-permute-done.7.rp
  101.3 11.4 %all_to_all.20.v = f32[8,8,768]{2,1,0:T(8,128)S(1)} all-to-all(f32[8,8,768]{2,1,0:T(8,128)S(1)} %add4.1), channel_id=1, replica_groups=mesh['z'=8,'y'=4,'x'=4,'core'=2] {'z'}, dimensions={0} | all-to-all | bytes 393216 | tf_op jit(solution)/shard_map/all_to_all | solution.py:462
  112.7 16.6 %all_to_all.21.v = f32[8,8,768]{2,1,0:T(8,128)S(1)} all-to-all(f32[8,8,768]{2,1,0:T(8,128)S(1)} %sum_z.1), channel_id=1, replica_groups=mesh['z'=8,'y'=4,'x'=4,'core'=2] {'x','core'}, dimensions={0} | all-to-all | bytes 393216 | tf_op jit(solution)/shard_map/all_to_all | solution.py:464
  129.3 0.7 place.1
  (6 shorter events, 0.2 us)
Async XLA Ops:
  9.9 28.3 %all-to-all-start = ((f32[32,32,128]{2,1,0:T(8,128)}), f32[32,32,128]{2,1,0:T(8,128)S(1)}, u32[]{:S(2)}, u32[]{:S(2)}) async-start(f32[32,32,128]{2,1,0:T(8,128)} %bitcast.14), calls=%async_computation | async-start | bytes 1048576 | tf_op jit(solution)/shard_map/all_to_all | solution.py:429
  33.7 17.5 %collective-permute-start = (f32[1024,768]{1,0:T(8,128)}, f32[1024,768]{1,0:T(8,128)}, u32[]{:S(2)}, u32[]{:S(2)}) collective-permute-start(f32[1024,768]{1,0:T(8,128)} %get-tuple-element.50), channel_id=1, source_target_pairs={{0,1},{1,0},{2,3},{3,2},{4,5},{5,4},{6,7},{7,6},{8,9},{9,8},{10,11... | collective-permute-start | bytes 9437192 | tf_op jit(solution)/shard_map/ppermute | solution.py:431
  39.1 21.7 %all-to-all-start.1 = ((f32[32,32,128]{2,1,0:T(8,128)}), f32[32,32,128]{2,1,0:T(8,128)S(1)}, u32[]{:S(2)}, u32[]{:S(2)}) async-start(f32[32,32,128]{2,1,0:T(8,128)} %scan_states.1), calls=%async_computation.1 | async-start | bytes 1048576 | tf_op jit(solution)/shard_map/all_to_all | solution.py:435
  50.2 13.7 %collective-permute-start.1 = (f32[1024,768]{1,0:T(8,128)}, f32[1024,768]{1,0:T(8,128)}, u32[]{:S(2)}, u32[]{:S(2)}) collective-permute-start(f32[1024,768]{1,0:T(8,128)} %factors.1), channel_id=1, source_target_pairs={{0,1},{1,0},{2,3},{3,2},{4,5},{5,4},{6,7},{7,6},{8,9},{9,8},{10,11... | collective-permute-start | bytes 9437192 | tf_op jit(solution)/shard_map/ppermute | solution.py:437
  60.8 7.8 %collective-permute-start.2 = (f32[2,4,128,128]{3,2,1,0:T(8,128)S(1)}, f32[2,4,128,128]{3,2,1,0:T(8,128)S(1)}, u32[]{:S(2)}, u32[]{:S(2)}) collective-permute-start(f32[2,4,128,128]{3,2,1,0:T(8,128)S(1)} %bitcast.6), channel_id=1, source_target_pairs={{0,1},{1,0},{2,3},{3,2},{4,5},{5,4},{6,7},{7,6},{8,9},{9,8},{10,11... | collective-permute-start | bytes 1572872 | tf_op jit(solution)/shard_map/ppermute | solution.py:442
  63.9 1.4 %copy-start.1 = (bf16[1024,768]{1,0:T(8,128)(2,1)S(1)}, bf16[1024,768]{1,0:T(8,128)(2,1)}, u32[]{:S(2)}) copy-start(bf16[1024,768]{1,0:T(8,128)(2,1)} %get-tuple-element.57.a_hbm) | copy-start | bytes 4718596
  68.6 5.5 %copy-start = (bf16[1024,512]{1,0:T(8,128)(2,1)S(1)}, bf16[1024,512]{1,0:T(8,128)(2,1)}, u32[]{:S(2)}) copy-start(bf16[1024,512]{1,0:T(8,128)(2,1)} %get-tuple-element.52.sg_ref.refs_3_.refs_0_) | copy-start | bytes 3145732
  69.6 13.0 %collective-permute-start.3 = (f32[8,4,2,8,384]{4,3,2,1,0:T(8,128)S(1)}, f32[8,4,2,8,384]{4,3,2,1,0:T(8,128)S(1)}, u32[]{:S(2)}, u32[]{:S(2)}) collective-permute-start(f32[8,4,2,8,384]{4,3,2,1,0:T(8,128)S(1)} %get-tuple-element.61), channel_id=1, source_target_pairs={{0,2},{1,7},{2,0},{3,5},{4,6},{5,3},{6,4},{7,1},{8,10},{9,15},{10,... | collective-permute-start | bytes 2359304 | tf_op jit(solution)/shard_map/ppermute | solution.py:421
  72.2 12.1 %collective-permute-start.4 = (f32[8,2,4,8,384]{4,3,2,1,0:T(8,128)S(1)}, f32[8,2,4,8,384]{4,3,2,1,0:T(8,128)S(1)}, u32[]{:S(2)}, u32[]{:S(2)}) collective-permute-start(f32[8,2,4,8,384]{4,3,2,1,0:T(8,128)S(1)} %get-tuple-element.62), channel_id=1, source_target_pairs={{0,8},{1,25},{8,0},{9,17},{16,24},{17,9},{24,16},{25,1},{2,10},{3,... | collective-permute-start | bytes 2359304 | tf_op jit(solution)/shard_map/ppermute | solution.py:421
  84.4 7.0 %collective-permute-start.8 = (f32[8,4,8,384]{3,2,1,0:T(8,128)S(1)}, f32[8,4,8,384]{3,2,1,0:T(8,128)S(1)}, u32[]{:S(2)}, u32[]{:S(2)}) collective-permute-start(f32[8,4,8,384]{3,2,1,0:T(8,128)S(1)} %get-tuple-element.75), channel_id=1, source_target_pairs={{0,24},{1,9},{8,16},{9,1},{16,8},{17,25},{24,0},{25,17},{2,26},{3,... | collective-permute-start | bytes 1179656 | tf_op jit(solution)/shard_map/ppermute | solution.py:421
  84.6 7.2 %collective-permute-start.5 = (f32[8,4,8,384]{3,2,1,0:T(8,128)S(1)}, f32[8,4,8,384]{3,2,1,0:T(8,128)S(1)}, u32[]{:S(2)}, u32[]{:S(2)}) collective-permute-start(f32[8,4,8,384]{3,2,1,0:T(8,128)S(1)} %get-tuple-element.67), channel_id=1, source_target_pairs={{0,6},{1,3},{2,4},{3,1},{4,2},{5,7},{6,0},{7,5},{8,14},{9,11},{10,... | collective-permute-start | bytes 1179656 | tf_op jit(solution)/shard_map/ppermute | solution.py:421
  91.4 5.8 %collective-permute-start.9 = (f32[8,2,8,384]{3,2,1,0:T(8,128)S(1)}, f32[8,2,8,384]{3,2,1,0:T(8,128)S(1)}, u32[]{:S(2)}, u32[]{:S(2)}) collective-permute-start(f32[8,2,8,384]{3,2,1,0:T(8,128)S(1)} %get-tuple-element.77), channel_id=1, source_target_pairs={{0,2},{1,7},{2,0},{3,5},{4,6},{5,3},{6,4},{7,1},{8,10},{9,15},{10,... | collective-permute-start | bytes 589832 | tf_op jit(solution)/shard_map/ppermute | solution.py:421
  91.8 5.8 %collective-permute-start.6 = (f32[8,2,8,384]{3,2,1,0:T(8,128)S(1)}, f32[8,2,8,384]{3,2,1,0:T(8,128)S(1)}, u32[]{:S(2)}, u32[]{:S(2)}) collective-permute-start(f32[8,2,8,384]{3,2,1,0:T(8,128)S(1)} %get-tuple-element.69), channel_id=1, source_target_pairs={{0,8},{1,25},{8,0},{9,17},{16,24},{17,9},{24,16},{25,1},{2,10},{3,... | collective-permute-start | bytes 589832 | tf_op jit(solution)/shard_map/ppermute | solution.py:421
  97.3 3.6 %collective-permute-start.10 = (f32[8,8,384]{2,1,0:T(8,128)S(1)}, f32[8,8,384]{2,1,0:T(8,128)S(1)}, u32[]{:S(2)}, u32[]{:S(2)}) collective-permute-start(f32[8,8,384]{2,1,0:T(8,128)S(1)} %get-tuple-element.79), channel_id=1, source_target_pairs={{0,6},{1,3},{2,4},{3,1},{4,2},{5,7},{6,0},{7,5},{8,14},{9,11},{10,... | collective-permute-start | bytes 294920 | tf_op jit(solution)/shard_map/ppermute | solution.py:421
  97.7 3.6 %collective-permute-start.7 = (f32[8,8,384]{2,1,0:T(8,128)S(1)}, f32[8,8,384]{2,1,0:T(8,128)S(1)}, u32[]{:S(2)}, u32[]{:S(2)}) collective-permute-start(f32[8,8,384]{2,1,0:T(8,128)S(1)} %get-tuple-element.71), channel_id=1, source_target_pairs={{0,24},{1,9},{8,16},{9,1},{16,8},{17,25},{24,0},{25,17},{2,26},{3,... | collective-permute-start | bytes 294920 | tf_op jit(solution)/shard_map/ppermute | solution.py:421

commit v9 on v8

--- a/solution.py
+++ b/solution.py
@@ -216,7 +216,10 @@
     for j in range(3):
         cols = slice(j * 256, (j + 1) * 256)
         w_ref[:, cols] = dot(x_ref[...], refs[j][...], TN) + r_ref[:, cols]
-        f_ref[:, cols] = dot(x_ref[...], refs[3 + j][...], TN).astype(BF16)
+        factor = dot(x_ref[...], refs[3 + j][...], TN)
+        high = factor.astype(BF16)
+        f_ref[0, :, cols] = high
+        f_ref[1, :, cols] = (factor - high.astype(F32)).astype(BF16)
 
 
 def keep(at, x, arrived, sources):
@@ -228,9 +231,9 @@
             num_scalar_prefetch=1,
             grid=(2,),
             in_specs=[pl.BlockSpec((TOK, DM // 2), lambda i, s: (0, i)), rows] + cols,
-            out_specs=[rows, rows],
+            out_specs=[rows, pl.BlockSpec((2, DM // 2, 768), lambda i, s: (0, i, 0))],
         ),
-        out_shape=[jax.ShapeDtypeStruct((DM, 768), F32), jax.ShapeDtypeStruct((DM, 768), BF16)],
+        out_shape=[jax.ShapeDtypeStruct((DM, 768), F32), jax.ShapeDtypeStruct((2, DM, 768), BF16)],
         compiler_params=params(60),
         cost_estimate=cost(40e9, 16e6),
         name="keep",
@@ -252,7 +255,7 @@
         copies.append(
             (
                 pltpu.make_async_copy(w_hbm.at[:, cols], w_ref.at[j], sems.at[0, j]),
-                pltpu.make_async_copy(a_hbm.at[:, cols], a_ref.at[j], sems.at[1, j]),
+                pltpu.make_async_copy(a_hbm.at[:, :, cols], a_ref.at[j], sems.at[1, j]),
                 pltpu.make_async_copy(b_hbm.at[:, cols], b_ref.at[j], sems.at[2, j]),
             )
         )
@@ -264,7 +267,8 @@
             copy.wait()
         for i in range(2):
             cols = slice(i * HD, (i + 1) * HD)
-            term = dot(a_ref[j, :, cols], s_ref[kind, 2 * core + i].astype(BF16), dims)
+            state = s_ref[kind, 2 * core + i].astype(BF16)
+            term = dot(a_ref[j, 0, :, cols], state, dims) + dot(a_ref[j, 1, :, cols], state, dims)
             o_ref[j, :, cols] = w_ref[j, :, cols] + term
         far_ref[j] = b_ref[j].astype(BF16)
 
@@ -282,7 +286,7 @@
         ],
         scratch_shapes=[
             pltpu.VMEM((3, DM, 256), F32),
-            pltpu.VMEM((3, DM, 256), BF16),
+            pltpu.VMEM((3, 2, DM, 256), BF16),
             pltpu.VMEM((3, DM, 256), F32),
             pltpu.SemaphoreType.DMA((3, 3)),
         ],

time: 130 us -> 131 us (level)
  Pallas kernels: 48.8 us -> 50.2 us
  local copies, waits for them, and re-layouts: 1.41 us -> 0.01 us
    unnamed x4 -> x2, local copies, waits for them, and re-layouts: 1.41 us -> 0.01 us
  transfers between devices with their start and end apart: 13 -> 13, of which waited for: 8 -> 8; matrix products, arithmetic and copies ran while one was open for 0% -> 0% of each run, Pallas kernels for 29% -> 30%
where the time goes in v9:
time: 131 us
  Pallas kernels  50.2 us (38%)
  starting transfers between devices  30.3 us (23%)
  blocking collectives  29.3 us (22%)
  waiting for transfers between devices  20.3 us (15%)
    all_to_all x1, blocking collectives, shards(): rows = lax.all_to_all(own, ('x', 'core'), 0, 0, tiled=True)  17.7 us
    ppermute x8, waiting for transfers between devices, exchange(): return lax.ppermute(value, (axis, 'core'), pairs)  15.6 us
    all_to_all x1, starting transfers between devices, shards(): lax.all_to_all(total.reshape(32, 32, HD), ('z', 'y'), 0, 0, tiled=True)  12 us
    pallas_call x1, Pallas kernels, local(): pl.pallas_call(local_body, grid_spec=pltpu.PrefetchScalarGridSpec(num_sca...  11.8 us
    all_to_all x1, blocking collectives, shards(): part = lax.all_to_all(part, 'z', 0, 0, tiled=True)  11.6 us
    pallas_call x1, Pallas kernels, project(): pl.pallas_call(project_body, grid=(NB,), in_specs=[block(DM), pl.BlockSpe...  9.22 us
    pallas_call x1, Pallas kernels, inputs_grad(): pl.pallas_call(inputs_body, grid=(NB,), in_specs=[block(3 * D), block(3 *...  8.6 us
    pallas_call x1, Pallas kernels, keep(): pl.pallas_call(keep_body, grid_spec=pltpu.PrefetchScalarGridSpec(num_scal...  8.31 us
  transfers between devices with their start and end apart: 13, of which 8 were waited for; matrix products, arithmetic and copies ran while one was open for 0% of the time, Pallas kernels for 30%

profile of v9, /device:TPU:1, one launch (start us, length us, event | category | flops | bytes accessed | tf_op | source)
XLA Modules:
  0.0 130.9 jit_solution(419041673731644144)
XLA Ops:
  0.6 9.2 %project.1 = (bf16[1024,1536]{1,0:T(8,128)(2,1)}, bf16[1024,512]{1,0:T(8,128)(2,1)}, f32[4,4,128,128]{3,2,1,0:T(8,128)}, f32[4,4,128,128]{3,2,1,0:T(8,128)}, f32[2,4,128,128]{3,2,1,0:T(8,128)}) custom-call(bf16[1024,1024]{1,0:T(8,128)(2,1)} %bitcast.9, bf16[1024,1536]{1,0:T(8,128)(2,1)} %w_ref.3, bf16[1024,512]{1,0:T(8,128)(2,1)} %bitcast.13), custom_call_target="tpu_custom_call" | custom-call | tf_op jit(solution)/shard_map/project/pallas_call | solution.py:69
  9.9 12.0 %all-to-all-start = ((f32[32,32,128]{2,1,0:T(8,128)}), f32[32,32,128]{2,1,0:T(8,128)S(1)}, u32[]{:S(2)}, u32[]{:S(2)}) async-start(f32[32,32,128]{2,1,0:T(8,128)} %bitcast.14), calls=%async_computation | async-start | bytes 1048576 | tf_op jit(solution)/shard_map/all_to_all | solution.py:433
  21.9 11.8 %local.1 = (bf16[1024,1536]{1,0:T(8,128)(2,1)}, f32[1024,768]{1,0:T(8,128)}) custom-call(s32[1]{0:T(128)} %bitcast.3.at_ref, bf16[1024,1536]{1,0:T(8,128)(2,1)} %get-tuple-element.53.qkv_ref.refs_4_.refs_5_.refs_1_.refs_2_, bf16[1024,512]{1,0:T(8,128)(2,1)} %get-tuple-element.52.sg_ref.refs_3_.refs_0_, f32[4,4,128,128]{3,2,1,0:T(8,128)} %get-tuple-element.44.kv_ref, ...), custom_call_target="tpu_custom_call" | custom-call | flops 8000000000 | bytes 24000000 | tf_op jit(solution)/shard_map/local/pallas_call | solution.py:163
  33.7 1.0 collective-permute-start
  34.7 3.5 %all-to-all-done.v_ref = f32[32,32,128]{2,1,0:T(8,128)S(1)} async-done(((f32[32,32,128]{2,1,0:T(8,128)}), f32[32,32,128]{2,1,0:T(8,128)S(1)}, u32[]{:S(2)}, u32[]{:S(2)}) %all-to-all-start) | async-done | bytes 524320 | tf_op jit(solution)/shard_map/all_to_all | solution.py:433
  38.2 1.0 scan_states.1
  39.1 6.0 %all-to-all-start.1 = ((f32[32,32,128]{2,1,0:T(8,128)}), f32[32,32,128]{2,1,0:T(8,128)S(1)}, u32[]{:S(2)}, u32[]{:S(2)}) async-start(f32[32,32,128]{2,1,0:T(8,128)} %scan_states.1), calls=%async_computation.1 | async-start | bytes 1048576 | tf_op jit(solution)/shard_map/all_to_all | solution.py:439
  45.2 5.0 %factors.1 = f32[1024,768]{1,0:T(8,128)} custom-call(s32[1]{0:T(128)} %bitcast.3.at_ref, bf16[1024,1024]{1,0:T(8,128)(2,1)} %bitcast.11, bf16[1024,512]{1,0:T(8,128)(2,1)} %get-tuple-element.52.sg_ref.refs_3_.refs_0_, bf16[1024,1536]{1,0:T(8,128)(2,1)} %get-tuple-element.53.qkv_ref.refs_4_.refs_5_.refs_1_.refs_2_, ...), custom_call_target="tpu_custom_call" | custom-call | flops 60000002048 | bytes 12000000 | tf_op jit(solution)/shard_map/factors/pallas_call | solution.py:199
  50.2 1.0 collective-permute-start.1
  51.2 0.0 collective-permute-done.r_ref
  51.2 8.3 %keep.1 = (f32[1024,768]{1,0:T(8,128)}, bf16[2,1024,768]{2,1,0:T(8,128)(2,1)}) custom-call(s32[1]{0:T(128)} %bitcast.3.at_ref, bf16[1024,1024]{1,0:T(8,128)(2,1)} %bitcast.12, f32[1024,768]{1,0:T(8,128)} %collective-permute-done.r_ref, bf16[1024,1536]{1,0:T(8,128)(2,1)} %get-tuple-element.51.refs_0_.refs_1_.refs_2_.loc_ref, ...), custom_call_target="tpu_custom_call" | custom-call | flops 40000000000 | bytes 16000000 | tf_op jit(solution)/shard_map/keep/pallas_call | solution.py:228
  59.5 1.3 all-to-all-done.1
  60.8 3.1 %collective-permute-start.2 = (f32[2,4,128,128]{3,2,1,0:T(8,128)S(1)}, f32[2,4,128,128]{3,2,1,0:T(8,128)S(1)}, u32[]{:S(2)}, u32[]{:S(2)}) collective-permute-start(f32[2,4,128,128]{3,2,1,0:T(8,128)S(1)} %bitcast.6), channel_id=1, source_target_pairs={{0,1},{1,0},{2,3},{3,2},{4,5},{5,4},{6,7},{7,6},{8,9},{9,8},{10,11... | collective-permute-start | bytes 1572872 | tf_op jit(solution)/shard_map/ppermute | solution.py:446
  63.9 0.0 collective-permute-done.1.b_hbm
  63.9 4.3 %own_states.1 = (f32[3,1024,256]{2,1,0:T(8,128)S(1)}, bf16[3,1024,256]{2,1,0:T(8,128)(2,1)S(1)}) custom-call(f32[1024,768]{1,0:T(8,128)} %get-tuple-element.56.w_hbm, bf16[2,1024,768]{2,1,0:T(8,128)(2,1)} %get-tuple-element.57.a_hbm, f32[1024,768]{1,0:T(8,128)} %collective-permute-done.1.b_hbm, f32[2,4,128,128]{3,2,1,0:T(8,128)S(1)} %bitcast.7), custom_call_target="tpu_custom_call" | custom-call | flops 5000000000 | bytes 12000000 | tf_op jit(solution)/shard_map/own_states/pallas_call | solution.py:279
  68.2 0.0 copy-start
  68.2 0.0 collective-permute-done.2.s_ref
  68.2 1.0 finish.1
  69.3 2.6 %collective-permute-start.3 = (f32[8,4,2,8,384]{4,3,2,1,0:T(8,128)S(1)}, f32[8,4,2,8,384]{4,3,2,1,0:T(8,128)S(1)}, u32[]{:S(2)}, u32[]{:S(2)}) collective-permute-start(f32[8,4,2,8,384]{4,3,2,1,0:T(8,128)S(1)} %get-tuple-element.61), channel_id=1, source_target_pairs={{0,2},{1,7},{2,0},{3,5},{4,6},{5,3},{6,4},{7,1},{8,10},{9,15},{10,... | collective-permute-start | bytes 2359304 | tf_op jit(solution)/shard_map/ppermute | solution.py:425
  71.9 1.8 %collective-permute-start.4 = (f32[8,2,4,8,384]{4,3,2,1,0:T(8,128)S(1)}, f32[8,2,4,8,384]{4,3,2,1,0:T(8,128)S(1)}, u32[]{:S(2)}, u32[]{:S(2)}) collective-permute-start(f32[8,2,4,8,384]{4,3,2,1,0:T(8,128)S(1)} %get-tuple-element.62), channel_id=1, source_target_pairs={{0,8},{1,25},{8,0},{9,17},{16,24},{17,9},{24,16},{25,1},{2,10},{3,... | collective-permute-start | bytes 2359304 | tf_op jit(solution)/shard_map/ppermute | solution.py:425
  73.7 0.0 copy-done
  73.7 8.6 %inputs_grad.1 = bf16[1024,1024]{1,0:T(8,128)(2,1)} custom-call(bf16[1024,1536]{1,0:T(8,128)(2,1)} %get-tuple-element.51.refs_0_.refs_1_.refs_2_.loc_ref, bf16[1024,1536]{1,0:T(8,128)(2,1)} %get-tuple-element.53.qkv_ref.refs_4_.refs_5_.refs_1_.refs_2_, bf16[1024,512]{1,0:T(8,128)(2,1)S(1)} %copy-done, f32[2,4,128,128]{3,2,1,0:T(8,128)S(1)} %bitcast.8, ...), custom_call_target="tpu_custom_call" | custom-call | flops 5000000000 | bytes 14000000 | tf_op jit(solution)/shard_map/inputs_grad/pallas_call | solution.py:348
  82.3 0.0 collective-permute-done.3.r
  82.3 1.6 %collective-permute-done.4.r = f32[8,2,4,8,384]{4,3,2,1,0:T(8,128)S(1)} collective-permute-done((f32[8,2,4,8,384]{4,3,2,1,0:T(8,128)S(1)}, f32[8,2,4,8,384]{4,3,2,1,0:T(8,128)S(1)}, u32[]{:S(2)}, u32[]{:S(2)}) %collective-permute-start.4) | collective-permute-done | bytes 786464 | tf_op jit(solution)/shard_map/ppermute | solution.py:425
  84.0 0.1 add1y.1
  84.0 0.1 collective-permute-start.8
  84.1 0.1 add1x.1
  84.2 0.1 collective-permute-start.5
  84.3 6.7 %collective-permute-done.8.r = f32[8,4,8,384]{3,2,1,0:T(8,128)S(1)} collective-permute-done((f32[8,4,8,384]{3,2,1,0:T(8,128)S(1)}, f32[8,4,8,384]{3,2,1,0:T(8,128)S(1)}, u32[]{:S(2)}, u32[]{:S(2)}) %collective-permute-start.8) | collective-permute-done | bytes 393248 | tf_op jit(solution)/shard_map/ppermute | solution.py:425
  91.1 0.4 collective-permute-start.9
  91.5 0.0 collective-permute-done.5.r
  91.5 1.9 %collective-permute-start.6 = (f32[8,2,8,384]{3,2,1,0:T(8,128)S(1)}, f32[8,2,8,384]{3,2,1,0:T(8,128)S(1)}, u32[]{:S(2)}, u32[]{:S(2)}) collective-permute-start(f32[8,2,8,384]{3,2,1,0:T(8,128)S(1)} %get-tuple-element.69), channel_id=1, source_target_pairs={{0,8},{1,25},{8,0},{9,17},{16,24},{17,9},{24,16},{25,1},{2,10},{3,... | collective-permute-start | bytes 589832 | tf_op jit(solution)/shard_map/ppermute | solution.py:425
  93.4 3.5 %collective-permute-done.9.r = f32[8,2,8,384]{3,2,1,0:T(8,128)S(1)} collective-permute-done((f32[8,2,8,384]{3,2,1,0:T(8,128)S(1)}, f32[8,2,8,384]{3,2,1,0:T(8,128)S(1)}, u32[]{:S(2)}, u32[]{:S(2)}) %collective-permute-start.9) | collective-permute-done | bytes 196640 | tf_op jit(solution)/shard_map/ppermute | solution.py:425
  96.9 0.1 collective-permute-start.10
  97.0 0.3 collective-permute-done.6.r
  97.3 0.1 collective-permute-start.7
  97.4 3.0 %collective-permute-done.10.rq = f32[8,8,384]{2,1,0:T(8,128)S(1)} collective-permute-done((f32[8,8,384]{2,1,0:T(8,128)S(1)}, f32[8,8,384]{2,1,0:T(8,128)S(1)}, u32[]{:S(2)}, u32[]{:S(2)}) %collective-permute-start.10) | collective-permute-done | bytes 98336 | tf_op jit(solution)/shard_map/ppermute | solution.py:425
  100.5 0.4 collective-permute-done.7.rp
  100.9 11.6 %all_to_all.20.v = f32[8,8,768]{2,1,0:T(8,128)S(1)} all-to-all(f32[8,8,768]{2,1,0:T(8,128)S(1)} %add4.1), channel_id=1, replica_groups=mesh['z'=8,'y'=4,'x'=4,'core'=2] {'z'}, dimensions={0} | all-to-all | bytes 393216 | tf_op jit(solution)/shard_map/all_to_all | solution.py:466
  112.6 17.7 %all_to_all.21.v = f32[8,8,768]{2,1,0:T(8,128)S(1)} all-to-all(f32[8,8,768]{2,1,0:T(8,128)S(1)} %sum_z.1), channel_id=1, replica_groups=mesh['z'=8,'y'=4,'x'=4,'core'=2] {'x','core'}, dimensions={0} | all-to-all | bytes 393216 | tf_op jit(solution)/shard_map/all_to_all | solution.py:468
  130.2 0.7 place.1
  (6 shorter events, 0.2 us)
Async XLA Ops:
  9.9 28.3 %all-to-all-start = ((f32[32,32,128]{2,1,0:T(8,128)}), f32[32,32,128]{2,1,0:T(8,128)S(1)}, u32[]{:S(2)}, u32[]{:S(2)}) async-start(f32[32,32,128]{2,1,0:T(8,128)} %bitcast.14), calls=%async_computation | async-start | bytes 1048576 | tf_op jit(solution)/shard_map/all_to_all | solution.py:433
  33.7 17.5 %collective-permute-start = (f32[1024,768]{1,0:T(8,128)}, f32[1024,768]{1,0:T(8,128)}, u32[]{:S(2)}, u32[]{:S(2)}) collective-permute-start(f32[1024,768]{1,0:T(8,128)} %get-tuple-element.50), channel_id=1, source_target_pairs={{0,1},{1,0},{2,3},{3,2},{4,5},{5,4},{6,7},{7,6},{8,9},{9,8},{10,11... | collective-permute-start | bytes 9437192 | tf_op jit(solution)/shard_map/ppermute | solution.py:435
  39.1 21.7 %all-to-all-start.1 = ((f32[32,32,128]{2,1,0:T(8,128)}), f32[32,32,128]{2,1,0:T(8,128)S(1)}, u32[]{:S(2)}, u32[]{:S(2)}) async-start(f32[32,32,128]{2,1,0:T(8,128)} %scan_states.1), calls=%async_computation.1 | async-start | bytes 1048576 | tf_op jit(solution)/shard_map/all_to_all | solution.py:439
  50.2 13.7 %collective-permute-start.1 = (f32[1024,768]{1,0:T(8,128)}, f32[1024,768]{1,0:T(8,128)}, u32[]{:S(2)}, u32[]{:S(2)}) collective-permute-start(f32[1024,768]{1,0:T(8,128)} %factors.1), channel_id=1, source_target_pairs={{0,1},{1,0},{2,3},{3,2},{4,5},{5,4},{6,7},{7,6},{8,9},{9,8},{10,11... | collective-permute-start | bytes 9437192 | tf_op jit(solution)/shard_map/ppermute | solution.py:441
  60.8 7.4 %collective-permute-start.2 = (f32[2,4,128,128]{3,2,1,0:T(8,128)S(1)}, f32[2,4,128,128]{3,2,1,0:T(8,128)S(1)}, u32[]{:S(2)}, u32[]{:S(2)}) collective-permute-start(f32[2,4,128,128]{3,2,1,0:T(8,128)S(1)} %bitcast.6), channel_id=1, source_target_pairs={{0,1},{1,0},{2,3},{3,2},{4,5},{5,4},{6,7},{7,6},{8,9},{9,8},{10,11... | collective-permute-start | bytes 1572872 | tf_op jit(solution)/shard_map/ppermute | solution.py:446
  68.2 5.5 %copy-start = (bf16[1024,512]{1,0:T(8,128)(2,1)S(1)}, bf16[1024,512]{1,0:T(8,128)(2,1)}, u32[]{:S(2)}) copy-start(bf16[1024,512]{1,0:T(8,128)(2,1)} %get-tuple-element.52.sg_ref.refs_3_.refs_0_) | copy-start | bytes 3145732
  69.3 13.0 %collective-permute-start.3 = (f32[8,4,2,8,384]{4,3,2,1,0:T(8,128)S(1)}, f32[8,4,2,8,384]{4,3,2,1,0:T(8,128)S(1)}, u32[]{:S(2)}, u32[]{:S(2)}) collective-permute-start(f32[8,4,2,8,384]{4,3,2,1,0:T(8,128)S(1)} %get-tuple-element.61), channel_id=1, source_target_pairs={{0,2},{1,7},{2,0},{3,5},{4,6},{5,3},{6,4},{7,1},{8,10},{9,15},{10,... | collective-permute-start | bytes 2359304 | tf_op jit(solution)/shard_map/ppermute | solution.py:425
  71.9 12.1 %collective-permute-start.4 = (f32[8,2,4,8,384]{4,3,2,1,0:T(8,128)S(1)}, f32[8,2,4,8,384]{4,3,2,1,0:T(8,128)S(1)}, u32[]{:S(2)}, u32[]{:S(2)}) collective-permute-start(f32[8,2,4,8,384]{4,3,2,1,0:T(8,128)S(1)} %get-tuple-element.62), channel_id=1, source_target_pairs={{0,8},{1,25},{8,0},{9,17},{16,24},{17,9},{24,16},{25,1},{2,10},{3,... | collective-permute-start | bytes 2359304 | tf_op jit(solution)/shard_map/ppermute | solution.py:425
  84.0 7.0 %collective-permute-start.8 = (f32[8,4,8,384]{3,2,1,0:T(8,128)S(1)}, f32[8,4,8,384]{3,2,1,0:T(8,128)S(1)}, u32[]{:S(2)}, u32[]{:S(2)}) collective-permute-start(f32[8,4,8,384]{3,2,1,0:T(8,128)S(1)} %get-tuple-element.75), channel_id=1, source_target_pairs={{0,24},{1,9},{8,16},{9,1},{16,8},{17,25},{24,0},{25,17},{2,26},{3,... | collective-permute-start | bytes 1179656 | tf_op jit(solution)/shard_map/ppermute | solution.py:425
  84.2 7.2 %collective-permute-start.5 = (f32[8,4,8,384]{3,2,1,0:T(8,128)S(1)}, f32[8,4,8,384]{3,2,1,0:T(8,128)S(1)}, u32[]{:S(2)}, u32[]{:S(2)}) collective-permute-start(f32[8,4,8,384]{3,2,1,0:T(8,128)S(1)} %get-tuple-element.67), channel_id=1, source_target_pairs={{0,6},{1,3},{2,4},{3,1},{4,2},{5,7},{6,0},{7,5},{8,14},{9,11},{10,... | collective-permute-start | bytes 1179656 | tf_op jit(solution)/shard_map/ppermute | solution.py:425
  91.1 5.8 %collective-permute-start.9 = (f32[8,2,8,384]{3,2,1,0:T(8,128)S(1)}, f32[8,2,8,384]{3,2,1,0:T(8,128)S(1)}, u32[]{:S(2)}, u32[]{:S(2)}) collective-permute-start(f32[8,2,8,384]{3,2,1,0:T(8,128)S(1)} %get-tuple-element.77), channel_id=1, source_target_pairs={{0,2},{1,7},{2,0},{3,5},{4,6},{5,3},{6,4},{7,1},{8,10},{9,15},{10,... | collective-permute-start | bytes 589832 | tf_op jit(solution)/shard_map/ppermute | solution.py:425
  91.5 5.8 %collective-permute-start.6 = (f32[8,2,8,384]{3,2,1,0:T(8,128)S(1)}, f32[8,2,8,384]{3,2,1,0:T(8,128)S(1)}, u32[]{:S(2)}, u32[]{:S(2)}) collective-permute-start(f32[8,2,8,384]{3,2,1,0:T(8,128)S(1)} %get-tuple-element.69), channel_id=1, source_target_pairs={{0,8},{1,25},{8,0},{9,17},{16,24},{17,9},{24,16},{25,1},{2,10},{3,... | collective-permute-start | bytes 589832 | tf_op jit(solution)/shard_map/ppermute | solution.py:425
  96.9 3.6 %collective-permute-start.10 = (f32[8,8,384]{2,1,0:T(8,128)S(1)}, f32[8,8,384]{2,1,0:T(8,128)S(1)}, u32[]{:S(2)}, u32[]{:S(2)}) collective-permute-start(f32[8,8,384]{2,1,0:T(8,128)S(1)} %get-tuple-element.79), channel_id=1, source_target_pairs={{0,6},{1,3},{2,4},{3,1},{4,2},{5,7},{6,0},{7,5},{8,14},{9,11},{10,... | collective-permute-start | bytes 294920 | tf_op jit(solution)/shard_map/ppermute | solution.py:425
  97.3 3.6 %collective-permute-start.7 = (f32[8,8,384]{2,1,0:T(8,128)S(1)}, f32[8,8,384]{2,1,0:T(8,128)S(1)}, u32[]{:S(2)}, u32[]{:S(2)}) collective-permute-start(f32[8,8,384]{2,1,0:T(8,128)S(1)} %get-tuple-element.71), channel_id=1, source_target_pairs={{0,24},{1,9},{8,16},{9,1},{16,8},{17,25},{24,0},{25,17},{2,26},{3,... | collective-permute-start | bytes 294920 | tf_op jit(solution)/shard_map/ppermute | solution.py:425

commit v10 on v8

--- a/solution.py
+++ b/solution.py
@@ -405,6 +405,13 @@
         o[i] = total
 
 
+def both_cores_body(mine, other, o):
+    core = lax.axis_index("core")
+    for i in range(4):
+        o[i, core] = mine[0]
+        o[i, 1 - core] = other[0]
+
+
 def place_body(v, o):
     for i in range(8):
         for p in range(6):
@@ -460,8 +467,10 @@
     rq = exchange(sq, "x", 1)
     (part,) = whole_call(add4_body, "add4", [(8, 8, 768)], kp, rp, kq, rq)
     part = lax.all_to_all(part, "z", 0, 0, tiled=True)
-    (own,) = whole_call(sum_body, "sum_z", [(8, 8, 768)], part)
-    rows = lax.all_to_all(own, ("x", "core"), 0, 0, tiled=True)
+    (own,) = whole_call(sum_body, "sum_z", [(1, 8, 768)], part)
+    other = lax.ppermute(own, "core", SWAP)
+    (pair,) = whole_call(both_cores_body, "both_cores", [(4, 2, 8, 768)], own, other)
+    rows = lax.all_to_all(pair, "x", 0, 0, tiled=True).reshape(8, 8, 768)
     (proj_grad,) = whole_call(place_body, "place", [(32, 3 * D)], rows)
     return record_grad[None], proj_grad
 

time: 130 us -> 131 us (level)
  blocking collectives: 28 us -> 20.3 us
  starting transfers between devices: 30.3 us -> 37.3 us
    all_to_all x1, blocking collectives: 16.6 us -> 8.89 us  [shards(): rows = lax.all_to_all(pair, 'x', 0, 0, tiled=True).reshape(8, 8, 768)]
    ppermute x0 -> x1, starting transfers between devices: none -> 6.98 us  [shards(): other = lax.ppermute(own, 'core', SWAP)]
  transfers between devices with their start and end apart: 13 -> 14, of which waited for: 8 -> 9; matrix products, arithmetic and copies ran while one was open for 0% -> 0% of each run, Pallas kernels for 29% -> 29%
where the time goes in v10:
time: 131 us; the launch traced here: 130 us
  Pallas kernels  48.8 us (37%)
  starting transfers between devices  37.3 us (28%)
  waiting for transfers between devices  21.5 us (16%)
  blocking collectives  20.3 us (15%)
  local copies, waits for them, and re-layouts  1.41 us (1%)
    ppermute x8, waiting for transfers between devices, exchange(): return lax.ppermute(value, (axis, 'core'), pairs)  15.6 us
    all_to_all x1, starting transfers between devices, shards(): lax.all_to_all(total.reshape(32, 32, HD), ('z', 'y'), 0, 0, tiled=True)  12 us
    pallas_call x1, Pallas kernels, local(): pl.pallas_call(local_body, grid_spec=pltpu.PrefetchScalarGridSpec(num_sca...  11.7 us
    all_to_all x1, blocking collectives, shards(): part = lax.all_to_all(part, 'z', 0, 0, tiled=True)  11.4 us
    pallas_call x1, Pallas kernels, project(): pl.pallas_call(project_body, grid=(NB,), in_specs=[block(DM), pl.BlockSpe...  9.23 us
    all_to_all x1, blocking collectives, shards(): rows = lax.all_to_all(pair, 'x', 0, 0, tiled=True).reshape(8, 8, 768)  8.89 us
    pallas_call x1, Pallas kernels, inputs_grad(): pl.pallas_call(inputs_body, grid=(NB,), in_specs=[block(3 * D), block(3 *...  8.6 us
    pallas_call x1, Pallas kernels, keep(): pl.pallas_call(keep_body, grid_spec=pltpu.PrefetchScalarGridSpec(num_scal...  7.96 us
  transfers between devices with their start and end apart: 14, of which 9 were waited for; matrix products, arithmetic and copies ran while one was open for 0% of the time, Pallas kernels for 29%

profile of v10, /device:TPU:1, one launch (start us, length us, event | category | flops | bytes accessed | tf_op | source)
XLA Modules:
  0.0 130.1 jit_solution(1784630968163380095)
XLA Ops:
  0.6 9.2 %project.1 = (bf16[1024,1536]{1,0:T(8,128)(2,1)}, bf16[1024,512]{1,0:T(8,128)(2,1)}, f32[4,4,128,128]{3,2,1,0:T(8,128)}, f32[4,4,128,128]{3,2,1,0:T(8,128)}, f32[2,4,128,128]{3,2,1,0:T(8,128)}) custom-call(bf16[1024,1024]{1,0:T(8,128)(2,1)} %bitcast.11, bf16[1024,1536]{1,0:T(8,128)(2,1)} %w_ref.3, bf16[1024,512]{1,0:T(8,128)(2,1)} %bitcast.15), custom_call_target="tpu_custom_call" | custom-call | tf_op jit(solution)/shard_map/project/pallas_call | solution.py:69
  9.9 12.0 %all-to-all-start = ((f32[32,32,128]{2,1,0:T(8,128)}), f32[32,32,128]{2,1,0:T(8,128)S(1)}, u32[]{:S(2)}, u32[]{:S(2)}) async-start(f32[32,32,128]{2,1,0:T(8,128)} %bitcast.16), calls=%async_computation | async-start | bytes 1048576 | tf_op jit(solution)/shard_map/all_to_all | solution.py:436
  21.9 11.7 %local.1 = (bf16[1024,1536]{1,0:T(8,128)(2,1)}, f32[1024,768]{1,0:T(8,128)}) custom-call(s32[1]{0:T(128)} %bitcast.3.at_ref, bf16[1024,1536]{1,0:T(8,128)(2,1)} %get-tuple-element.53.qkv_ref.refs_4_.refs_5_.refs_1_.refs_2_, bf16[1024,512]{1,0:T(8,128)(2,1)} %get-tuple-element.52.sg_ref.refs_3_.refs_0_, f32[4,4,128,128]{3,2,1,0:T(8,128)} %get-tuple-element.44.kv_ref, ...), custom_call_target="tpu_custom_call" | custom-call | flops 8000000000 | bytes 24000000 | tf_op jit(solution)/shard_map/local/pallas_call | solution.py:163
  33.7 1.0 collective-permute-start
  34.7 3.5 %all-to-all-done.v_ref = f32[32,32,128]{2,1,0:T(8,128)S(1)} async-done(((f32[32,32,128]{2,1,0:T(8,128)}), f32[32,32,128]{2,1,0:T(8,128)S(1)}, u32[]{:S(2)}, u32[]{:S(2)}) %all-to-all-start) | async-done | bytes 524320 | tf_op jit(solution)/shard_map/all_to_all | solution.py:436
  38.2 1.0 scan_states.1
  39.2 6.0 %all-to-all-start.1 = ((f32[32,32,128]{2,1,0:T(8,128)}), f32[32,32,128]{2,1,0:T(8,128)S(1)}, u32[]{:S(2)}, u32[]{:S(2)}) async-start(f32[32,32,128]{2,1,0:T(8,128)} %scan_states.1), calls=%async_computation.1 | async-start | bytes 1048576 | tf_op jit(solution)/shard_map/all_to_all | solution.py:442
  45.2 5.0 %factors.1 = f32[1024,768]{1,0:T(8,128)} custom-call(s32[1]{0:T(128)} %bitcast.3.at_ref, bf16[1024,1024]{1,0:T(8,128)(2,1)} %bitcast.13, bf16[1024,512]{1,0:T(8,128)(2,1)} %get-tuple-element.52.sg_ref.refs_3_.refs_0_, bf16[1024,1536]{1,0:T(8,128)(2,1)} %get-tuple-element.53.qkv_ref.refs_4_.refs_5_.refs_1_.refs_2_, ...), custom_call_target="tpu_custom_call" | custom-call | flops 60000002048 | bytes 12000000 | tf_op jit(solution)/shard_map/factors/pallas_call | solution.py:199
  50.2 1.1 collective-permute-start.1
  51.2 0.0 collective-permute-done.r_ref
  51.2 8.0 %keep.1 = (f32[1024,768]{1,0:T(8,128)}, bf16[1024,768]{1,0:T(8,128)(2,1)}) custom-call(s32[1]{0:T(128)} %bitcast.3.at_ref, bf16[1024,1024]{1,0:T(8,128)(2,1)} %bitcast.14, f32[1024,768]{1,0:T(8,128)} %collective-permute-done.r_ref, bf16[1024,1536]{1,0:T(8,128)(2,1)} %get-tuple-element.51.refs_0_.refs_1_.refs_2_.loc_ref, ...), custom_call_target="tpu_custom_call" | custom-call | flops 40000000000 | bytes 16000000 | tf_op jit(solution)/shard_map/keep/pallas_call | solution.py:225
  59.2 1.6 %all-to-all-done.1 = f32[32,32,128]{2,1,0:T(8,128)S(1)} async-done(((f32[32,32,128]{2,1,0:T(8,128)}), f32[32,32,128]{2,1,0:T(8,128)S(1)}, u32[]{:S(2)}, u32[]{:S(2)}) %all-to-all-start.1) | async-done | bytes 524320 | tf_op jit(solution)/shard_map/all_to_all | solution.py:442
  60.8 3.1 %collective-permute-start.2 = (f32[2,4,128,128]{3,2,1,0:T(8,128)S(1)}, f32[2,4,128,128]{3,2,1,0:T(8,128)S(1)}, u32[]{:S(2)}, u32[]{:S(2)}) collective-permute-start(f32[2,4,128,128]{3,2,1,0:T(8,128)S(1)} %bitcast.8), channel_id=1, source_target_pairs={{0,1},{1,0},{2,3},{3,2},{4,5},{5,4},{6,7},{7,6},{8,9},{9,8},{10,11... | collective-permute-start | bytes 1572872 | tf_op jit(solution)/shard_map/ppermute | solution.py:449
  63.9 0.0 collective-permute-done.1.b_hbm
  63.9 0.0 copy-start.1
  63.9 1.4 %copy-done.1 = bf16[1024,768]{1,0:T(8,128)(2,1)S(1)} copy-done((bf16[1024,768]{1,0:T(8,128)(2,1)S(1)}, bf16[1024,768]{1,0:T(8,128)(2,1)}, u32[]{:S(2)}) %copy-start.1) | copy-done | bytes 1572888
  65.3 3.3 %own_states.1 = (f32[3,1024,256]{2,1,0:T(8,128)S(1)}, bf16[3,1024,256]{2,1,0:T(8,128)(2,1)S(1)}) custom-call(f32[1024,768]{1,0:T(8,128)} %get-tuple-element.56.w_hbm, bf16[1024,768]{1,0:T(8,128)(2,1)S(1)} %copy-done.1, f32[1024,768]{1,0:T(8,128)} %collective-permute-done.1.b_hbm, f32[2,4,128,128]{3,2,1,0:T(8,128)S(1)} %bitcast.9), custom_call_target="tpu_custom_call" | custom-call | flops 5000000000 | bytes 12000000 | tf_op jit(solution)/shard_map/own_states/pallas_call | solution.py:275
  68.6 0.0 copy-start
  68.6 0.0 collective-permute-done.2.s_ref
  68.6 1.1 finish.1
  69.7 2.6 %collective-permute-start.3 = (f32[8,4,2,8,384]{4,3,2,1,0:T(8,128)S(1)}, f32[8,4,2,8,384]{4,3,2,1,0:T(8,128)S(1)}, u32[]{:S(2)}, u32[]{:S(2)}) collective-permute-start(f32[8,4,2,8,384]{4,3,2,1,0:T(8,128)S(1)} %get-tuple-element.61), channel_id=1, source_target_pairs={{0,2},{1,7},{2,0},{3,5},{4,6},{5,3},{6,4},{7,1},{8,10},{9,15},{10,... | collective-permute-start | bytes 2359304 | tf_op jit(solution)/shard_map/ppermute | solution.py:428
  72.3 1.8 %collective-permute-start.4 = (f32[8,2,4,8,384]{4,3,2,1,0:T(8,128)S(1)}, f32[8,2,4,8,384]{4,3,2,1,0:T(8,128)S(1)}, u32[]{:S(2)}, u32[]{:S(2)}) collective-permute-start(f32[8,2,4,8,384]{4,3,2,1,0:T(8,128)S(1)} %get-tuple-element.62), channel_id=1, source_target_pairs={{0,8},{1,25},{8,0},{9,17},{16,24},{17,9},{24,16},{25,1},{2,10},{3,... | collective-permute-start | bytes 2359304 | tf_op jit(solution)/shard_map/ppermute | solution.py:428
  74.1 0.0 copy-done
  74.1 8.6 %inputs_grad.1 = bf16[1024,1024]{1,0:T(8,128)(2,1)} custom-call(bf16[1024,1536]{1,0:T(8,128)(2,1)} %get-tuple-element.51.refs_0_.refs_1_.refs_2_.loc_ref, bf16[1024,1536]{1,0:T(8,128)(2,1)} %get-tuple-element.53.qkv_ref.refs_4_.refs_5_.refs_1_.refs_2_, bf16[1024,512]{1,0:T(8,128)(2,1)S(1)} %copy-done, f32[2,4,128,128]{3,2,1,0:T(8,128)S(1)} %bitcast.10, ...), custom_call_target="tpu_custom_call" | custom-call | flops 5000000000 | bytes 14000000 | tf_op jit(solution)/shard_map/inputs_grad/pallas_call | solution.py:344
  82.7 0.0 collective-permute-done.3.r
  82.7 1.6 %collective-permute-done.4.r = f32[8,2,4,8,384]{4,3,2,1,0:T(8,128)S(1)} collective-permute-done((f32[8,2,4,8,384]{4,3,2,1,0:T(8,128)S(1)}, f32[8,2,4,8,384]{4,3,2,1,0:T(8,128)S(1)}, u32[]{:S(2)}, u32[]{:S(2)}) %collective-permute-start.4) | collective-permute-done | bytes 786464 | tf_op jit(solution)/shard_map/ppermute | solution.py:428
  84.3 0.1 add1y.1
  84.4 0.1 collective-permute-start.8
  84.5 0.1 add1x.1
  84.6 0.1 collective-permute-start.5
  84.7 6.7 %collective-permute-done.8.r = f32[8,4,8,384]{3,2,1,0:T(8,128)S(1)} collective-permute-done((f32[8,4,8,384]{3,2,1,0:T(8,128)S(1)}, f32[8,4,8,384]{3,2,1,0:T(8,128)S(1)}, u32[]{:S(2)}, u32[]{:S(2)}) %collective-permute-start.8) | collective-permute-done | bytes 393248 | tf_op jit(solution)/shard_map/ppermute | solution.py:428
  91.5 0.4 collective-permute-start.9
  91.8 0.0 collective-permute-done.5.r
  91.9 1.9 %collective-permute-start.6 = (f32[8,2,8,384]{3,2,1,0:T(8,128)S(1)}, f32[8,2,8,384]{3,2,1,0:T(8,128)S(1)}, u32[]{:S(2)}, u32[]{:S(2)}) collective-permute-start(f32[8,2,8,384]{3,2,1,0:T(8,128)S(1)} %get-tuple-element.69), channel_id=1, source_target_pairs={{0,8},{1,25},{8,0},{9,17},{16,24},{17,9},{24,16},{25,1},{2,10},{3,... | collective-permute-start | bytes 589832 | tf_op jit(solution)/shard_map/ppermute | solution.py:428
  93.8 3.5 %collective-permute-done.9.r = f32[8,2,8,384]{3,2,1,0:T(8,128)S(1)} collective-permute-done((f32[8,2,8,384]{3,2,1,0:T(8,128)S(1)}, f32[8,2,8,384]{3,2,1,0:T(8,128)S(1)}, u32[]{:S(2)}, u32[]{:S(2)}) %collective-permute-start.9) | collective-permute-done | bytes 196640 | tf_op jit(solution)/shard_map/ppermute | solution.py:428
  97.3 0.1 collective-permute-start.10
  97.4 0.3 collective-permute-done.6.r
  97.7 0.1 collective-permute-start.7
  97.8 3.0 %collective-permute-done.10.rq = f32[8,8,384]{2,1,0:T(8,128)S(1)} collective-permute-done((f32[8,8,384]{2,1,0:T(8,128)S(1)}, f32[8,8,384]{2,1,0:T(8,128)S(1)}, u32[]{:S(2)}, u32[]{:S(2)}) %collective-permute-start.10) | collective-permute-done | bytes 98336 | tf_op jit(solution)/shard_map/ppermute | solution.py:428
  100.9 0.4 collective-permute-done.7.rp
  101.3 11.4 %all_to_all.20.v = f32[8,8,768]{2,1,0:T(8,128)S(1)} all-to-all(f32[8,8,768]{2,1,0:T(8,128)S(1)} %add4.1), channel_id=1, replica_groups=mesh['z'=8,'y'=4,'x'=4,'core'=2] {'z'}, dimensions={0} | all-to-all | bytes 393216 | tf_op jit(solution)/shard_map/all_to_all | solution.py:469
  112.7 7.0 %collective-permute-start.11 = (f32[1,8,768]{2,1,0:T(8,128)S(1)}, f32[1,8,768]{2,1,0:T(8,128)S(1)}, u32[]{:S(2)}, u32[]{:S(2)}) collective-permute-start(f32[1,8,768]{2,1,0:T(8,128)S(1)} %sum_z.1.mine), channel_id=1, source_target_pairs={{0,1},{1,0},{2,3},{3,2},{4,5},{5,4},{6,7},{7,6},{8,9},{9,8},{10,11... | collective-permute-start | bytes 73736 | tf_op jit(solution)/shard_map/ppermute | solution.py:471
  119.7 0.8 collective-permute-done.11.other
  120.5 8.9 %all_to_all.21 = f32[4,2,8,768]{3,2,1,0:T(8,128)S(1)} all-to-all(f32[4,2,8,768]{3,2,1,0:T(8,128)S(1)} %both_cores.1), channel_id=1, replica_groups=mesh['z'=8,'y'=4,'x'=4,'core'=2] {'x'}, dimensions={0} | all-to-all | bytes 393216 | tf_op jit(solution)/shard_map/all_to_all | solution.py:473
  129.4 0.7 place.1
  (7 shorter events, 0.2 us)
Async XLA Ops:
  9.9 28.3 %all-to-all-start = ((f32[32,32,128]{2,1,0:T(8,128)}), f32[32,32,128]{2,1,0:T(8,128)S(1)}, u32[]{:S(2)}, u32[]{:S(2)}) async-start(f32[32,32,128]{2,1,0:T(8,128)} %bitcast.16), calls=%async_computation | async-start | bytes 1048576 | tf_op jit(solution)/shard_map/all_to_all | solution.py:436
  33.7 17.6 %collective-permute-start = (f32[1024,768]{1,0:T(8,128)}, f32[1024,768]{1,0:T(8,128)}, u32[]{:S(2)}, u32[]{:S(2)}) collective-permute-start(f32[1024,768]{1,0:T(8,128)} %get-tuple-element.50), channel_id=1, source_target_pairs={{0,1},{1,0},{2,3},{3,2},{4,5},{5,4},{6,7},{7,6},{8,9},{9,8},{10,11... | collective-permute-start | bytes 9437192 | tf_op jit(solution)/shard_map/ppermute | solution.py:438
  39.2 21.6 %all-to-all-start.1 = ((f32[32,32,128]{2,1,0:T(8,128)}), f32[32,32,128]{2,1,0:T(8,128)S(1)}, u32[]{:S(2)}, u32[]{:S(2)}) async-start(f32[32,32,128]{2,1,0:T(8,128)} %scan_states.1), calls=%async_computation.1 | async-start | bytes 1048576 | tf_op jit(solution)/shard_map/all_to_all | solution.py:442
  50.2 13.7 %collective-permute-start.1 = (f32[1024,768]{1,0:T(8,128)}, f32[1024,768]{1,0:T(8,128)}, u32[]{:S(2)}, u32[]{:S(2)}) collective-permute-start(f32[1024,768]{1,0:T(8,128)} %factors.1), channel_id=1, source_target_pairs={{0,1},{1,0},{2,3},{3,2},{4,5},{5,4},{6,7},{7,6},{8,9},{9,8},{10,11... | collective-permute-start | bytes 9437192 | tf_op jit(solution)/shard_map/ppermute | solution.py:444
  60.8 7.8 %collective-permute-start.2 = (f32[2,4,128,128]{3,2,1,0:T(8,128)S(1)}, f32[2,4,128,128]{3,2,1,0:T(8,128)S(1)}, u32[]{:S(2)}, u32[]{:S(2)}) collective-permute-start(f32[2,4,128,128]{3,2,1,0:T(8,128)S(1)} %bitcast.8), channel_id=1, source_target_pairs={{0,1},{1,0},{2,3},{3,2},{4,5},{5,4},{6,7},{7,6},{8,9},{9,8},{10,11... | collective-permute-start | bytes 1572872 | tf_op jit(solution)/shard_map/ppermute | solution.py:449
  63.9 1.4 %copy-start.1 = (bf16[1024,768]{1,0:T(8,128)(2,1)S(1)}, bf16[1024,768]{1,0:T(8,128)(2,1)}, u32[]{:S(2)}) copy-start(bf16[1024,768]{1,0:T(8,128)(2,1)} %get-tuple-element.57.a_hbm) | copy-start | bytes 4718596
  68.6 5.5 %copy-start = (bf16[1024,512]{1,0:T(8,128)(2,1)S(1)}, bf16[1024,512]{1,0:T(8,128)(2,1)}, u32[]{:S(2)}) copy-start(bf16[1024,512]{1,0:T(8,128)(2,1)} %get-tuple-element.52.sg_ref.refs_3_.refs_0_) | copy-start | bytes 3145732
  69.7 13.0 %collective-permute-start.3 = (f32[8,4,2,8,384]{4,3,2,1,0:T(8,128)S(1)}, f32[8,4,2,8,384]{4,3,2,1,0:T(8,128)S(1)}, u32[]{:S(2)}, u32[]{:S(2)}) collective-permute-start(f32[8,4,2,8,384]{4,3,2,1,0:T(8,128)S(1)} %get-tuple-element.61), channel_id=1, source_target_pairs={{0,2},{1,7},{2,0},{3,5},{4,6},{5,3},{6,4},{7,1},{8,10},{9,15},{10,... | collective-permute-start | bytes 2359304 | tf_op jit(solution)/shard_map/ppermute | solution.py:428
  72.3 12.1 %collective-permute-start.4 = (f32[8,2,4,8,384]{4,3,2,1,0:T(8,128)S(1)}, f32[8,2,4,8,384]{4,3,2,1,0:T(8,128)S(1)}, u32[]{:S(2)}, u32[]{:S(2)}) collective-permute-start(f32[8,2,4,8,384]{4,3,2,1,0:T(8,128)S(1)} %get-tuple-element.62), channel_id=1, source_target_pairs={{0,8},{1,25},{8,0},{9,17},{16,24},{17,9},{24,16},{25,1},{2,10},{3,... | collective-permute-start | bytes 2359304 | tf_op jit(solution)/shard_map/ppermute | solution.py:428
  84.4 7.0 %collective-permute-start.8 = (f32[8,4,8,384]{3,2,1,0:T(8,128)S(1)}, f32[8,4,8,384]{3,2,1,0:T(8,128)S(1)}, u32[]{:S(2)}, u32[]{:S(2)}) collective-permute-start(f32[8,4,8,384]{3,2,1,0:T(8,128)S(1)} %get-tuple-element.75), channel_id=1, source_target_pairs={{0,24},{1,9},{8,16},{9,1},{16,8},{17,25},{24,0},{25,17},{2,26},{3,... | collective-permute-start | bytes 1179656 | tf_op jit(solution)/shard_map/ppermute | solution.py:428
  84.6 7.2 %collective-permute-start.5 = (f32[8,4,8,384]{3,2,1,0:T(8,128)S(1)}, f32[8,4,8,384]{3,2,1,0:T(8,128)S(1)}, u32[]{:S(2)}, u32[]{:S(2)}) collective-permute-start(f32[8,4,8,384]{3,2,1,0:T(8,128)S(1)} %get-tuple-element.67), channel_id=1, source_target_pairs={{0,6},{1,3},{2,4},{3,1},{4,2},{5,7},{6,0},{7,5},{8,14},{9,11},{10,... | collective-permute-start | bytes 1179656 | tf_op jit(solution)/shard_map/ppermute | solution.py:428
  91.5 5.8 %collective-permute-start.9 = (f32[8,2,8,384]{3,2,1,0:T(8,128)S(1)}, f32[8,2,8,384]{3,2,1,0:T(8,128)S(1)}, u32[]{:S(2)}, u32[]{:S(2)}) collective-permute-start(f32[8,2,8,384]{3,2,1,0:T(8,128)S(1)} %get-tuple-element.77), channel_id=1, source_target_pairs={{0,2},{1,7},{2,0},{3,5},{4,6},{5,3},{6,4},{7,1},{8,10},{9,15},{10,... | collective-permute-start | bytes 589832 | tf_op jit(solution)/shard_map/ppermute | solution.py:428
  91.9 5.8 %collective-permute-start.6 = (f32[8,2,8,384]{3,2,1,0:T(8,128)S(1)}, f32[8,2,8,384]{3,2,1,0:T(8,128)S(1)}, u32[]{:S(2)}, u32[]{:S(2)}) collective-permute-start(f32[8,2,8,384]{3,2,1,0:T(8,128)S(1)} %get-tuple-element.69), channel_id=1, source_target_pairs={{0,8},{1,25},{8,0},{9,17},{16,24},{17,9},{24,16},{25,1},{2,10},{3,... | collective-permute-start | bytes 589832 | tf_op jit(solution)/shard_map/ppermute | solution.py:428
  97.3 3.6 %collective-permute-start.10 = (f32[8,8,384]{2,1,0:T(8,128)S(1)}, f32[8,8,384]{2,1,0:T(8,128)S(1)}, u32[]{:S(2)}, u32[]{:S(2)}) collective-permute-start(f32[8,8,384]{2,1,0:T(8,128)S(1)} %get-tuple-element.79), channel_id=1, source_target_pairs={{0,6},{1,3},{2,4},{3,1},{4,2},{5,7},{6,0},{7,5},{8,14},{9,11},{10,... | collective-permute-start | bytes 294920 | tf_op jit(solution)/shard_map/ppermute | solution.py:428
  97.7 3.6 %collective-permute-start.7 = (f32[8,8,384]{2,1,0:T(8,128)S(1)}, f32[8,8,384]{2,1,0:T(8,128)S(1)}, u32[]{:S(2)}, u32[]{:S(2)}) collective-permute-start(f32[8,8,384]{2,1,0:T(8,128)S(1)} %get-tuple-element.71), channel_id=1, source_target_pairs={{0,24},{1,9},{8,16},{9,1},{16,8},{17,25},{24,0},{25,17},{2,26},{3,... | collective-permute-start | bytes 294920 | tf_op jit(solution)/shard_map/ppermute | solution.py:428
  112.7 7.8 %collective-permute-start.11 = (f32[1,8,768]{2,1,0:T(8,128)S(1)}, f32[1,8,768]{2,1,0:T(8,128)S(1)}, u32[]{:S(2)}, u32[]{:S(2)}) collective-permute-start(f32[1,8,768]{2,1,0:T(8,128)S(1)} %sum_z.1.mine), channel_id=1, source_target_pairs={{0,1},{1,0},{2,3},{3,2},{4,5},{5,4},{6,7},{7,6},{8,9},{9,8},{10,11... | collective-permute-start | bytes 73736 | tf_op jit(solution)/shard_map/ppermute | solution.py:471
